TPU v7x, 512 devices: a whole 4x4x16 slice. The times are simulated.
512 devices in a mesh: tensor: 32 (over z, y_lo), dp: 16 (over y_hi, x, core).
Axes of the slice: x: 4, y: 4 (y_hi: 2, y_lo: 2; y = y_hi * 2 + y_lo), z: 16, core: 2. Of those that a mesh axis runs over, the one named last changes fastest.
Arguments:
- stream: bfloat16 [512, 12288], P('tensor', 'dp'), may hold values from -150 to 150
- norm_gain: float32 [12288], P('dp'), may hold values from 0.1 to 1.9
- head_weight: bfloat16 [16384, 12288], P('tensor', 'dp'), may hold values from -1 to 1
- down_weight: bfloat16 [14336, 12288], P('tensor', 'dp'), may hold values from -0.046875 to 0.046875
- gate_pre: bfloat16 [512, 14336], P('dp', 'tensor'), may hold values from -6 to 6
- up_pre: bfloat16 [512, 14336], P('dp', 'tensor'), may hold values from -6 to 6
- targets: int32 [512], P('dp'), may hold values from 0 to 16383
- token_weight: float32 [512], P('dp'), may hold values from 1 to 120
Outputs:
- head_grad: float32 [16384, 12288], P('tensor', 'dp')
- down_grad: float32 [14336, 12288], P('tensor', 'dp')
- stream_grad: bfloat16 [512, 12288], P('tensor', 'dp')
- gain_grad: float32 [12288], P('dp')
- gate_grad: bfloat16 [512, 14336], P('dp', 'tensor')
- up_grad: bfloat16 [512, 14336], P('dp', 'tensor')
All inputs are finite; a program needn't handle non-finite values.
Results may differ from a plain program's by a relative error of at most 0.02.
Values may be sent and summed in bfloat16 or wider, within the bound.
No kernel may reach another device: no remote copies, remote signals or barrier semaphores. Data moves between devices by JAX's collectives and lax.ppermute only.
A program may use at most 64 MiB of HBM per device.

v0:
```python
import jax
import jax.numpy as jnp
from jax import lax
from jax.sharding import PartitionSpec as P

D = 12288


epsilon = 1e-05


def per_device(
    stream, norm_gain, head_weight, down_weight, gate_pre, up_pre, targets, token_weight
):
    vocab_local = head_weight.shape[0]
    stream_float = stream.astype(jnp.float32)
    squares = lax.psum(jnp.sum(stream_float * stream_float, axis=1), "dp")
    inv_rms = lax.rsqrt(squares / D + epsilon)
    unit_rows = stream_float * inv_rms[:, None]
    normed = (unit_rows * norm_gain).astype(jnp.bfloat16)
    normed_all = lax.all_gather(normed, "tensor", axis=0, tiled=True)
    rows_here = normed_all
    logits = lax.psum_scatter(
        jnp.einsum("td,vd->tv", rows_here, head_weight, preferred_element_type=jnp.float32),
        "dp",
        scatter_dimension=0,
        tiled=True,
    )
    row_top = jnp.max(logits, axis=1)
    global_top = lax.pmax(row_top, "tensor")
    global_total = lax.psum(jnp.sum(jnp.exp(logits - global_top[:, None]), axis=1), "tensor")
    probability = jnp.exp(logits - global_top[:, None]) / global_total[:, None]
    columns = lax.axis_index("tensor") * vocab_local + lax.iota(jnp.int32, vocab_local)
    matches = (targets[:, None] == columns[None, :]).astype(jnp.float32)
    dlogits = ((probability - matches) * token_weight[:, None]).astype(jnp.bfloat16)
    piece = lax.all_gather(dlogits, "dp", axis=0, tiled=True)
    rows_here = normed_all
    weight_part = jnp.einsum("tv,td->vd", piece, rows_here, preferred_element_type=jnp.float32)
    back_rows = jnp.dot(piece, head_weight, preferred_element_type=jnp.float32)
    normed_back = lax.psum_scatter(back_rows, "tensor", scatter_dimension=0, tiled=True)
    scaled = normed_back * norm_gain
    inner_sums = lax.psum(jnp.sum(scaled * unit_rows, axis=1), "dp") / D
    stream_grad = (inv_rms[:, None] * (scaled - unit_rows * inner_sums[:, None])).astype(
        jnp.bfloat16
    )
    gain_grad = lax.psum(jnp.sum(normed_back * unit_rows, axis=0), "tensor")
    stream_all = lax.all_gather(stream_grad, "tensor", axis=0, tiled=True)
    rows_here = stream_all
    hidden_back = lax.psum_scatter(
        jnp.einsum("td,fd->tf", rows_here, down_weight, preferred_element_type=jnp.float32).astype(
            jnp.bfloat16
        ),
        "dp",
        scatter_dimension=0,
        tiled=True,
    ).astype(jnp.float32)
    gate_float = gate_pre.astype(jnp.float32)
    up_float = up_pre.astype(jnp.float32)
    sigmoid_gate = jax.nn.sigmoid(gate_float)
    hidden = (gate_float * sigmoid_gate * up_float).astype(jnp.bfloat16)
    rows_here = stream_all
    down_grad = jnp.einsum(
        "tf,td->fd",
        lax.all_gather(hidden, "dp", axis=0, tiled=True),
        rows_here,
        preferred_element_type=jnp.float32,
    )
    up_grad = (hidden_back * gate_float * sigmoid_gate).astype(jnp.bfloat16)
    gate_grad = (
        hidden_back * up_float * sigmoid_gate * (1.0 + gate_float * (1.0 - sigmoid_gate))
    ).astype(jnp.bfloat16)
    return (weight_part, down_grad, stream_grad, gain_grad, gate_grad, up_grad)


def solution(mesh):
    return jax.shard_map(
        per_device,
        mesh=mesh,
        in_specs=(
            P("tensor", "dp"),
            P("dp"),
            P("tensor", "dp"),
            P("tensor", "dp"),
            P("dp", "tensor"),
            P("dp", "tensor"),
            P("dp"),
            P("dp"),
        ),
        out_specs=(
            P("tensor", "dp"),
            P("tensor", "dp"),
            P("tensor", "dp"),
            P("dp"),
            P("dp", "tensor"),
            P("dp", "tensor"),
        ),
        check_vma=False,
    )
```

profile of v0, /device:TPU:1, one launch (start us, length us, event | category | flops | bytes accessed | tf_op | source)
XLA Modules:
  0.0 709.7 jit_solution(10887034967986209091)
XLA Ops:
  7.2 0.9 fusion.21
  8.1 39.4 %psum.28 = f32[16]{0:T(128)S(1)} all-reduce(f32[16]{0:T(128)S(1)} %fusion.21), channel_id=1, replica_groups=mesh['tensor'=32,'dp'=16] {'dp'}, use_global_device_ids=true, to_apply=%region_1.0 | all-reduce | flops 16 | bytes 128 | tf_op jit(solution)/shard_map/psum | solution.py:17
  48.4 54.2 %all_gather.12 = bf16[512,768]{1,0:T(8,128)(2,1)S(1)} all-gather(bf16[16,768]{1,0:T(8,128)(2,1)S(1)} %fusion.15), channel_id=1, replica_groups=mesh['tensor'=32,'dp'=16] {'tensor'}, dimensions={0}, use_global_device_ids=true | all-gather | bytes 811008 | tf_op jit(solution)/shard_map/all_gather | solution.py:21
  102.6 1.6 fusion.22
  104.2 97.5 %reduce-scatter.4.cloned.1.call-done = f32[32,512]{1,0:T(8,128)} async-done(((f32[512,512]{1,0:T(8,128)}), f32[32,512]{1,0:T(8,128)}) %reduce-scatter.4.cloned.1.call-update) | async-done | bytes 65552 | tf_op jit(solution)/shard_map/reduce_scatter | solution.py:23
  201.7 1.0 reduce_max.9
  202.7 50.2 %pmax.7 = f32[32]{0:T(128)S(1)} all-reduce(f32[32]{0:T(128)S(1)} %reduce_max.9), channel_id=1, replica_groups=mesh['tensor'=32,'dp'=16] {'tensor'}, use_global_device_ids=true, to_apply=%region_4.0 | all-reduce | flops 32 | bytes 256 | tf_op jit(solution)/shard_map/pmax | solution.py:30
  252.9 1.0 fusion.14
  254.0 46.1 %psum.29 = f32[32]{0:T(128)S(1)} all-reduce(f32[32]{0:T(128)S(1)} %fusion.14), channel_id=1, replica_groups=mesh['tensor'=32,'dp'=16] {'tensor'}, use_global_device_ids=true, to_apply=%region_6.0 | all-reduce | flops 32 | bytes 256 | tf_op jit(solution)/shard_map/psum | solution.py:31
  300.0 0.9 multiply_convert_fusion
  301.0 54.2 %all_gather.13 = bf16[512,512]{1,0:T(8,128)(2,1)S(1)} all-gather(bf16[32,512]{1,0:T(8,128)(2,1)S(1)} %multiply_convert_fusion), channel_id=1, replica_groups=mesh['tensor'=32,'dp'=16] {'dp'}, dimensions={0}, use_global_device_ids=true | all-gather | bytes 557056 | tf_op jit(solution)/shard_map/all_gather | solution.py:36
  355.2 1.7 fusion.24
  357.0 109.9 %reduce-scatter.6.cloned.1.call-done = f32[16,768]{1,0:T(8,128)} async-done(((f32[512,768]{1,0:T(8,128)}), f32[16,768]{1,0:T(8,128)}) %reduce-scatter.6.cloned.1.call-update) | async-done | bytes 49168 | tf_op jit(solution)/shard_map/reduce_scatter | solution.py:40
  466.9 1.0 fusion.20
  467.9 55.7 %psum.30 = f32[16]{0:T(128)S(1)} all-reduce(f32[16]{0:T(128)S(1)} %get-tuple-element.7), channel_id=1, replica_groups=mesh['tensor'=32,'dp'=16] {'dp'}, use_global_device_ids=true, to_apply=%region_9.0 | all-reduce | flops 16 | bytes 128 | tf_op jit(solution)/shard_map/psum | solution.py:42
  523.7 0.9 fusion.19
  524.6 49.4 %all_gather.15 = bf16[512,768]{1,0:T(8,128)(2,1)S(1)} all-gather(bf16[16,768]{1,0:T(8,128)(2,1)S(1)} %fusion.19), channel_id=1, replica_groups=mesh['tensor'=32,'dp'=16] {'tensor'}, dimensions={0}, use_global_device_ids=true | all-gather | bytes 811008 | tf_op jit(solution)/shard_map/all_gather | solution.py:47
  574.0 2.5 convolution_convert_fusion
  576.5 1.7 fusion.23
  578.2 48.7 %psum.31 = f32[768]{0:T(1024)} all-reduce(f32[768]{0:T(1024)S(1)} %get-tuple-element.6), channel_id=1, replica_groups=mesh['tensor'=32,'dp'=16] {'tensor'}, use_global_device_ids=true, to_apply=%region_11.0 | all-reduce | flops 768 | bytes 6144 | tf_op jit(solution)/shard_map/psum | solution.py:46
  627.0 47.8 %reduce-scatter.8.cloned.1.call-done = bf16[32,448]{1,0:T(8,128)(2,1)} async-done(((bf16[512,448]{1,0:T(8,128)(2,1)}), bf16[32,448]{1,0:T(8,128)(2,1)}) %reduce-scatter.8.cloned.1.call-update) | async-done | bytes 28688 | tf_op jit(solution)/shard_map/reduce_scatter | solution.py:49
  674.7 1.4 fusion.9
  676.2 25.4 %all_gather.14 = bf16[512,448]{1,0:T(8,128)(2,1)S(1)} all-gather(bf16[32,448]{1,0:T(8,128)(2,1)S(1)} %get-tuple-element.10), channel_id=1, replica_groups=mesh['tensor'=32,'dp'=16] {'dp'}, dimensions={0}, use_global_device_ids=true | all-gather | bytes 487424 | tf_op jit(solution)/shard_map/all_gather | solution.py:64
  701.6 1.6 fusion.25
  (26 shorter events, 1.1 us)
Async XLA Ops:
  7.2 95.4 %copy-start = (bf16[512,768]{1,0:T(8,128)(2,1)S(1)}, bf16[512,768]{1,0:T(8,128)(2,1)}, u32[]{:S(2)}) copy-start(bf16[512,768]{1,0:T(8,128)(2,1)} %param.10) | copy-start | bytes 2359300
  7.2 194.6 %reduce-scatter.4.cloned.1.call-start = ((), (), s32[]{:S(2)}) async-start(), calls=%async_computation.3 | async-start | bytes 1114112 | tf_op jit(solution)/shard_map/reduce_scatter | solution.py:23
  102.6 197.5 %copy-start.6 = (f32[32]{0:T(128)S(1)}, f32[32]{0:T(128)}, u32[]{:S(2)}) copy-start(f32[32]{0:T(128)} %param.15) | copy-start | bytes 388
  102.6 197.5 %copy-start.7 = (s32[32]{0:T(128)S(1)}, s32[32]{0:T(128)}, u32[]{:S(2)}) copy-start(s32[32]{0:T(128)} %param.14) | copy-start | bytes 388
  104.2 362.8 %reduce-scatter.6.cloned.1.call-start = ((), (), s32[]{:S(2)}) async-start(), calls=%async_computation.4 | async-start | bytes 1622016 | tf_op jit(solution)/shard_map/reduce_scatter | solution.py:40
  355.2 111.7 %copy-start.1 = (bf16[16,768]{1,0:T(8,128)(2,1)S(1)}, bf16[16,768]{1,0:T(8,128)(2,1)}, u32[]{:S(2)}) copy-start(bf16[16,768]{1,0:T(8,128)(2,1)} %param.8) | copy-start | bytes 73732
  355.2 111.7 %copy-start.3 = (f32[768]{0:T(1024)S(1)}, f32[768]{0:T(1024)}, u32[]{:S(2)}) copy-start(f32[768]{0:T(1024)} %param.9) | copy-start | bytes 9220
  357.0 317.8 %reduce-scatter.8.cloned.1.call-start = ((), (), s32[]{:S(2)}) async-start(), calls=%async_computation.5 | async-start | bytes 557056 | tf_op jit(solution)/shard_map/reduce_scatter | solution.py:49
  524.6 51.9 %copy-start.2 = (bf16[16,768]{1,0:T(8,128)(2,1)}, bf16[16,768]{1,0:T(8,128)(2,1)S(1)}, u32[]{:S(2)}) copy-start(bf16[16,768]{1,0:T(8,128)(2,1)S(1)} %fusion.19) | copy-start | bytes 73732
  576.5 98.3 %copy-start.4 = (bf16[32,448]{1,0:T(8,128)(2,1)S(1)}, bf16[32,448]{1,0:T(8,128)(2,1)}, u32[]{:S(2)}) copy-start(bf16[32,448]{1,0:T(8,128)(2,1)} %param.12) | copy-start | bytes 86020
  576.5 98.3 %copy-start.5 = (bf16[32,448]{1,0:T(8,128)(2,1)S(1)}, bf16[32,448]{1,0:T(8,128)(2,1)}, u32[]{:S(2)}) copy-start(bf16[32,448]{1,0:T(8,128)(2,1)} %param.13) | copy-start | bytes 86020
Sparse Core Ops, SparseCore 0:
  104.3 97.4 reduce-scatter.3
  357.1 109.8 reduce-scatter.5
  576.6 98.0 reduce-scatter.7
where the time goes:
time: 710 us
  blocking collectives  423 us (60%)
  waiting for transfers between devices  255 us (36%)
  between operations  13.8 us (2%)
  matrix products  9.15 us (1%)
  other arithmetic  7.97 us (1%)
    reduce_scatter x1, waiting for transfers between devices, per_device(): lax.psum_scatter(back_rows, 'tensor', scatter_dimension=0, tiled=True)  110 us
    reduce_scatter x1, waiting for transfers between devices, per_device(): lax.psum_scatter(jnp.einsum('td,vd->tv', rows_here, head_weight, preferre...  97.5 us
    psum x1, blocking collectives, per_device(): inner_sums = lax.psum(jnp.sum(scaled * unit_rows, axis=1), 'dp') / D  55.7 us
    all_gather x1, blocking collectives, per_device(): piece = lax.all_gather(dlogits, 'dp', axis=0, tiled=True)  54.2 us
    all_gather x1, blocking collectives, per_device(): normed_all = lax.all_gather(normed, 'tensor', axis=0, tiled=True)  54.2 us
    pmax x1, blocking collectives, per_device(): global_top = lax.pmax(row_top, 'tensor')  50.2 us
    all_gather x1, blocking collectives, per_device(): stream_all = lax.all_gather(stream_grad, 'tensor', axis=0, tiled=True)  49.4 us
    psum x1, blocking collectives, per_device(): gain_grad = lax.psum(jnp.sum(normed_back * unit_rows, axis=0), 'tensor')  48.7 us
  transfers between devices with their start and end apart: 3, of which 3 were waited for; matrix products, arithmetic and copies ran while one was open for 0% of the time, Pallas kernels for 0%

commit v1 on v0

v1 whole, which is shorter than its diff:
```python
import jax
import jax.numpy as jnp
from jax import lax
from jax.sharding import Mesh, PartitionSpec as P

D = 12288
EPSILON = 1e-05
FAR, NEAR = ("za",), ("zb", "yl")
TENSOR = FAR + NEAR
DP = ("yh", "x", "c")
f32, bf16 = jnp.float32, jnp.bfloat16


def exchange(blocks, axes):
    return lax.all_to_all(blocks, axes, 0, 0, tiled=True)


def spread(block, axes, n):
    return exchange(jnp.broadcast_to(block[None], (n,) + block.shape), axes)


def gather_tensor(block):
    far = spread(block, FAR, 4)
    near = spread(far, NEAR, 8)
    return near.transpose(1, 0, 2, 3).reshape(32 * block.shape[0], block.shape[1])


def scatter_tensor(partial):
    rows, columns = partial.shape[0] // 32, partial.shape[1]
    near = exchange(
        partial.reshape(4, 8, rows, columns).transpose(1, 0, 2, 3).astype(bf16), NEAR
    )
    near = jnp.sum(near.astype(f32), axis=0).astype(bf16)
    far = exchange(near, FAR)
    return jnp.sum(far.astype(f32), axis=0)


def split3(v):
    hi = lax.reduce_precision(v, 8, 7)
    mid = lax.reduce_precision(v - hi, 8, 7)
    lo = lax.reduce_precision(v - hi - mid, 8, 7)
    return jnp.stack([hi, mid, lo], axis=-1).astype(bf16)


def join3(s):
    s = s.astype(f32)
    return s[..., 0] + s[..., 1] + s[..., 2]


def gather_and_sum(block, term):
    def join_rows(rows, row):
        extra = jnp.pad(split3(row).T, ((0, 5), (0, 0)))
        return jnp.concatenate([rows, extra], axis=0)

    def sum_rows(got, at):
        extra = got[:, at : at + 3].astype(f32)
        return jnp.sum(extra, axis=(0, 1))

    n = block.shape[0]
    far = spread(join_rows(block, term), FAR, 4)
    term = sum_rows(far, n)
    near = spread(join_rows(far[:, :n].reshape(4 * n, -1), term), NEAR, 8)
    term = sum_rows(near, 4 * n)
    near = near[:, : 4 * n].reshape(8, 4, n, -1)
    return near.transpose(1, 0, 2, 3).reshape(32 * n, -1), term


def per_device(
    stream, norm_gain, head_weight, down_weight, gate_pre, up_pre, targets, token_weight
):
    vocab_local = head_weight.shape[0]
    t = lax.axis_index(TENSOR)
    x_all = gather_tensor(stream).astype(f32)
    xg = (x_all * norm_gain).astype(bf16)
    squares = jnp.sum(x_all * x_all, axis=1)
    part = jnp.einsum("td,vd->tv", xg, head_weight, preferred_element_type=f32).astype(bf16)
    sq = jnp.pad(split3(squares), ((0, 0), (0, 125)))
    got = exchange(jnp.concatenate([part, sq], axis=1).reshape(16, 32, 640), DP)
    got = jnp.sum(got.astype(f32), axis=0)
    inv = lax.rsqrt((got[:, 512] + got[:, 513] + got[:, 514]) / D + EPSILON)
    logits = got[:, :512] * inv[:, None]
    top = jnp.max(logits, axis=1)
    e = jnp.exp(logits - top[:, None])
    columns = t * vocab_local + lax.iota(jnp.int32, vocab_local)
    matches = targets[:, None] == columns[None, :]
    stats = jnp.stack(
        [
            top,
            jnp.sum(e, axis=1),
            jnp.sum(e * logits, axis=1),
            jnp.sum(jnp.where(matches, logits, 0.0), axis=1),
        ]
    ).reshape(1, 128)
    stats = spread(stats, TENSOR, 32).reshape(32, 4, 32)
    tops = stats[:, 0]
    global_top = jnp.max(tops, axis=0)
    scale = jnp.exp(tops - global_top)
    total = jnp.sum(stats[:, 1] * scale, axis=0)
    mean = jnp.sum(stats[:, 2] * scale, axis=0) / total
    inner = token_weight * (mean - jnp.sum(stats[:, 3], axis=0)) / D
    here = jnp.exp(logits - global_top[:, None]) / total[:, None]
    dlogits = ((here - matches.astype(f32)) * token_weight[:, None]).astype(bf16)
    gate_float = gate_pre.astype(f32)
    up_float = up_pre.astype(f32)
    sigmoid_gate = jax.nn.sigmoid(gate_float)
    hidden = (gate_float * sigmoid_gate * up_float).astype(bf16)
    scalars = jnp.pad(
        jnp.concatenate([split3(inv), split3(inner)], axis=1), ((0, 0), (0, 58))
    )
    sent = jnp.concatenate([dlogits, hidden, scalars], axis=1)
    got = spread(sent, DP, 16).reshape(512, 1024)
    piece = got[:, :512]
    hidden_all = got[:, 512:960]
    inv_all = join3(got[:, 960:963])
    inner_all = join3(got[:, 963:966])
    normed_all = (x_all * inv_all[:, None] * norm_gain).astype(bf16)
    weight_part = jnp.einsum("tv,td->vd", piece, normed_all, preferred_element_type=f32)
    back_rows = jnp.dot(piece, head_weight, preferred_element_type=f32)
    normed_back = scatter_tensor(back_rows)
    inv_own = lax.dynamic_slice_in_dim(inv_all, t * 16, 16)[:, None]
    inner_own = lax.dynamic_slice_in_dim(inner_all, t * 16, 16)[:, None]
    unit_rows = stream.astype(f32) * inv_own
    stream_grad = (inv_own * (normed_back * norm_gain - unit_rows * inner_own)).astype(bf16)
    gain_part = jnp.sum(normed_back * unit_rows, axis=0)
    stream_all, gain_grad = gather_and_sum(stream_grad, gain_part)
    hidden_part = jnp.einsum(
        "td,fd->tf", stream_all, down_weight, preferred_element_type=f32
    ).astype(bf16)
    hidden_back = jnp.sum(exchange(hidden_part.reshape(16, 32, 448), DP).astype(f32), axis=0)
    down_grad = jnp.einsum("tf,td->fd", hidden_all, stream_all, preferred_element_type=f32)
    up_grad = (hidden_back * gate_float * sigmoid_gate).astype(bf16)
    gate_grad = (
        hidden_back * up_float * sigmoid_gate * (1.0 + gate_float * (1.0 - sigmoid_gate))
    ).astype(bf16)
    return (weight_part, down_grad, stream_grad, gain_grad, gate_grad, up_grad)


def solution(mesh):
    fine = Mesh(mesh.devices.reshape(4, 4, 2, 2, 4, 2), ("za", "zb", "yl", "yh", "x", "c"))
    return jax.shard_map(
        per_device,
        mesh=fine,
        in_specs=(
            P(TENSOR, DP),
            P(DP),
            P(TENSOR, DP),
            P(TENSOR, DP),
            P(DP, TENSOR),
            P(DP, TENSOR),
            P(DP),
            P(DP),
        ),
        out_specs=(
            P(TENSOR, DP),
            P(TENSOR, DP),
            P(TENSOR, DP),
            P(DP),
            P(DP, TENSOR),
            P(DP, TENSOR),
        ),
        check_vma=False,
    )
```

time: 710 us -> 225 us (0.32)
  blocking collectives: 423 us -> 87.2 us
  waiting for transfers between devices: 255 us -> 80.8 us
  starting transfers between devices: 0.12 us -> 32.7 us
  between operations: 13.8 us -> 1.03 us
  local copies, waits for them, and re-layouts: 0.04 us -> 9.31 us
    reduce_scatter x3 -> x0, waiting for transfers between devices: 255 us -> none  [the longest x1 110 us: per_device(): lax.psum_scatter(back_rows, 'tensor', scatter_dimension=0, tiled=True)]
    psum x4 -> x0, blocking collectives: 190 us -> none  [the longest x1 55.7 us: per_device(): inner_sums = lax.psum(jnp.sum(scaled * unit_rows, axis=1), 'dp') / D]
    all_gather x4 -> x0, blocking collectives: 183 us -> none  [the longest x1 54.2 us: per_device(): piece = lax.all_gather(dlogits, 'dp', axis=0, tiled=True)]
    all_to_all x0 -> x4, blocking collectives: none -> 87.2 us  [exchange(): return lax.all_to_all(blocks, axes, 0, 0, tiled=True)]
    all_to_all x0 -> x6, waiting for transfers between devices: none -> 80.8 us  [exchange(): return lax.all_to_all(blocks, axes, 0, 0, tiled=True)]
    pmax x1 -> x0, blocking collectives: 50.2 us -> none  [per_device(): global_top = lax.pmax(row_top, 'tensor')]
    all_to_all x0 -> x6, starting transfers between devices: none -> 32.7 us  [exchange(): return lax.all_to_all(blocks, axes, 0, 0, tiled=True)]
  transfers between devices with their start and end apart: 3 -> 6, of which waited for: 3 -> 6; matrix products, arithmetic and copies ran while one was open for 0% -> 3% of each run, Pallas kernels for 0% -> 0%
where the time goes in v1:
time: 225 us; the launch traced here: 224 us
  blocking collectives  87.2 us (39%)
  waiting for transfers between devices  80.8 us (36%)
  starting transfers between devices  32.7 us (15%)
  local copies, waits for them, and re-layouts  9.31 us (4%)
  other arithmetic  7.18 us (3%)
  matrix products  5.9 us (3%)
    all_to_all x4, blocking collectives, exchange(): return lax.all_to_all(blocks, axes, 0, 0, tiled=True)  87.2 us
    all_to_all x6, waiting for transfers between devices, exchange(): return lax.all_to_all(blocks, axes, 0, 0, tiled=True)  80.8 us
    all_to_all x6, starting transfers between devices, exchange(): return lax.all_to_all(blocks, axes, 0, 0, tiled=True)  32.7 us
  transfers between devices with their start and end apart: 6, of which 6 were waited for; matrix products, arithmetic and copies ran while one was open for 3% of the time, Pallas kernels for 0%

profile of v1, /device:TPU:1, one launch (start us, length us, event | category | flops | bytes accessed | tf_op | source)
XLA Modules:
  0.0 224.1 jit_solution(14718545052518956043)
XLA Ops:
  1.5 28.0 %all_to_all.50 = bf16[4,16,768]{2,1,0:T(8,128)(2,1)S(1)} all-to-all(bf16[4,16,768]{2,1,0:T(8,128)(2,1)S(1)} %broadcast_in_dim.18), channel_id=1, replica_groups=mesh['za'=4,'zb'=4,'yl'=2,'yh'=2,'x'=4,'c'=2] {'za'}, dimensions={0} | all-to-all | bytes 196608 | tf_op jit(solution)/shard_map/all_to_all | solution.py:15
  29.6 22.2 %all_to_all.51 = bf16[8,4,16,768]{3,2,1,0:T(8,128)(2,1)S(1)} all-to-all(bf16[8,4,16,768]{3,2,1,0:T(8,128)(2,1)S(1)} %broadcast_in_dim.19), channel_id=1, replica_groups=mesh['za'=4,'zb'=4,'yl'=2,'yh'=2,'x'=4,'c'=2] {'zb','yl'}, dimensions={0} | all-to-all | bytes 1572864 | tf_op jit(solution)/shard_map/all_to_all | solution.py:15
  53.0 1.1 copy.104
  54.0 9.4 %all-to-all-start.2 = ((bf16[16,32,640]{2,1,0:T(8,128)(2,1)}), bf16[16,32,640]{2,1,0:T(8,128)(2,1)S(1)}, u32[]{:S(2)}, u32[]{:S(2)}) async-start(bf16[16,32,640]{2,1,0:T(8,128)(2,1)} %bitcast.3), calls=%async_computation.2 | async-start | bytes 1310720 | tf_op jit(solution)/shard_map/all_to_all | solution.py:15
  63.5 12.9 %all-to-all-done.2 = bf16[16,32,640]{2,1,0:T(8,128)(2,1)S(1)} async-done(((bf16[16,32,640]{2,1,0:T(8,128)(2,1)}), bf16[16,32,640]{2,1,0:T(8,128)(2,1)S(1)}, u32[]{:S(2)}, u32[]{:S(2)}) %all-to-all-start.2) | async-done | bytes 655392 | tf_op jit(solution)/shard_map/all_to_all | solution.py:15
  78.0 4.1 %all-to-all-start.3 = ((f32[32,1,128]{2,1,0:T(1,128)}), f32[32,1,128]{2,1,0:T(1,128)S(1)}, u32[]{:S(2)}, u32[]{:S(2)}) async-start(f32[32,1,128]{2,1,0:T(1,128)} %broadcast_in_dim.22), calls=%async_computation.3 | async-start | bytes 32768 | tf_op jit(solution)/shard_map/all_to_all | solution.py:15
  82.1 12.0 %all-to-all-done.3 = f32[32,1,128]{2,1,0:T(1,128)S(1)} async-done(((f32[32,1,128]{2,1,0:T(1,128)}), f32[32,1,128]{2,1,0:T(1,128)S(1)}, u32[]{:S(2)}, u32[]{:S(2)}) %all-to-all-start.3) | async-done | bytes 16416 | tf_op jit(solution)/shard_map/all_to_all | solution.py:15
  96.0 22.0 %all_to_all.52 = bf16[16,32,1024]{2,1,0:T(8,128)(2,1)S(1)} all-to-all(bf16[16,32,1024]{2,1,0:T(8,128)(2,1)S(1)} %broadcast_in_dim.23), channel_id=1, replica_groups=mesh['za'=4,'zb'=4,'yl'=2,'yh'=2,'x'=4,'c'=2] {'yh','x','c'}, dimensions={0} | all-to-all | bytes 2097152 | tf_op jit(solution)/shard_map/all_to_all | solution.py:15
  119.5 3.5 %all-to-all-start.5 = ((bf16[8,4,16,768]{3,2,1,0:T(8,128)(2,1)}), bf16[8,4,16,768]{3,2,1,0:T(8,128)(2,1)S(1)}, u32[]{:S(2)}, u32[]{:S(2)}) async-start(bf16[8,4,16,768]{3,2,1,0:T(8,128)(2,1)} %bitcast.58), calls=%async_computation.5 | async-start | bytes 1572864 | tf_op jit(solution)/shard_map/all_to_all | solution.py:15
  123.1 19.0 %all-to-all-done.5 = bf16[8,4,16,768]{3,2,1,0:T(8,128)(2,1)S(1)} async-done(((bf16[8,4,16,768]{3,2,1,0:T(8,128)(2,1)}), bf16[8,4,16,768]{3,2,1,0:T(8,128)(2,1)S(1)}, u32[]{:S(2)}, u32[]{:S(2)}) %all-to-all-start.5) | async-done | bytes 786464 | tf_op jit(solution)/shard_map/all_to_all | solution.py:15
  142.8 3.3 %all-to-all-start.6 = ((bf16[4,16,768]{2,1,0:T(8,128)(2,1)}), bf16[4,16,768]{2,1,0:T(8,128)(2,1)S(1)}, u32[]{:S(2)}, u32[]{:S(2)}) async-start(bf16[4,16,768]{2,1,0:T(8,128)(2,1)} %reduce_sum.147), calls=%async_computation.6 | async-start | bytes 196608 | tf_op jit(solution)/shard_map/all_to_all | solution.py:15
  146.9 11.1 %all-to-all-done.6 = bf16[4,16,768]{2,1,0:T(8,128)(2,1)S(1)} async-done(((bf16[4,16,768]{2,1,0:T(8,128)(2,1)}), bf16[4,16,768]{2,1,0:T(8,128)(2,1)S(1)}, u32[]{:S(2)}, u32[]{:S(2)}) %all-to-all-start.6) | async-done | bytes 98336 | tf_op jit(solution)/shard_map/all_to_all | solution.py:15
  158.3 15.0 %all_to_all.53 = bf16[4,24,768]{2,1,0:T(8,128)(2,1)S(1)} all-to-all(bf16[4,24,768]{2,1,0:T(8,128)(2,1)S(1)} %broadcast_in_dim.24), channel_id=1, replica_groups=mesh['za'=4,'zb'=4,'yl'=2,'yh'=2,'x'=4,'c'=2] {'za'}, dimensions={0} | all-to-all | bytes 294912 | tf_op jit(solution)/shard_map/all_to_all | solution.py:15
  173.3 1.0 broadcast_in_dim.25
  174.3 4.4 %all-to-all-start.8 = ((bf16[8,72,768]{2,1,0:T(8,128)(2,1)}), bf16[8,72,768]{2,1,0:T(8,128)(2,1)S(1)}, u32[]{:S(2)}, u32[]{:S(2)}) async-start(bf16[8,72,768]{2,1,0:T(8,128)(2,1)} %broadcast_in_dim.25), calls=%async_computation.8 | async-start | bytes 1769472 | tf_op jit(solution)/shard_map/all_to_all | solution.py:15
  178.7 1.1 fusion.3
  179.8 18.3 %all-to-all-done.8 = bf16[8,72,768]{2,1,0:T(8,128)(2,1)S(1)} async-done(((bf16[8,72,768]{2,1,0:T(8,128)(2,1)}), bf16[8,72,768]{2,1,0:T(8,128)(2,1)S(1)}, u32[]{:S(2)}, u32[]{:S(2)}) %all-to-all-start.8) | async-done | bytes 884768 | tf_op jit(solution)/shard_map/all_to_all | solution.py:15
  199.4 1.3 convolution_convert_fusion.2
  200.7 2.0 copy.114
  202.8 8.0 %all-to-all-start.9 = ((bf16[16,32,448]{2,1,0:T(8,128)(2,1)}), bf16[16,32,448]{2,1,0:T(8,128)(2,1)}, u32[]{:S(2)}, u32[]{:S(2)}) async-start(bf16[16,32,448]{2,1,0:T(8,128)(2,1)} %bitcast.62), calls=%async_computation.9 | async-start | bytes 1048576 | tf_op jit(solution)/shard_map/all_to_all | solution.py:15
  210.8 1.8 fusion.7
  213.1 1.6 fusion.4
  214.8 7.6 %all-to-all-done.9 = bf16[16,32,448]{2,1,0:T(8,128)(2,1)} async-done(((bf16[16,32,448]{2,1,0:T(8,128)(2,1)}), bf16[16,32,448]{2,1,0:T(8,128)(2,1)}, u32[]{:S(2)}, u32[]{:S(2)}) %all-to-all-start.9) | async-done | bytes 458784 | tf_op jit(solution)/shard_map/all_to_all | solution.py:15
  222.3 1.1 convert_reduce_fusion.1
  (85 shorter events, 11.3 us)
Async XLA Ops:
  0.6 51.6 %copy-start = (bf16[512,768]{1,0:T(8,128)(2,1)S(1)}, bf16[512,768]{1,0:T(8,128)(2,1)}, u32[]{:S(2)}) copy-start(bf16[512,768]{1,0:T(8,128)(2,1)} %param.10) | copy-start | bytes 2359300
  29.5 22.6 %copy-start.9 = (f32[768]{0:T(1024)S(1)}, f32[768]{0:T(1024)}, u32[]{:S(2)}) copy-start(f32[768]{0:T(1024)} %param.9) | copy-start | bytes 9220
  52.9 10.5 %copy-start.4 = (bf16[32,448]{1,0:T(8,128)(2,1)S(1)}, bf16[32,448]{1,0:T(8,128)(2,1)}, u32[]{:S(2)}) copy-start(bf16[32,448]{1,0:T(8,128)(2,1)} %param.13) | copy-start | bytes 86020
  52.9 10.5 %copy-start.5 = (bf16[32,448]{1,0:T(8,128)(2,1)S(1)}, bf16[32,448]{1,0:T(8,128)(2,1)}, u32[]{:S(2)}) copy-start(bf16[32,448]{1,0:T(8,128)(2,1)} %param.12) | copy-start | bytes 86020
  53.0 24.1 %copy-start.10 = (s32[32]{0:T(128)S(1)}, s32[32]{0:T(128)}, u32[]{:S(2)}) copy-start(s32[32]{0:T(128)} %param.14) | copy-start | bytes 388
  54.0 41.4 %copy-start.11 = (f32[32]{0:T(128)S(1)}, f32[32]{0:T(128)}, u32[]{:S(2)}) copy-start(f32[32]{0:T(128)} %param.15) | copy-start | bytes 388
  54.0 22.3 %all-to-all-start.2 = ((bf16[16,32,640]{2,1,0:T(8,128)(2,1)}), bf16[16,32,640]{2,1,0:T(8,128)(2,1)S(1)}, u32[]{:S(2)}, u32[]{:S(2)}) async-start(bf16[16,32,640]{2,1,0:T(8,128)(2,1)} %bitcast.3), calls=%async_computation.2 | async-start | bytes 1310720 | tf_op jit(solution)/shard_map/all_to_all | solution.py:15
  78.0 16.1 %all-to-all-start.3 = ((f32[32,1,128]{2,1,0:T(1,128)}), f32[32,1,128]{2,1,0:T(1,128)S(1)}, u32[]{:S(2)}, u32[]{:S(2)}) async-start(f32[32,1,128]{2,1,0:T(1,128)} %broadcast_in_dim.22), calls=%async_computation.3 | async-start | bytes 32768 | tf_op jit(solution)/shard_map/all_to_all | solution.py:15
  119.5 22.5 %all-to-all-start.5 = ((bf16[8,4,16,768]{3,2,1,0:T(8,128)(2,1)}), bf16[8,4,16,768]{3,2,1,0:T(8,128)(2,1)S(1)}, u32[]{:S(2)}, u32[]{:S(2)}) async-start(bf16[8,4,16,768]{3,2,1,0:T(8,128)(2,1)} %bitcast.58), calls=%async_computation.5 | async-start | bytes 1572864 | tf_op jit(solution)/shard_map/all_to_all | solution.py:15
  142.8 15.3 %all-to-all-start.6 = ((bf16[4,16,768]{2,1,0:T(8,128)(2,1)}), bf16[4,16,768]{2,1,0:T(8,128)(2,1)S(1)}, u32[]{:S(2)}, u32[]{:S(2)}) async-start(bf16[4,16,768]{2,1,0:T(8,128)(2,1)} %reduce_sum.147), calls=%async_computation.6 | async-start | bytes 196608 | tf_op jit(solution)/shard_map/all_to_all | solution.py:15
  146.2 11.8 %copy-start.8 = (bf16[16,768]{1,0:T(8,128)(2,1)S(1)}, bf16[16,768]{1,0:T(8,128)(2,1)}, u32[]{:S(2)}) copy-start(bf16[16,768]{1,0:T(8,128)(2,1)} %param.8) | copy-start | bytes 73732
  158.2 16.2 %copy-start.7 = (bf16[16,768]{1,0:T(8,128)(2,1)}, bf16[16,768]{1,0:T(8,128)(2,1)S(1)}, u32[]{:S(2)}) copy-start(bf16[16,768]{1,0:T(8,128)(2,1)S(1)} %get-tuple-element.45) | copy-start | bytes 73732
  174.3 23.8 %all-to-all-start.8 = ((bf16[8,72,768]{2,1,0:T(8,128)(2,1)}), bf16[8,72,768]{2,1,0:T(8,128)(2,1)S(1)}, u32[]{:S(2)}, u32[]{:S(2)}) async-start(bf16[8,72,768]{2,1,0:T(8,128)(2,1)} %broadcast_in_dim.25), calls=%async_computation.8 | async-start | bytes 1769472 | tf_op jit(solution)/shard_map/all_to_all | solution.py:15
  198.2 1.2 copy-start.12
  198.3 0.9 copy-start.2
  199.4 11.3 %copy-start.1 = (bf16[512,768]{1,0:T(8,128)(2,1)S(1)}, bf16[512,768]{1,0:T(8,128)(2,1)}, u32[]{:S(2)}) copy-start(bf16[512,768]{1,0:T(8,128)(2,1)} %fusion.3) | copy-start | bytes 2359300
  202.8 19.6 %all-to-all-start.9 = ((bf16[16,32,448]{2,1,0:T(8,128)(2,1)}), bf16[16,32,448]{2,1,0:T(8,128)(2,1)}, u32[]{:S(2)}, u32[]{:S(2)}) async-start(bf16[16,32,448]{2,1,0:T(8,128)(2,1)} %bitcast.62), calls=%async_computation.9 | async-start | bytes 1048576 | tf_op jit(solution)/shard_map/all_to_all | solution.py:15
  210.8 2.4 %copy-start.3 = (bf16[4,8,16,768]{3,2,1,0:T(8,128)(2,1)S(1)}, bf16[4,8,16,768]{3,2,1,0:T(8,128)(2,1)}, u32[]{:S(2)}) copy-start(bf16[4,8,16,768]{3,2,1,0:T(8,128)(2,1)} %copy-done.2) | copy-start | bytes 2359300
  213.1 10.3 %copy-start.6 = (bf16[32,448]{1,0:T(8,128)(2,1)S(1)}, bf16[32,448]{1,0:T(8,128)(2,1)}, u32[]{:S(2)}) copy-start(bf16[32,448]{1,0:T(8,128)(2,1)} %param.12) | copy-start | bytes 86020

commit v2 on v1

--- a/solution.py
+++ b/solution.py
@@ -5,9 +5,10 @@
 
 D = 12288
 EPSILON = 1e-05
-FAR, NEAR = ("za",), ("zb", "yl")
+FAR, NEAR = ("zf",), ("zn", "yl")
 TENSOR = FAR + NEAR
 DP = ("yh", "x", "c")
+FARS, NEARS = 8, 4
 f32, bf16 = jnp.float32, jnp.bfloat16
 
 
@@ -20,16 +21,16 @@
 
 
 def gather_tensor(block):
-    far = spread(block, FAR, 4)
-    near = spread(far, NEAR, 8)
-    return near.transpose(1, 0, 2, 3).reshape(32 * block.shape[0], block.shape[1])
+    return spread(spread(block, FAR, FARS), NEAR, NEARS)
+
+
+def in_order(blocks):
+    return blocks.transpose(1, 0, 2, 3).reshape(-1, blocks.shape[-1])
 
 
 def scatter_tensor(partial):
     rows, columns = partial.shape[0] // 32, partial.shape[1]
-    near = exchange(
-        partial.reshape(4, 8, rows, columns).transpose(1, 0, 2, 3).astype(bf16), NEAR
-    )
+    near = exchange(partial.reshape(NEARS, FARS, rows, columns).astype(bf16), NEAR)
     near = jnp.sum(near.astype(f32), axis=0).astype(bf16)
     far = exchange(near, FAR)
     return jnp.sum(far.astype(f32), axis=0)
@@ -48,21 +49,17 @@
 
 
 def gather_and_sum(block, term):
-    def join_rows(rows, row):
-        extra = jnp.pad(split3(row).T, ((0, 5), (0, 0)))
-        return jnp.concatenate([rows, extra], axis=0)
-
-    def sum_rows(got, at):
-        extra = got[:, at : at + 3].astype(f32)
-        return jnp.sum(extra, axis=(0, 1))
-
-    n = block.shape[0]
-    far = spread(join_rows(block, term), FAR, 4)
-    term = sum_rows(far, n)
-    near = spread(join_rows(far[:, :n].reshape(4 * n, -1), term), NEAR, 8)
-    term = sum_rows(near, 4 * n)
-    near = near[:, : 4 * n].reshape(8, 4, n, -1)
-    return near.transpose(1, 0, 2, 3).reshape(32 * n, -1), term
+    n, columns = block.shape
+    pair = split3(term)[:, :2].T.reshape(2 * columns // 128, 128)
+    side = jnp.pad(pair, ((0, n - pair.shape[0]), (0, 0)))
+    far = spread(jnp.concatenate([block, side], axis=1), FAR, FARS)
+    side = far[:, : pair.shape[0], columns:].astype(f32).reshape(FARS, 2, columns)
+    term = jnp.sum(side, axis=(0, 1))
+    rows = far[:, :, :columns].reshape(FARS * n, columns)
+    extra = jnp.pad(split3(term).T, ((0, 5), (0, 0)))
+    near = spread(jnp.concatenate([rows, extra], axis=0), NEAR, NEARS)
+    term = jnp.sum(near[:, FARS * n : FARS * n + 3].astype(f32), axis=(0, 1))
+    return near[:, : FARS * n].reshape(NEARS, FARS, n, columns), term
 
 
 def per_device(
@@ -70,8 +67,8 @@
 ):
     vocab_local = head_weight.shape[0]
     t = lax.axis_index(TENSOR)
-    x_all = gather_tensor(stream).astype(f32)
-    xg = (x_all * norm_gain).astype(bf16)
+    x_all = in_order(gather_tensor(stream)).astype(f32)
+    xg = lax.optimization_barrier((x_all * norm_gain).astype(bf16))
     squares = jnp.sum(x_all * x_all, axis=1)
     part = jnp.einsum("td,vd->tv", xg, head_weight, preferred_element_type=f32).astype(bf16)
     sq = jnp.pad(split3(squares), ((0, 0), (0, 125)))
@@ -115,7 +112,9 @@
     inner_all = join3(got[:, 963:966])
     normed_all = (x_all * inv_all[:, None] * norm_gain).astype(bf16)
     weight_part = jnp.einsum("tv,td->vd", piece, normed_all, preferred_element_type=f32)
-    back_rows = jnp.dot(piece, head_weight, preferred_element_type=f32)
+    mixed = piece.reshape(FARS, NEARS, 16, vocab_local).transpose(1, 0, 2, 3)
+    mixed = lax.optimization_barrier(mixed.reshape(512, vocab_local))
+    back_rows = jnp.dot(mixed, head_weight, preferred_element_type=f32)
     normed_back = scatter_tensor(back_rows)
     inv_own = lax.dynamic_slice_in_dim(inv_all, t * 16, 16)[:, None]
     inner_own = lax.dynamic_slice_in_dim(inner_all, t * 16, 16)[:, None]
@@ -123,6 +122,7 @@
     stream_grad = (inv_own * (normed_back * norm_gain - unit_rows * inner_own)).astype(bf16)
     gain_part = jnp.sum(normed_back * unit_rows, axis=0)
     stream_all, gain_grad = gather_and_sum(stream_grad, gain_part)
+    stream_all = lax.optimization_barrier(in_order(stream_all))
     hidden_part = jnp.einsum(
         "td,fd->tf", stream_all, down_weight, preferred_element_type=f32
     ).astype(bf16)
@@ -136,7 +136,7 @@
 
 
 def solution(mesh):
-    fine = Mesh(mesh.devices.reshape(4, 4, 2, 2, 4, 2), ("za", "zb", "yl", "yh", "x", "c"))
+    fine = Mesh(mesh.devices.reshape(8, 2, 2, 2, 4, 2), ("zf", "zn", "yl", "yh", "x", "c"))
     return jax.shard_map(
         per_device,
         mesh=fine,

time: 225 us -> 209 us (0.929)
  waiting for transfers between devices: 80.8 us -> 52.6 us
  blocking collectives: 87.2 us -> 95.6 us
  starting transfers between devices: 32.7 us -> 37.7 us
    all_to_all x6 -> x5, waiting for transfers between devices: 80.8 us -> 52.6 us  [exchange(): return lax.all_to_all(blocks, axes, 0, 0, tiled=True)]
    all_to_all x4 -> x5, blocking collectives: 87.2 us -> 95.6 us  [exchange(): return lax.all_to_all(blocks, axes, 0, 0, tiled=True)]
    all_to_all x6 -> x5, starting transfers between devices: 32.7 us -> 37.7 us  [exchange(): return lax.all_to_all(blocks, axes, 0, 0, tiled=True)]
  transfers between devices with their start and end apart: 6 -> 5, of which waited for: 6 -> 5; matrix products, arithmetic and copies ran while one was open for 3% -> 3% of each run, Pallas kernels for 0% -> 0%
where the time goes in v2:
time: 209 us; the launch traced here: 208 us
  blocking collectives  95.6 us (46%)
  waiting for transfers between devices  52.6 us (25%)
  starting transfers between devices  37.7 us (18%)
  local copies, waits for them, and re-layouts  8.46 us (4%)
  other arithmetic  7.27 us (3%)
  matrix products  5.89 us (3%)
    all_to_all x5, blocking collectives, exchange(): return lax.all_to_all(blocks, axes, 0, 0, tiled=True)  95.6 us
    all_to_all x5, waiting for transfers between devices, exchange(): return lax.all_to_all(blocks, axes, 0, 0, tiled=True)  52.6 us
    all_to_all x5, starting transfers between devices, exchange(): return lax.all_to_all(blocks, axes, 0, 0, tiled=True)  37.7 us
  transfers between devices with their start and end apart: 5, of which 5 were waited for; matrix products, arithmetic and copies ran while one was open for 3% of the time, Pallas kernels for 0%

profile of v2, /device:TPU:1, one launch (start us, length us, event | category | flops | bytes accessed | tf_op | source)
XLA Modules:
  0.0 208.5 jit_solution(7918724598998339565)
XLA Ops:
  1.5 30.6 %all_to_all.50 = bf16[8,16,768]{2,1,0:T(8,128)(2,1)S(1)} all-to-all(bf16[8,16,768]{2,1,0:T(8,128)(2,1)S(1)} %broadcast_in_dim.18), channel_id=1, replica_groups=mesh['zf'=8,'zn'=2,'yl'=2,'yh'=2,'x'=4,'c'=2] {'zf'}, dimensions={0} | all-to-all | bytes 393216 | tf_op jit(solution)/shard_map/all_to_all | solution.py:16
  32.1 9.9 %all_to_all.51 = bf16[4,8,16,768]{3,2,1,0:T(8,128)(2,1)S(1)} all-to-all(bf16[4,8,16,768]{3,2,1,0:T(8,128)(2,1)S(1)} %broadcast_in_dim.19), channel_id=1, replica_groups=mesh['zf'=8,'zn'=2,'yl'=2,'yh'=2,'x'=4,'c'=2] {'zn','yl'}, dimensions={0} | all-to-all | bytes 1572864 | tf_op jit(solution)/shard_map/all_to_all | solution.py:16
  43.2 1.1 copy.106
  44.3 12.6 %all-to-all-start.2 = ((bf16[16,32,640]{2,1,0:T(8,128)(2,1)}), bf16[16,32,640]{2,1,0:T(8,128)(2,1)S(1)}, u32[]{:S(2)}, u32[]{:S(2)}) async-start(bf16[16,32,640]{2,1,0:T(8,128)(2,1)} %bitcast.3), calls=%async_computation.2 | async-start | bytes 1310720 | tf_op jit(solution)/shard_map/all_to_all | solution.py:16
  57.0 12.9 %all-to-all-done.2 = bf16[16,32,640]{2,1,0:T(8,128)(2,1)S(1)} async-done(((bf16[16,32,640]{2,1,0:T(8,128)(2,1)}), bf16[16,32,640]{2,1,0:T(8,128)(2,1)S(1)}, u32[]{:S(2)}, u32[]{:S(2)}) %all-to-all-start.2) | async-done | bytes 655392 | tf_op jit(solution)/shard_map/all_to_all | solution.py:16
  71.4 6.2 %all-to-all-start.3 = ((f32[32,1,128]{2,1,0:T(1,128)}), f32[32,1,128]{2,1,0:T(1,128)S(1)}, u32[]{:S(2)}, u32[]{:S(2)}) async-start(f32[32,1,128]{2,1,0:T(1,128)} %broadcast_in_dim.22), calls=%async_computation.3 | async-start | bytes 32768 | tf_op jit(solution)/shard_map/all_to_all | solution.py:16
  77.6 12.0 %all-to-all-done.3 = f32[32,1,128]{2,1,0:T(1,128)S(1)} async-done(((f32[32,1,128]{2,1,0:T(1,128)}), f32[32,1,128]{2,1,0:T(1,128)S(1)}, u32[]{:S(2)}, u32[]{:S(2)}) %all-to-all-start.3) | async-done | bytes 16416 | tf_op jit(solution)/shard_map/all_to_all | solution.py:16
  91.5 21.9 %all_to_all.52 = bf16[16,32,1024]{2,1,0:T(8,128)(2,1)S(1)} all-to-all(bf16[16,32,1024]{2,1,0:T(8,128)(2,1)S(1)} %broadcast_in_dim.23), channel_id=1, replica_groups=mesh['zf'=8,'zn'=2,'yl'=2,'yh'=2,'x'=4,'c'=2] {'yh','x','c'}, dimensions={0} | all-to-all | bytes 2097152 | tf_op jit(solution)/shard_map/all_to_all | solution.py:16
  114.1 12.4 %all_to_all.53 = bf16[4,8,16,768]{3,2,1,0:T(8,128)(2,1)S(1)} all-to-all(bf16[4,8,16,768]{3,2,1,0:T(8,128)(2,1)S(1)} %bitcast.65), channel_id=1, replica_groups=mesh['zf'=8,'zn'=2,'yl'=2,'yh'=2,'x'=4,'c'=2] {'zn','yl'}, dimensions={0} | all-to-all | bytes 1572864 | tf_op jit(solution)/shard_map/all_to_all | solution.py:16
  127.3 3.4 %all-to-all-start.6 = ((bf16[8,16,768]{2,1,0:T(8,128)(2,1)}), bf16[8,16,768]{2,1,0:T(8,128)(2,1)S(1)}, u32[]{:S(2)}, u32[]{:S(2)}) async-start(bf16[8,16,768]{2,1,0:T(8,128)(2,1)} %reduce_sum.154), calls=%async_computation.6 | async-start | bytes 393216 | tf_op jit(solution)/shard_map/all_to_all | solution.py:16
  131.5 14.3 %all-to-all-done.6 = bf16[8,16,768]{2,1,0:T(8,128)(2,1)S(1)} async-done(((bf16[8,16,768]{2,1,0:T(8,128)(2,1)}), bf16[8,16,768]{2,1,0:T(8,128)(2,1)S(1)}, u32[]{:S(2)}, u32[]{:S(2)}) %all-to-all-start.6) | async-done | bytes 196640 | tf_op jit(solution)/shard_map/all_to_all | solution.py:16
  146.0 20.8 %all_to_all.54 = bf16[8,16,896]{2,1,0:T(8,128)(2,1)S(1)} all-to-all(bf16[8,16,896]{2,1,0:T(8,128)(2,1)S(1)} %broadcast_in_dim.24), channel_id=1, replica_groups=mesh['zf'=8,'zn'=2,'yl'=2,'yh'=2,'x'=4,'c'=2] {'zf'}, dimensions={0} | all-to-all | bytes 458752 | tf_op jit(solution)/shard_map/all_to_all | solution.py:16
  167.0 1.0 broadcast_in_dim.25
  168.0 3.5 %all-to-all-start.8 = ((bf16[4,136,768]{2,1,0:T(8,128)(2,1)}), bf16[4,136,768]{2,1,0:T(8,128)(2,1)S(1)}, u32[]{:S(2)}, u32[]{:S(2)}) async-start(bf16[4,136,768]{2,1,0:T(8,128)(2,1)} %broadcast_in_dim.25), calls=%async_computation.8 | async-start | bytes 1671168 | tf_op jit(solution)/shard_map/all_to_all | solution.py:16
  171.5 1.1 fusion.3
  172.6 6.0 %all-to-all-done.8 = bf16[4,136,768]{2,1,0:T(8,128)(2,1)S(1)} async-done(((bf16[4,136,768]{2,1,0:T(8,128)(2,1)}), bf16[4,136,768]{2,1,0:T(8,128)(2,1)S(1)}, u32[]{:S(2)}, u32[]{:S(2)}) %all-to-all-start.8) | async-done | bytes 835616 | tf_op jit(solution)/shard_map/all_to_all | solution.py:16
  178.7 0.9 copy-done.2
  179.8 1.3 convolution_convert_fusion.2
  181.1 2.0 copy.116
  183.2 12.0 %all-to-all-start.9 = ((bf16[16,32,448]{2,1,0:T(8,128)(2,1)}), bf16[16,32,448]{2,1,0:T(8,128)(2,1)}, u32[]{:S(2)}, u32[]{:S(2)}) async-start(bf16[16,32,448]{2,1,0:T(8,128)(2,1)} %bitcast.63), calls=%async_computation.9 | async-start | bytes 1048576 | tf_op jit(solution)/shard_map/all_to_all | solution.py:16
  195.2 1.8 fusion.47
  197.5 1.6 fusion.4
  199.2 7.5 %all-to-all-done.9 = bf16[16,32,448]{2,1,0:T(8,128)(2,1)} async-done(((bf16[16,32,448]{2,1,0:T(8,128)(2,1)}), bf16[16,32,448]{2,1,0:T(8,128)(2,1)}, u32[]{:S(2)}, u32[]{:S(2)}) %all-to-all-start.9) | async-done | bytes 458784 | tf_op jit(solution)/shard_map/all_to_all | solution.py:16
  206.7 1.1 convert_reduce_fusion.1
  (86 shorter events, 9.7 us)
Async XLA Ops:
  0.6 41.9 %copy-start = (bf16[512,768]{1,0:T(8,128)(2,1)S(1)}, bf16[512,768]{1,0:T(8,128)(2,1)}, u32[]{:S(2)}) copy-start(bf16[512,768]{1,0:T(8,128)(2,1)} %param.10) | copy-start | bytes 2359300
  32.0 10.3 %copy-start.8 = (f32[768]{0:T(1024)S(1)}, f32[768]{0:T(1024)}, u32[]{:S(2)}) copy-start(f32[768]{0:T(1024)} %param.9) | copy-start | bytes 9220
  43.2 13.7 %copy-start.4 = (bf16[32,448]{1,0:T(8,128)(2,1)S(1)}, bf16[32,448]{1,0:T(8,128)(2,1)}, u32[]{:S(2)}) copy-start(bf16[32,448]{1,0:T(8,128)(2,1)} %param.13) | copy-start | bytes 86020
  43.2 13.7 %copy-start.5 = (bf16[32,448]{1,0:T(8,128)(2,1)S(1)}, bf16[32,448]{1,0:T(8,128)(2,1)}, u32[]{:S(2)}) copy-start(bf16[32,448]{1,0:T(8,128)(2,1)} %param.12) | copy-start | bytes 86020
  43.2 27.3 %copy-start.9 = (s32[32]{0:T(128)S(1)}, s32[32]{0:T(128)}, u32[]{:S(2)}) copy-start(s32[32]{0:T(128)} %param.14) | copy-start | bytes 388
  44.3 46.7 %copy-start.10 = (f32[32]{0:T(128)S(1)}, f32[32]{0:T(128)}, u32[]{:S(2)}) copy-start(f32[32]{0:T(128)} %param.15) | copy-start | bytes 388
  44.3 25.5 %all-to-all-start.2 = ((bf16[16,32,640]{2,1,0:T(8,128)(2,1)}), bf16[16,32,640]{2,1,0:T(8,128)(2,1)S(1)}, u32[]{:S(2)}, u32[]{:S(2)}) async-start(bf16[16,32,640]{2,1,0:T(8,128)(2,1)} %bitcast.3), calls=%async_computation.2 | async-start | bytes 1310720 | tf_op jit(solution)/shard_map/all_to_all | solution.py:16
  71.4 18.1 %all-to-all-start.3 = ((f32[32,1,128]{2,1,0:T(1,128)}), f32[32,1,128]{2,1,0:T(1,128)S(1)}, u32[]{:S(2)}, u32[]{:S(2)}) async-start(f32[32,1,128]{2,1,0:T(1,128)} %broadcast_in_dim.22), calls=%async_computation.3 | async-start | bytes 32768 | tf_op jit(solution)/shard_map/all_to_all | solution.py:16
  127.3 18.5 %all-to-all-start.6 = ((bf16[8,16,768]{2,1,0:T(8,128)(2,1)}), bf16[8,16,768]{2,1,0:T(8,128)(2,1)S(1)}, u32[]{:S(2)}, u32[]{:S(2)}) async-start(bf16[8,16,768]{2,1,0:T(8,128)(2,1)} %reduce_sum.154), calls=%async_computation.6 | async-start | bytes 393216 | tf_op jit(solution)/shard_map/all_to_all | solution.py:16
  130.8 15.0 %copy-start.6 = (bf16[16,768]{1,0:T(8,128)(2,1)S(1)}, bf16[16,768]{1,0:T(8,128)(2,1)}, u32[]{:S(2)}) copy-start(bf16[16,768]{1,0:T(8,128)(2,1)} %param.8) | copy-start | bytes 73732
  145.9 22.0 %copy-start.7 = (bf16[16,768]{1,0:T(8,128)(2,1)}, bf16[16,768]{1,0:T(8,128)(2,1)S(1)}, u32[]{:S(2)}) copy-start(bf16[16,768]{1,0:T(8,128)(2,1)S(1)} %get-tuple-element.45) | copy-start | bytes 73732
  168.0 10.6 %all-to-all-start.8 = ((bf16[4,136,768]{2,1,0:T(8,128)(2,1)}), bf16[4,136,768]{2,1,0:T(8,128)(2,1)S(1)}, u32[]{:S(2)}, u32[]{:S(2)}) async-start(bf16[4,136,768]{2,1,0:T(8,128)(2,1)} %broadcast_in_dim.25), calls=%async_computation.8 | async-start | bytes 1671168 | tf_op jit(solution)/shard_map/all_to_all | solution.py:16
  178.6 1.2 copy-start.11
  178.7 0.9 copy-start.2
  179.8 15.3 %copy-start.1 = (bf16[512,768]{1,0:T(8,128)(2,1)S(1)}, bf16[512,768]{1,0:T(8,128)(2,1)}, u32[]{:S(2)}) copy-start(bf16[512,768]{1,0:T(8,128)(2,1)} %fusion.3) | copy-start | bytes 2359300
  183.2 23.5 %all-to-all-start.9 = ((bf16[16,32,448]{2,1,0:T(8,128)(2,1)}), bf16[16,32,448]{2,1,0:T(8,128)(2,1)}, u32[]{:S(2)}, u32[]{:S(2)}) async-start(bf16[16,32,448]{2,1,0:T(8,128)(2,1)} %bitcast.63), calls=%async_computation.9 | async-start | bytes 1048576 | tf_op jit(solution)/shard_map/all_to_all | solution.py:16
  195.2 2.4 %copy-start.3 = (bf16[8,4,16,768]{3,2,1,0:T(8,128)(2,1)S(1)}, bf16[8,4,16,768]{3,2,1,0:T(8,128)(2,1)}, u32[]{:S(2)}) copy-start(bf16[8,4,16,768]{3,2,1,0:T(8,128)(2,1)} %copy-done.2) | copy-start | bytes 2359300

commit v3 on v2

v3 whole, which is shorter than its diff:
```python
import jax
import jax.numpy as jnp
from jax import lax
from jax.experimental import pallas as pl
from jax.experimental.pallas import tpu as pltpu
from jax.sharding import Mesh, PartitionSpec as P

D = 12288
EPSILON = 1e-05
FAR, NEAR = ("zf",), ("zn", "yl")
TENSOR = FAR + NEAR
DP = ("yh", "x", "c")
FARS, NEARS = 8, 4
f32, bf16 = jnp.float32, jnp.bfloat16


def on_core(kernel, outs, *args, flops=0):
    whole = pl.BlockSpec(memory_space=pltpu.VMEM)
    outs = [jax.ShapeDtypeStruct(s, d) for s, d in outs]
    moved = sum(a.size * a.dtype.itemsize for a in list(args) + outs)
    return pl.pallas_call(
        kernel,
        out_shape=outs,
        in_specs=[whole] * len(args),
        out_specs=[whole] * len(outs),
        compiler_params=pltpu.CompilerParams(vmem_limit_bytes=16 << 20),
        cost_estimate=pl.CostEstimate(flops=flops, bytes_accessed=moved, transcendentals=0),
    )(*args)


def exchange(blocks, axes):
    return lax.all_to_all(blocks, axes, 0, 0, tiled=True)


def spread(block, axes, n):
    return exchange(jnp.broadcast_to(block[None], (n,) + block.shape), axes)


def gather_tensor(block):
    return spread(spread(block, FAR, FARS), NEAR, NEARS)


def in_order(blocks):
    return blocks.transpose(1, 0, 2, 3).reshape(-1, blocks.shape[-1])


def scatter_tensor(partial):
    rows, columns = partial.shape[0] // 32, partial.shape[1]
    near = exchange(partial.reshape(NEARS, FARS, rows, columns).astype(bf16), NEAR)
    near = jnp.sum(near.astype(f32), axis=0).astype(bf16)
    far = exchange(near, FAR)
    return jnp.sum(far.astype(f32), axis=0)


def split3(v):
    hi = lax.reduce_precision(v, 8, 7)
    mid = lax.reduce_precision(v - hi, 8, 7)
    lo = lax.reduce_precision(v - hi - mid, 8, 7)
    return jnp.stack([hi, mid, lo], axis=-1).astype(bf16)


def join3(s):
    s = s.astype(f32)
    return s[..., 0] + s[..., 1] + s[..., 2]


def gather_and_sum(block, term):
    n, columns = block.shape
    pair = split3(term)[:, :2].T.reshape(2 * columns // 128, 128)
    side = jnp.pad(pair, ((0, n - pair.shape[0]), (0, 0)))
    far = spread(jnp.concatenate([block, side], axis=1), FAR, FARS)
    side = far[:, : pair.shape[0], columns:].astype(f32).reshape(FARS, 2, columns)
    term = jnp.sum(side, axis=(0, 1))
    rows = far[:, :, :columns].reshape(FARS * n, columns)
    extra = jnp.pad(split3(term).T, ((0, 5), (0, 0)))
    return spread(jnp.concatenate([rows, extra], axis=0), NEAR, NEARS)


def token_rows(ref, first, count):
    return jnp.concatenate(
        [ref[n, f * 16 : f * 16 + 16] for f in range(first, first + count) for n in range(NEARS)]
    )


def columns_of(parts, width):
    lane = lax.broadcasted_iota(jnp.int32, (parts[0].shape[0], width), 1)
    out = jnp.zeros((parts[0].shape[0], width), f32)
    for k, part in enumerate(parts):
        out = jnp.where(lane == k, part, out)
    return out


def thirds(v):
    hi = v.astype(bf16).astype(f32)
    mid = (v - hi).astype(bf16).astype(f32)
    return [hi, mid, v - hi - mid]


def logits_kernel(x_ref, gain_ref, weight_ref, out_ref):
    for half in range(2):
        x = token_rows(x_ref, 4 * half, 4).astype(f32)
        scaled = (x * gain_ref[...]).astype(bf16)
        part = lax.dot_general(
            scaled, weight_ref[...], (((1,), (1,)), ((), ())), preferred_element_type=f32
        )
        rows = pl.ds(256 * half, 256)
        out_ref[rows, :512] = part.astype(bf16)
        squares = jnp.sum(x * x, axis=1, keepdims=True)
        out_ref[rows, 512:] = columns_of(thirds(squares), 128).astype(bf16)


def row_of(columns):
    lane = lax.broadcasted_iota(jnp.int32, (32, 128), 1)
    token = lax.broadcasted_iota(jnp.int32, (32, 128), 0)
    spreaded = jnp.zeros((32, 128), f32)
    for k, column in enumerate(columns):
        spreaded = jnp.where(lane == token + 32 * k, column, spreaded)
    return jnp.sum(spreaded, axis=0, keepdims=True)


def column_of(row):
    lane = lax.broadcasted_iota(jnp.int32, (32, 128), 1)
    token = lax.broadcasted_iota(jnp.int32, (32, 128), 0)
    return jnp.sum(jnp.where(lane == token, row, 0.0), axis=1, keepdims=True)


def stats_kernel(got_ref, mark_ref, logits_ref, inv_ref, stats_ref):
    total = jnp.zeros((32, 640), f32)
    for k in range(16):
        total = total + got_ref[k].astype(f32)
    squares = jnp.sum(total[:, 512:], axis=1, keepdims=True)
    inv = lax.rsqrt(squares / D + EPSILON)
    logits = total[:, :512] * inv
    top = jnp.max(logits, axis=1, keepdims=True)
    e = jnp.exp(logits - top)
    row = row_of(
        [
            top,
            jnp.sum(e, axis=1, keepdims=True),
            jnp.sum(e * logits, axis=1, keepdims=True),
            jnp.sum(logits * mark_ref[...], axis=1, keepdims=True),
        ]
    )
    logits_ref[...] = logits
    inv_ref[...] = jnp.broadcast_to(inv, (32, 128))
    stats_ref[...] = jnp.broadcast_to(row[None], (32, 1, 128))


def dlogits_kernel(stats_ref, logits_ref, inv_ref, mark_ref, weight_ref, hidden_ref, out_ref):
    stats = stats_ref[...].reshape(32, 128)
    lane = lax.broadcasted_iota(jnp.int32, (32, 128), 1)
    top = jnp.max(stats, axis=0, keepdims=True)
    scale = jnp.exp(jnp.where(lane < 32, stats - top, 0.0))
    sums = pltpu.roll(stats, 96, 1)
    means = pltpu.roll(stats, 64, 1)
    picked = pltpu.roll(stats, 32, 1)
    total = jnp.sum(sums * scale, axis=0, keepdims=True)
    mean = jnp.sum(means * scale, axis=0, keepdims=True) / total
    inner = mean - jnp.sum(picked, axis=0, keepdims=True)
    weight = weight_ref[:, :1]
    top, total, inner = column_of(top), column_of(total), column_of(inner) * weight / D
    probability = jnp.exp(logits_ref[...] - top) / total
    dlogits = ((probability - mark_ref[...]) * weight).astype(bf16)
    tail = columns_of(thirds(inv_ref[:, :1]) + thirds(inner), 64).astype(bf16)
    for k in range(16):
        out_ref[k, :, :512] = dlogits
        out_ref[k, :, 512:960] = hidden_ref[...]
        out_ref[k, :, 960:] = tail


def hidden_back_kernel(rows_ref, weight_ref, out_ref):
    for half in range(2):
        part = lax.dot_general(
            token_rows(rows_ref, 4 * half, 4),
            weight_ref[...],
            (((1,), (1,)), ((), ())),
            preferred_element_type=f32,
        )
        out_ref[pl.ds(256 * half, 256), :] = part.astype(bf16)


def per_device(
    stream, norm_gain, head_weight, down_weight, gate_pre, up_pre, targets, token_weight
):
    vocab_local = head_weight.shape[0]
    t = lax.axis_index(TENSOR)
    gate_float = gate_pre.astype(f32)
    up_float = up_pre.astype(f32)
    sigmoid_gate = jax.nn.sigmoid(gate_float)
    hidden = (gate_float * sigmoid_gate * up_float).astype(bf16)
    columns = t * vocab_local + lax.iota(jnp.int32, vocab_local)
    matches = (targets[:, None] == columns[None, :]).astype(f32)
    own = t.astype(jnp.uint32) * 16
    first, stream_float, gain_row, gain_rows, hidden, matches, weight, own = (
        lax.optimization_barrier(
            (
                stream,
                stream.astype(f32),
                norm_gain[None],
                jnp.broadcast_to(norm_gain, stream.shape),
                hidden,
                matches,
                jnp.broadcast_to(token_weight[:, None], (32, 128)),
                own,
            )
        )
    )
    x_blocks = gather_tensor(first)
    part = on_core(
        logits_kernel,
        [((512, 640), bf16)],
        x_blocks.reshape(NEARS, FARS * 16, 768),
        gain_row,
        head_weight,
        flops=2 * 512 * 512 * 768,
    )[0]
    got = exchange(part.reshape(16, 32, 640), DP)
    logits, inv, stats = on_core(
        stats_kernel,
        [((32, 512), f32), ((32, 128), f32), ((32, 1, 128), f32)],
        got,
        matches,
    )
    stats = exchange(stats, TENSOR)
    sent = on_core(
        dlogits_kernel, [((16, 32, 1024), bf16)], stats, logits, inv, matches, weight, hidden
    )[0]
    got = exchange(sent, DP).reshape(512, 1024)
    piece = got[:, :512]
    inv_all = join3(got[:, 960:963])
    inner_all = join3(got[:, 963:966])
    inv_own = lax.dynamic_slice_in_dim(inv_all, own, 16)[:, None]
    inner_own = lax.dynamic_slice_in_dim(inner_all, own, 16)[:, None]
    mixed = piece.reshape(FARS, NEARS, 16, vocab_local).transpose(1, 0, 2, 3)
    unit_rows = stream_float * inv_own
    grown, pulled = inv_own * gain_rows, inv_own * inner_own * unit_rows
    mixed, unit_rows, grown, pulled = lax.optimization_barrier(
        (mixed.reshape(512, vocab_local), unit_rows, grown, pulled)
    )
    back_rows = jnp.dot(mixed, head_weight, preferred_element_type=f32)
    normed_back = scatter_tensor(back_rows)
    stream_grad = (normed_back * grown - pulled).astype(bf16)
    gathered = gather_and_sum(stream_grad, jnp.sum(normed_back * unit_rows, axis=0))
    hidden_part = on_core(
        hidden_back_kernel,
        [((512, 448), bf16)],
        gathered,
        down_weight,
        flops=2 * 512 * 448 * 768,
    )[0]
    gathered, inv_all, x_blocks = lax.optimization_barrier((gathered, inv_all, x_blocks))
    gain_grad = jnp.sum(gathered[:, 128:131].astype(f32), axis=(0, 1))
    stream_all = in_order(gathered[:, :128].reshape(NEARS, FARS, 16, 768))
    x_all = in_order(x_blocks).astype(f32)
    normed_all = (x_all * inv_all[:, None] * norm_gain).astype(bf16)
    weight_part = jnp.einsum("tv,td->vd", piece, normed_all, preferred_element_type=f32)
    down_grad = jnp.einsum("tf,td->fd", got[:, 512:960], stream_all, preferred_element_type=f32)
    hidden_back = jnp.sum(exchange(hidden_part.reshape(16, 32, 448), DP).astype(f32), axis=0)
    up_grad = (hidden_back * gate_float * sigmoid_gate).astype(bf16)
    gate_grad = (
        hidden_back * up_float * sigmoid_gate * (1.0 + gate_float * (1.0 - sigmoid_gate))
    ).astype(bf16)
    return (weight_part, down_grad, stream_grad, gain_grad, gate_grad, up_grad)


def solution(mesh):
    fine = Mesh(mesh.devices.reshape(8, 2, 2, 2, 4, 2), ("zf", "zn", "yl", "yh", "x", "c"))
    return jax.shard_map(
        per_device,
        mesh=fine,
        in_specs=(
            P(TENSOR, DP),
            P(DP),
            P(TENSOR, DP),
            P(TENSOR, DP),
            P(DP, TENSOR),
            P(DP, TENSOR),
            P(DP),
            P(DP),
        ),
        out_specs=(
            P(TENSOR, DP),
            P(TENSOR, DP),
            P(TENSOR, DP),
            P(DP),
            P(DP, TENSOR),
            P(DP, TENSOR),
        ),
        check_vma=False,
    )
```

time: 209 us -> 202 us (0.967)
  blocking collectives: 95.6 us -> 165 us
  waiting for transfers between devices: 52.6 us -> 6.85 us
  starting transfers between devices: 37.7 us -> 12.8 us
  local copies, waits for them, and re-layouts: 8.46 us -> 3.53 us
  Pallas kernels: 0 us -> 2.62 us
  other arithmetic: 7.27 us -> 4.95 us
    all_to_all x5 -> x9, blocking collectives: 95.6 us -> 165 us  [exchange(): return lax.all_to_all(blocks, axes, 0, 0, tiled=True)]
    all_to_all x5 -> x1, waiting for transfers between devices: 52.6 us -> 6.85 us  [exchange(): return lax.all_to_all(blocks, axes, 0, 0, tiled=True)]
    all_to_all x5 -> x1, starting transfers between devices: 37.7 us -> 12.8 us  [exchange(): return lax.all_to_all(blocks, axes, 0, 0, tiled=True)]
    pallas_call x0 -> x4, Pallas kernels: none -> 2.62 us  [on_core(): pl.pallas_call(kernel, out_shape=outs, in_specs=[whole] * len(args), out_...]
    broadcast_in_dim x0 -> x3, local copies, waits for them, and re-layouts: none -> 2.11 us  [the longest x1 0.72 us: per_device(): jnp.broadcast_to(token_weight[:, None], (32, 128))]
  transfers between devices with their start and end apart: 5 -> 1, of which waited for: 5 -> 1; matrix products, arithmetic and copies ran while one was open for 3% -> 2% of each run, Pallas kernels for 0% -> 0%
where the time goes in v3:
time: 202 us; the launch traced here: 201 us
  blocking collectives  165 us (82%)
  starting transfers between devices  12.8 us (6%)
  waiting for transfers between devices  6.85 us (3%)
  other arithmetic  4.95 us (2%)
  matrix products  3.96 us (2%)
  local copies, waits for them, and re-layouts  3.53 us (2%)
  Pallas kernels  2.62 us (1%)
    all_to_all x9, blocking collectives, exchange(): return lax.all_to_all(blocks, axes, 0, 0, tiled=True)  165 us
    all_to_all x1, starting transfers between devices, exchange(): return lax.all_to_all(blocks, axes, 0, 0, tiled=True)  12.8 us
    all_to_all x1, waiting for transfers between devices, exchange(): return lax.all_to_all(blocks, axes, 0, 0, tiled=True)  6.85 us
  transfers between devices with their start and end apart: 1, of which 1 were waited for; matrix products, arithmetic and copies ran while one was open for 2% of the time, Pallas kernels for 0%

profile of v3, /device:TPU:1, one launch (start us, length us, event | category | flops | bytes accessed | tf_op | source)
XLA Modules:
  0.0 201.0 jit_solution(3852285445604794195)
XLA Ops:
  0.7 0.7 broadcast_in_dim.14.gain_ref
  1.3 0.7 convert_element_type.71
  2.1 0.8 fusion.6.hidden_ref
  2.9 0.7 compare_convert_fusion.mark_ref
  3.6 0.7 broadcast_in_dim.16.weight_ref
  4.4 0.7 broadcast_in_dim.15
  5.0 0.8 broadcast_in_dim.17
  5.9 30.6 %all_to_all.50 = bf16[8,16,768]{2,1,0:T(8,128)(2,1)S(1)} all-to-all(bf16[8,16,768]{2,1,0:T(8,128)(2,1)S(1)} %broadcast_in_dim.17), channel_id=1, replica_groups=mesh['zf'=8,'zn'=2,'yl'=2,'yh'=2,'x'=4,'c'=2] {'zf'}, dimensions={0} | all-to-all | bytes 393216 | tf_op jit(solution)/shard_map/all_to_all | solution.py:32
  36.5 9.9 %all_to_all.51 = bf16[4,8,16,768]{3,2,1,0:T(8,128)(2,1)S(1)} all-to-all(bf16[4,8,16,768]{3,2,1,0:T(8,128)(2,1)S(1)} %broadcast_in_dim.18), channel_id=1, replica_groups=mesh['zf'=8,'zn'=2,'yl'=2,'yh'=2,'x'=4,'c'=2] {'zn','yl'}, dimensions={0} | all-to-all | bytes 1572864 | tf_op jit(solution)/shard_map/all_to_all | solution.py:32
  46.4 0.6 shard_map.127
  47.0 25.5 %all_to_all.52.got_ref = bf16[16,32,640]{2,1,0:T(8,128)(2,1)S(1)} all-to-all(bf16[16,32,640]{2,1,0:T(8,128)(2,1)S(1)} %bitcast.31), channel_id=1, replica_groups=mesh['zf'=8,'zn'=2,'yl'=2,'yh'=2,'x'=4,'c'=2] {'yh','x','c'}, dimensions={0} | all-to-all | bytes 1310720 | tf_op jit(solution)/shard_map/all_to_all | solution.py:32
  72.8 18.0 %all_to_all.53.stats_ref = f32[32,1,128]{2,1,0:T(1,128)S(1)} all-to-all(f32[32,1,128]{2,1,0:T(1,128)S(1)} %get-tuple-element.27), channel_id=1, replica_groups=mesh['zf'=8,'zn'=2,'yl'=2,'yh'=2,'x'=4,'c'=2] {'zf','zn','yl'}, dimensions={0} | all-to-all | bytes 32768 | tf_op jit(solution)/shard_map/all_to_all | solution.py:32
  91.2 21.6 %all_to_all.54 = bf16[16,32,1024]{2,1,0:T(8,128)(2,1)S(1)} all-to-all(bf16[16,32,1024]{2,1,0:T(8,128)(2,1)S(1)} %shard_map.129), channel_id=1, replica_groups=mesh['zf'=8,'zn'=2,'yl'=2,'yh'=2,'x'=4,'c'=2] {'yh','x','c'}, dimensions={0} | all-to-all | bytes 2097152 | tf_op jit(solution)/shard_map/all_to_all | solution.py:32
  114.3 12.3 %all_to_all.55 = bf16[4,8,16,768]{3,2,1,0:T(8,128)(2,1)S(1)} all-to-all(bf16[4,8,16,768]{3,2,1,0:T(8,128)(2,1)S(1)} %bitcast.39), channel_id=1, replica_groups=mesh['zf'=8,'zn'=2,'yl'=2,'yh'=2,'x'=4,'c'=2] {'zn','yl'}, dimensions={0} | all-to-all | bytes 1572864 | tf_op jit(solution)/shard_map/all_to_all | solution.py:32
  126.8 17.6 %all_to_all.56 = bf16[8,16,768]{2,1,0:T(8,128)(2,1)S(1)} all-to-all(bf16[8,16,768]{2,1,0:T(8,128)(2,1)S(1)} %reduce_sum.68), channel_id=1, replica_groups=mesh['zf'=8,'zn'=2,'yl'=2,'yh'=2,'x'=4,'c'=2] {'zf'}, dimensions={0} | all-to-all | bytes 393216 | tf_op jit(solution)/shard_map/all_to_all | solution.py:32
  144.6 19.5 %all_to_all.57 = bf16[8,16,896]{2,1,0:T(8,128)(2,1)S(1)} all-to-all(bf16[8,16,896]{2,1,0:T(8,128)(2,1)S(1)} %broadcast_in_dim.19), channel_id=1, replica_groups=mesh['zf'=8,'zn'=2,'yl'=2,'yh'=2,'x'=4,'c'=2] {'zf'}, dimensions={0} | all-to-all | bytes 458752 | tf_op jit(solution)/shard_map/all_to_all | solution.py:32
  164.3 10.4 %all_to_all.58.rows_ref = bf16[4,136,768]{2,1,0:T(8,128)(2,1)S(1)} all-to-all(bf16[4,136,768]{2,1,0:T(8,128)(2,1)S(1)} %broadcast_in_dim.20), channel_id=1, replica_groups=mesh['zf'=8,'zn'=2,'yl'=2,'yh'=2,'x'=4,'c'=2] {'zn','yl'}, dimensions={0} | all-to-all | bytes 1671168 | tf_op jit(solution)/shard_map/all_to_all | solution.py:32
  174.7 1.4 shard_map.130
  176.1 12.8 %all-to-all-start.9 = ((bf16[16,32,448]{2,1,0:T(8,128)(2,1)}), bf16[16,32,448]{2,1,0:T(8,128)(2,1)S(1)}, u32[]{:S(2)}, u32[]{:S(2)}) async-start(bf16[16,32,448]{2,1,0:T(8,128)(2,1)} %bitcast.15), calls=%async_computation.9 | async-start | bytes 1048576 | tf_op jit(solution)/shard_map/all_to_all | solution.py:32
  189.2 1.6 fusion.2
  191.0 0.6 convert_reduce_fusion.3
  191.6 1.8 fusion.23
  193.4 6.8 %all-to-all-done.9 = bf16[16,32,448]{2,1,0:T(8,128)(2,1)S(1)} async-done(((bf16[16,32,448]{2,1,0:T(8,128)(2,1)}), bf16[16,32,448]{2,1,0:T(8,128)(2,1)S(1)}, u32[]{:S(2)}, u32[]{:S(2)}) %all-to-all-start.9) | async-done | bytes 458784 | tf_op jit(solution)/shard_map/all_to_all | solution.py:32
  200.3 0.7 fusion.15
  (46 shorter events, 3.2 us)
Async XLA Ops:
  5.0 41.3 %copy-start = (bf16[512,768]{1,0:T(8,128)(2,1)S(1)}, bf16[512,768]{1,0:T(8,128)(2,1)}, u32[]{:S(2)}) copy-start(bf16[512,768]{1,0:T(8,128)(2,1)} %weight_ref.2) | copy-start | bytes 2359300
  144.5 30.2 %copy-start.4 = (bf16[16,768]{1,0:T(8,128)(2,1)}, bf16[16,768]{1,0:T(8,128)(2,1)S(1)}, u32[]{:S(2)}) copy-start(bf16[16,768]{1,0:T(8,128)(2,1)S(1)} %get-tuple-element.53) | copy-start | bytes 73732
  164.2 10.5 %copy-start.1 = (bf16[448,768]{1,0:T(8,128)(2,1)S(1)}, bf16[448,768]{1,0:T(8,128)(2,1)}, u32[]{:S(2)}) copy-start(bf16[448,768]{1,0:T(8,128)(2,1)} %weight_ref.3) | copy-start | bytes 2064388
  176.1 24.2 %all-to-all-start.9 = ((bf16[16,32,448]{2,1,0:T(8,128)(2,1)}), bf16[16,32,448]{2,1,0:T(8,128)(2,1)S(1)}, u32[]{:S(2)}, u32[]{:S(2)}) async-start(bf16[16,32,448]{2,1,0:T(8,128)(2,1)} %bitcast.15), calls=%async_computation.9 | async-start | bytes 1048576 | tf_op jit(solution)/shard_map/all_to_all | solution.py:32
  189.1 1.7 copy-start.5
  191.6 8.7 %copy-start.2 = (bf16[32,448]{1,0:T(8,128)(2,1)S(1)}, bf16[32,448]{1,0:T(8,128)(2,1)}, u32[]{:S(2)}) copy-start(bf16[32,448]{1,0:T(8,128)(2,1)} %param.13) | copy-start | bytes 86020
  191.6 8.7 %copy-start.3 = (bf16[32,448]{1,0:T(8,128)(2,1)S(1)}, bf16[32,448]{1,0:T(8,128)(2,1)}, u32[]{:S(2)}) copy-start(bf16[32,448]{1,0:T(8,128)(2,1)} %param.12) | copy-start | bytes 86020

commit v4 on v3

v4 whole, which is shorter than its diff:
```python
import jax
import jax.numpy as jnp
from jax import lax
from jax.experimental import pallas as pl
from jax.experimental.pallas import tpu as pltpu
from jax.sharding import Mesh, PartitionSpec as P

D = 12288
EPSILON = 1e-05
FAR, NEAR = ("zf",), ("zn", "yl")
TENSOR = FAR + NEAR
CHIPS = ("yh", "x")
DP = CHIPS + ("c",)
FARS, NEARS = 8, 4
f32, bf16 = jnp.float32, jnp.bfloat16


def on_core(kernel, outs, *args, flops=0):
    whole = pl.BlockSpec(memory_space=pltpu.VMEM)
    outs = [jax.ShapeDtypeStruct(s, d) for s, d in outs]
    moved = sum(a.size * a.dtype.itemsize for a in list(args) + outs)
    return pl.pallas_call(
        kernel,
        out_shape=outs,
        in_specs=[
            pl.BlockSpec(memory_space=pltpu.SMEM) if a.shape == (1,) else whole for a in args
        ],
        out_specs=[whole] * len(outs),
        compiler_params=pltpu.CompilerParams(vmem_limit_bytes=16 << 20),
        cost_estimate=pl.CostEstimate(flops=flops, bytes_accessed=moved, transcendentals=0),
    )(*args)


def exchange(blocks, axes):
    return lax.all_to_all(blocks, axes, 0, 0, tiled=True)


def spread(block, axes, n):
    return exchange(jnp.broadcast_to(block[None], (n,) + block.shape), axes)


def other_core(block):
    return lax.ppermute(block, "c", [(0, 1), (1, 0)])


def split3(v):
    hi = lax.reduce_precision(v, 8, 7)
    mid = lax.reduce_precision(v - hi, 8, 7)
    lo = lax.reduce_precision(v - hi - mid, 8, 7)
    return jnp.stack([hi, mid, lo], axis=-1).astype(bf16)


def near_gather(far):
    side = far[:, :12, 768:].astype(f32).reshape(FARS, 2, 768)
    rows = far[:, :, :768].reshape(FARS * 16, 768)
    extra = jnp.pad(split3(jnp.sum(side, axis=(0, 1))).T, ((0, 5), (0, 0)))
    return spread(jnp.concatenate([rows, extra], axis=0), NEAR, NEARS)


def token_rows(ref, first, count):
    return jnp.concatenate(
        [ref[n, f * 16 : f * 16 + 16] for f in range(first, first + count) for n in range(NEARS)]
    )


def columns_of(parts, width):
    lane = lax.broadcasted_iota(jnp.int32, (parts[0].shape[0], width), 1)
    out = jnp.zeros((parts[0].shape[0], width), f32)
    for k, part in enumerate(parts):
        out = jnp.where(lane == k, part, out)
    return out


def thirds(v):
    hi = v.astype(bf16).astype(f32)
    mid = (v - hi).astype(bf16).astype(f32)
    return [hi, mid, v - hi - mid]


def logits_kernel(x_ref, gain_ref, weight_ref, out_ref):
    gain = gain_ref[...].reshape(1, 768)
    for half in range(2):
        x = token_rows(x_ref, 4 * half, 4).astype(f32)
        scaled = (x * gain).astype(bf16)
        part = lax.dot_general(
            scaled, weight_ref[...], (((1,), (1,)), ((), ())), preferred_element_type=f32
        )
        rows = pl.ds(256 * half, 256)
        out_ref[rows, :512] = part.astype(bf16)
        squares = jnp.sum(x * x, axis=1, keepdims=True)
        out_ref[rows, 512:] = columns_of(thirds(squares), 128).astype(bf16)


def row_of(columns):
    lane = lax.broadcasted_iota(jnp.int32, (32, 128), 1)
    token = lax.broadcasted_iota(jnp.int32, (32, 128), 0)
    spreaded = jnp.zeros((32, 128), f32)
    for k, column in enumerate(columns):
        spreaded = jnp.where(lane == token + 32 * k, column, spreaded)
    return jnp.sum(spreaded, axis=0, keepdims=True)


def column_of(row):
    lane = lax.broadcasted_iota(jnp.int32, (32, 128), 1)
    token = lax.broadcasted_iota(jnp.int32, (32, 128), 0)
    return jnp.sum(jnp.where(lane == token, row, 0.0), axis=1, keepdims=True)


def column(ref):
    row = ref[...].astype(f32).reshape(1, 32)
    lane = lax.broadcasted_iota(jnp.int32, (32, 32), 1)
    token = lax.broadcasted_iota(jnp.int32, (32, 32), 0)
    return jnp.sum(jnp.where(lane == token, row, 0.0), axis=1, keepdims=True)


def stats_kernel(
    first_ref, got_ref, targets_ref, weight_ref, logits_ref, scale_ref, stats_ref, mark_ref
):
    at = column(targets_ref).astype(jnp.int32) - first_ref[0]
    mark = (lax.broadcasted_iota(jnp.int32, (32, 512), 1) == at).astype(f32)
    total = jnp.zeros((32, 640), f32)
    for k in range(16):
        total = total + got_ref[k].astype(f32)
    squares = jnp.sum(total[:, 512:], axis=1, keepdims=True)
    inv = lax.rsqrt(squares / D + EPSILON)
    logits = total[:, :512] * inv
    top = jnp.max(logits, axis=1, keepdims=True)
    e = jnp.exp(logits - top)
    row = row_of(
        [
            top,
            jnp.sum(e, axis=1, keepdims=True),
            jnp.sum(e * logits, axis=1, keepdims=True),
            jnp.sum(logits * mark, axis=1, keepdims=True),
        ]
    )
    logits_ref[...] = logits
    scale_ref[...] = columns_of([inv, column(weight_ref)], 128)
    mark_ref[...] = mark
    stats_ref[...] = jnp.broadcast_to(row[None], (32, 1, 128))


def dlogits_kernel(stats_ref, logits_ref, scale_ref, mark_ref, gate_ref, up_ref, out_ref):
    gate, up = gate_ref[...].astype(f32), up_ref[...].astype(f32)
    hidden = (gate * jax.nn.sigmoid(gate) * up).astype(bf16)
    stats = stats_ref[...].reshape(32, 128)
    lane = lax.broadcasted_iota(jnp.int32, (32, 128), 1)
    top = jnp.max(stats, axis=0, keepdims=True)
    scale = jnp.exp(jnp.where(lane < 32, stats - top, 0.0))
    sums = pltpu.roll(stats, 96, 1)
    means = pltpu.roll(stats, 64, 1)
    picked = pltpu.roll(stats, 32, 1)
    total = jnp.sum(sums * scale, axis=0, keepdims=True)
    mean = jnp.sum(means * scale, axis=0, keepdims=True) / total
    inner = mean - jnp.sum(picked, axis=0, keepdims=True)
    weight = scale_ref[:, 1:2]
    top, total, inner = column_of(top), column_of(total), column_of(inner) * weight / D
    probability = jnp.exp(logits_ref[...] - top) / total
    dlogits = ((probability - mark_ref[...]) * weight).astype(bf16)
    tail = columns_of(thirds(scale_ref[:, :1]) + thirds(inner), 64).astype(bf16)
    for k in range(8):
        out_ref[k, :, :512] = dlogits
        out_ref[k, :, 512:960] = hidden
        out_ref[k, :, 960:] = tail


def half_rows(core_ref, side, mine_ref, others_ref, lanes):
    here = core_ref[0] == side
    return jnp.concatenate(
        [
            jnp.where(here, mine_ref[f, y : y + 16, lanes], others_ref[f, y : y + 16, lanes])
            for y in (0, 16)
            for f in range(FARS)
        ]
    )


def back_kernel(core_ref, mine_ref, others_ref, weight_ref, out_ref):
    for side in range(2):
        rows = half_rows(core_ref, side, mine_ref, others_ref, slice(0, 512))
        part = jnp.dot(rows, weight_ref[...], preferred_element_type=f32)
        out_ref[2 * side] = part[:128].astype(bf16)
        out_ref[2 * side + 1] = part[128:].astype(bf16)


def weights_kernel(
    core_ref, mine_ref, others_ref, x_ref, gain_ref, rows_ref, head_ref, down_ref
):
    def add(ref, side, a, b):
        part = lax.dot_general(a, b, (((0,), (0,)), ((), ())), preferred_element_type=f32)
        ref[...] = part if side == 0 else ref[...] + part

    for side in range(2):
        got = half_rows(core_ref, side, mine_ref, others_ref, slice(0, 1024))
        tail = got[:, 896:].astype(f32)
        inv = tail[:, 64:65] + tail[:, 65:66] + tail[:, 66:67]
        x = x_ref[2 * side : 2 * side + 2].reshape(256, 768).astype(f32)
        normed = (x * inv * gain_ref[...].reshape(1, 768)).astype(bf16)
        add(head_ref, side, got[:, :512], normed)
        rows = rows_ref[2 * side : 2 * side + 2, :128].reshape(256, 768)
        add(down_ref, side, got[:, 512:960], rows)


def grad_kernel(
    core_ref, near_ref, far_ref, low_ref, got_ref, mine_ref, others_ref, x_ref, gain_ref,
    out_ref,
):
    rows = pl.ds(pl.multiple_of(low_ref[0] * 16, 16), 16)
    here = core_ref[0] == near_ref[0]
    tail = jnp.where(
        here, mine_ref[far_ref[0], rows, 896:], others_ref[far_ref[0], rows, 896:]
    ).astype(f32)
    inv = tail[:, 64:65] + tail[:, 65:66] + tail[:, 66:67]
    inner = tail[:, 67:68] + tail[:, 68:69] + tail[:, 69:70]
    normed_back = jnp.zeros((16, 768), f32)
    for k in range(FARS):
        normed_back = normed_back + got_ref[k].astype(f32)
    unit_rows = x_ref[...].astype(f32) * inv
    grad = (inv * (normed_back * gain_ref[...].reshape(1, 768) - unit_rows * inner)).astype(bf16)
    term = thirds(jnp.sum(normed_back * unit_rows, axis=0, keepdims=True))
    row = lax.broadcasted_iota(jnp.int32, (16, 128), 0)
    side = jnp.zeros((16, 128), f32)
    for k in range(12):
        piece = term[k // 6][:, k % 6 * 128 : k % 6 * 128 + 128]
        side = jnp.where(row == k, piece, side)
    for k in range(FARS):
        out_ref[k, :, :768] = grad
        out_ref[k, :, 768:] = side.astype(bf16)


def hidden_back_kernel(rows_ref, weight_ref, out_ref):
    for half in range(2):
        part = lax.dot_general(
            token_rows(rows_ref, 4 * half, 4),
            weight_ref[...],
            (((1,), (1,)), ((), ())),
            preferred_element_type=f32,
        )
        out_ref[pl.ds(256 * half, 256), :] = part.astype(bf16)


def per_device(
    stream, norm_gain, head_weight, down_weight, gate_pre, up_pre, targets, token_weight
):
    vocab_local = head_weight.shape[0]
    t = lax.axis_index(TENSOR)
    first = (t * vocab_local).astype(jnp.int32)[None]
    places = [lax.axis_index(a).astype(jnp.int32)[None] for a in ("c", "zn", "zf", "yl")]
    rows, first, places = lax.optimization_barrier((stream, first, places))
    core = places[0]
    far = spread(rows, FAR, FARS)
    x_blocks = spread(far, NEAR, NEARS)
    part = on_core(
        logits_kernel,
        [((512, 640), bf16)],
        x_blocks.reshape(NEARS, FARS * 16, 768),
        norm_gain,
        head_weight,
        flops=2 * 512 * 512 * 768,
    )[0]
    got = exchange(part.reshape(16, 32, 640), DP)
    logits, scale, stats, mark = on_core(
        stats_kernel,
        [((32, 512), f32), ((32, 128), f32), ((32, 1, 128), f32), ((32, 512), f32)],
        first,
        got,
        targets,
        token_weight,
    )
    stats = exchange(stats, TENSOR)
    sent = on_core(
        dlogits_kernel, [((8, 32, 1024), bf16)], stats, logits, scale, mark, gate_pre, up_pre
    )[0]
    mine = exchange(sent, CHIPS)
    others = other_core(mine)

    back = on_core(
        back_kernel,
        [((NEARS, FARS * 16, 768), bf16)],
        core,
        mine,
        others,
        head_weight,
        flops=2 * 512 * 512 * 768,
    )[0]
    near = jnp.sum(exchange(back, NEAR).astype(f32), axis=0).astype(bf16)
    got = exchange(near.reshape(FARS, 16, 768), FAR)
    sent = on_core(
        grad_kernel,
        [((FARS, 16, 896), bf16)],
        *places,
        got,
        mine,
        others,
        stream,
        norm_gain,
    )[0]
    gathered = near_gather(exchange(sent, FAR))
    hidden_part = on_core(
        hidden_back_kernel,
        [((512, 448), bf16)],
        gathered,
        down_weight,
        flops=2 * 512 * 448 * 768,
    )[0]
    gathered, sent, x_blocks, mine, others, hidden_part = lax.optimization_barrier(
        (gathered, sent, x_blocks, mine, others, hidden_part)
    )
    stream_grad = sent[0, :, :768]
    gain_grad = jnp.sum(gathered[:, 128:131].astype(f32), axis=(0, 1))
    head_grad, down_grad = on_core(
        weights_kernel,
        [((512, 768), f32), ((448, 768), f32)],
        core,
        mine,
        others,
        x_blocks.reshape(NEARS, FARS * 16, 768),
        norm_gain,
        gathered,
        flops=2 * 512 * 960 * 768,
    )
    hidden_back = jnp.sum(exchange(hidden_part.reshape(16, 32, 448), DP).astype(f32), axis=0)
    gate_float = gate_pre.astype(f32)
    up_float = up_pre.astype(f32)
    sigmoid_gate = jax.nn.sigmoid(gate_float)
    up_grad = (hidden_back * gate_float * sigmoid_gate).astype(bf16)
    gate_grad = (
        hidden_back * up_float * sigmoid_gate * (1.0 + gate_float * (1.0 - sigmoid_gate))
    ).astype(bf16)
    return (head_grad, down_grad, stream_grad, gain_grad, gate_grad, up_grad)


def solution(mesh):
    fine = Mesh(mesh.devices.reshape(8, 2, 2, 2, 4, 2), ("zf", "zn", "yl", "yh", "x", "c"))
    return jax.shard_map(
        per_device,
        mesh=fine,
        in_specs=(
            P(TENSOR, DP),
            P(DP),
            P(TENSOR, DP),
            P(TENSOR, DP),
            P(DP, TENSOR),
            P(DP, TENSOR),
            P(DP),
            P(DP),
        ),
        out_specs=(
            P(TENSOR, DP),
            P(TENSOR, DP),
            P(TENSOR, DP),
            P(DP),
            P(DP, TENSOR),
            P(DP, TENSOR),
        ),
        check_vma=False,
    )
```

time: 202 us -> 193 us (0.955)
  blocking collectives: 165 us -> 160 us
  matrix products: 3.96 us -> 0 us
  Pallas kernels: 2.62 us -> 6.06 us
  other arithmetic: 4.95 us -> 1.56 us
  waiting for transfers between devices: 6.85 us -> 9.08 us
    all_to_all x9, blocking collectives: 165 us -> 160 us  [exchange(): return lax.all_to_all(blocks, axes, 0, 0, tiled=True)]
    ppermute x0 -> x1, starting transfers between devices: none -> 4.88 us  [other_core(): return lax.ppermute(block, 'c', [(0, 1), (1, 0)])]
    dot_general x3 -> x0, matrix products: 3.96 us -> none  [the longest x1 1.76 us: per_device(): jnp.einsum('tv,td->vd', piece, normed_all, preferred_element_type=f32)]
    all_to_all x1, starting transfers between devices: 12.8 us -> 8.95 us  [exchange(): return lax.all_to_all(blocks, axes, 0, 0, tiled=True)]
    pallas_call x4 -> x7, Pallas kernels: 2.62 us -> 6.06 us  [on_core(): pl.pallas_call(kernel, out_shape=outs, in_specs=[pl.BlockSpec(memory_spac...]
    convert_element_type x7 -> x0, other arithmetic: 2.81 us -> none  [the longest x1 0.81 us: per_device(): hidden = (gate_float * sigmoid_gate * up_float).astype(bf16)]
    broadcast_in_dim x3 -> x0, local copies, waits for them, and re-layouts: 2.11 us -> none  [the longest x1 0.72 us: per_device(): jnp.broadcast_to(token_weight[:, None], (32, 128))]
  transfers between devices with their start and end apart: 1 -> 2, of which waited for: 1 -> 2; matrix products, arithmetic and copies ran while one was open for 2% -> 1% of each run, Pallas kernels for 0% -> 1%
where the time goes in v4:
time: 193 us
  blocking collectives  160 us (83%)
  starting transfers between devices  13.8 us (7%)
  waiting for transfers between devices  9.08 us (5%)
  Pallas kernels  6.06 us (3%)
    all_to_all x9, blocking collectives, exchange(): return lax.all_to_all(blocks, axes, 0, 0, tiled=True)  160 us
    all_to_all x1, starting transfers between devices, exchange(): return lax.all_to_all(blocks, axes, 0, 0, tiled=True)  8.95 us
    all_to_all x1, waiting for transfers between devices, exchange(): return lax.all_to_all(blocks, axes, 0, 0, tiled=True)  7.57 us
    pallas_call x7, Pallas kernels, on_core(): pl.pallas_call(kernel, out_shape=outs, in_specs=[pl.BlockSpec(memory_spac...  6.06 us
    ppermute x1, starting transfers between devices, other_core(): return lax.ppermute(block, 'c', [(0, 1), (1, 0)])  4.88 us
  transfers between devices with their start and end apart: 2, of which 2 were waited for; matrix products, arithmetic and copies ran while one was open for 1% of the time, Pallas kernels for 1%

profile of v4, /device:TPU:1, one launch (start us, length us, event | category | flops | bytes accessed | tf_op | source)
XLA Modules:
  0.0 192.6 jit_solution(15168460606176335313)
XLA Ops:
  0.7 0.8 broadcast_in_dim.38
  1.5 30.6 %all_to_all.50 = bf16[8,16,768]{2,1,0:T(8,128)(2,1)S(1)} all-to-all(bf16[8,16,768]{2,1,0:T(8,128)(2,1)S(1)} %broadcast_in_dim.38), channel_id=1, replica_groups=mesh['zf'=8,'zn'=2,'yl'=2,'yh'=2,'x'=4,'c'=2] {'zf'}, dimensions={0} | all-to-all | bytes 393216 | tf_op jit(solution)/shard_map/all_to_all | solution.py:35
  32.1 9.9 %all_to_all.51 = bf16[4,8,16,768]{3,2,1,0:T(8,128)(2,1)S(1)} all-to-all(bf16[4,8,16,768]{3,2,1,0:T(8,128)(2,1)S(1)} %broadcast_in_dim.39), channel_id=1, replica_groups=mesh['zf'=8,'zn'=2,'yl'=2,'yh'=2,'x'=4,'c'=2] {'zn','yl'}, dimensions={0} | all-to-all | bytes 1572864 | tf_op jit(solution)/shard_map/all_to_all | solution.py:35
  42.0 0.6 shard_map.127
  42.7 25.5 %all_to_all.52.got_ref = bf16[16,32,640]{2,1,0:T(8,128)(2,1)S(1)} all-to-all(bf16[16,32,640]{2,1,0:T(8,128)(2,1)S(1)} %bitcast.17), channel_id=1, replica_groups=mesh['zf'=8,'zn'=2,'yl'=2,'yh'=2,'x'=4,'c'=2] {'yh','x','c'}, dimensions={0} | all-to-all | bytes 1310720 | tf_op jit(solution)/shard_map/all_to_all | solution.py:35
  68.2 0.3 shard_map.128
  68.5 18.0 %all_to_all.53.stats_ref = f32[32,1,128]{2,1,0:T(1,128)S(1)} all-to-all(f32[32,1,128]{2,1,0:T(1,128)S(1)} %get-tuple-element.30), channel_id=1, replica_groups=mesh['zf'=8,'zn'=2,'yl'=2,'yh'=2,'x'=4,'c'=2] {'zf','zn','yl'}, dimensions={0} | all-to-all | bytes 32768 | tf_op jit(solution)/shard_map/all_to_all | solution.py:35
  86.5 0.3 shard_map.129
  86.8 12.1 %all_to_all.54.mine_ref = bf16[8,32,1024]{2,1,0:T(8,128)(2,1)S(1)} all-to-all(bf16[8,32,1024]{2,1,0:T(8,128)(2,1)S(1)} %shard_map.129), channel_id=1, replica_groups=mesh['zf'=8,'zn'=2,'yl'=2,'yh'=2,'x'=4,'c'=2] {'yh','x'}, dimensions={0} | all-to-all | bytes 1048576 | tf_op jit(solution)/shard_map/all_to_all | solution.py:35
  99.0 4.9 %collective-permute-start = (bf16[8,32,1024]{2,1,0:T(8,128)(2,1)S(1)}, bf16[8,32,1024]{2,1,0:T(8,128)(2,1)S(1)}, u32[]{:S(2)}, u32[]{:S(2)}) collective-permute-start(bf16[8,32,1024]{2,1,0:T(8,128)(2,1)S(1)} %all_to_all.54.mine_ref), channel_id=1, source_target_pairs={{0,1},{1,0},{2,3},{3,2},{4,5},{5,4},{6,7},{7,6},{8,9},{9,8},{10,11... | collective-permute-start | bytes 1572872 | tf_op jit(solution)/shard_map/ppermute | solution.py:43
  103.8 1.5 collective-permute-done.others_ref
  105.4 0.6 shard_map.130
  106.0 13.1 %all_to_all.55 = bf16[4,128,768]{2,1,0:T(8,128)(2,1)S(1)} all-to-all(bf16[4,128,768]{2,1,0:T(8,128)(2,1)S(1)} %shard_map.130), channel_id=1, replica_groups=mesh['zf'=8,'zn'=2,'yl'=2,'yh'=2,'x'=4,'c'=2] {'zn','yl'}, dimensions={0} | all-to-all | bytes 1572864 | tf_op jit(solution)/shard_map/all_to_all | solution.py:35
  119.2 18.7 %all_to_all.56.got_ref = bf16[8,16,768]{2,1,0:T(8,128)(2,1)S(1)} all-to-all(bf16[8,16,768]{2,1,0:T(8,128)(2,1)S(1)} %bitcast.18), channel_id=1, replica_groups=mesh['zf'=8,'zn'=2,'yl'=2,'yh'=2,'x'=4,'c'=2] {'zf'}, dimensions={0} | all-to-all | bytes 393216 | tf_op jit(solution)/shard_map/all_to_all | solution.py:35
  137.9 0.2 shard_map.131
  138.1 19.9 %all_to_all.57 = bf16[8,16,896]{2,1,0:T(8,128)(2,1)S(1)} all-to-all(bf16[8,16,896]{2,1,0:T(8,128)(2,1)S(1)} %shard_map.131), channel_id=1, replica_groups=mesh['zf'=8,'zn'=2,'yl'=2,'yh'=2,'x'=4,'c'=2] {'zf'}, dimensions={0} | all-to-all | bytes 458752 | tf_op jit(solution)/shard_map/all_to_all | solution.py:35
  158.3 11.8 %all_to_all.58.rows_ref = bf16[4,136,768]{2,1,0:T(8,128)(2,1)S(1)} all-to-all(bf16[4,136,768]{2,1,0:T(8,128)(2,1)S(1)} %broadcast_in_dim.40), channel_id=1, replica_groups=mesh['zf'=8,'zn'=2,'yl'=2,'yh'=2,'x'=4,'c'=2] {'zn','yl'}, dimensions={0} | all-to-all | bytes 1671168 | tf_op jit(solution)/shard_map/all_to_all | solution.py:35
  170.0 1.4 shard_map.132
  171.4 8.9 %all-to-all-start.9 = ((bf16[16,32,448]{2,1,0:T(8,128)(2,1)}), bf16[16,32,448]{2,1,0:T(8,128)(2,1)S(1)}, u32[]{:S(2)}, u32[]{:S(2)}) async-start(bf16[16,32,448]{2,1,0:T(8,128)(2,1)} %bitcast.12), calls=%async_computation.9 | async-start | bytes 1048576 | tf_op jit(solution)/shard_map/all_to_all | solution.py:35
  180.3 2.7 %shard_map.133 = (f32[512,768]{1,0:T(8,128)}, f32[448,768]{1,0:T(8,128)}) custom-call(s32[1]{0:T(128)} %bitcast.1.core_ref, bf16[8,32,1024]{2,1,0:T(8,128)(2,1)S(1)} %all_to_all.54.mine_ref, bf16[8,32,1024]{2,1,0:T(8,128)(2,1)S(1)} %collective-permute-done.others_ref, bf16[4,128,768]{2,1,0:T(8,128)(2,1)S(1)} %bitcast.16, f32[768]{0:T(1024)S(1)} %copy-done.5, ...), custom_call_target="tpu_custom_call" | custom-call | flops 754974720 | bytes 5622788 | tf_op jit(solution)/shard_map/pallas_call | solution.py:22
  183.0 0.6 convert_reduce_fusion.2
  183.6 0.6 slice_bitcast_fusion
  184.2 7.6 %all-to-all-done.9 = bf16[16,32,448]{2,1,0:T(8,128)(2,1)S(1)} async-done(((bf16[16,32,448]{2,1,0:T(8,128)(2,1)}), bf16[16,32,448]{2,1,0:T(8,128)(2,1)S(1)}, u32[]{:S(2)}, u32[]{:S(2)}) %all-to-all-start.9) | async-done | bytes 458784 | tf_op jit(solution)/shard_map/all_to_all | solution.py:35
  191.9 0.7 fusion.9
  (27 shorter events, 0.5 us)
Async XLA Ops:
  0.6 41.4 %copy-start = (bf16[512,768]{1,0:T(8,128)(2,1)S(1)}, bf16[512,768]{1,0:T(8,128)(2,1)}, u32[]{:S(2)}) copy-start(bf16[512,768]{1,0:T(8,128)(2,1)} %weight_ref.6) | copy-start | bytes 2359300
  0.7 41.4 %copy-start.5 = (f32[768]{0:T(1024)S(1)}, f32[768]{0:T(1024)}, u32[]{:S(2)}) copy-start(f32[768]{0:T(1024)} %gain_ref.5) | copy-start | bytes 9220
  42.0 26.1 %copy-start.6 = (s32[32]{0:T(128)S(1)}, s32[32]{0:T(128)}, u32[]{:S(2)}) copy-start(s32[32]{0:T(128)} %targets_ref.1) | copy-start | bytes 388
  42.0 26.1 %copy-start.7 = (f32[32]{0:T(128)S(1)}, f32[32]{0:T(128)}, u32[]{:S(2)}) copy-start(f32[32]{0:T(128)} %weight_ref.5) | copy-start | bytes 388
  42.0 44.4 %copy-start.2 = (bf16[32,448]{1,0:T(8,128)(2,1)S(1)}, bf16[32,448]{1,0:T(8,128)(2,1)}, u32[]{:S(2)}) copy-start(bf16[32,448]{1,0:T(8,128)(2,1)} %gate_ref.1) | copy-start | bytes 86020
  42.0 44.4 %copy-start.3 = (bf16[32,448]{1,0:T(8,128)(2,1)S(1)}, bf16[32,448]{1,0:T(8,128)(2,1)}, u32[]{:S(2)}) copy-start(bf16[32,448]{1,0:T(8,128)(2,1)} %up_ref.1) | copy-start | bytes 86020
  99.0 6.4 %collective-permute-start = (bf16[8,32,1024]{2,1,0:T(8,128)(2,1)S(1)}, bf16[8,32,1024]{2,1,0:T(8,128)(2,1)S(1)}, u32[]{:S(2)}, u32[]{:S(2)}) collective-permute-start(bf16[8,32,1024]{2,1,0:T(8,128)(2,1)S(1)} %all_to_all.54.mine_ref), channel_id=1, source_target_pairs={{0,1},{1,0},{2,3},{3,2},{4,5},{5,4},{6,7},{7,6},{8,9},{9,8},{10,11... | collective-permute-start | bytes 1572872 | tf_op jit(solution)/shard_map/ppermute | solution.py:43
  105.9 32.0 %copy-start.4 = (bf16[16,768]{1,0:T(8,128)(2,1)S(1)}, bf16[16,768]{1,0:T(8,128)(2,1)}, u32[]{:S(2)}) copy-start(bf16[16,768]{1,0:T(8,128)(2,1)} %x_ref.1) | copy-start | bytes 73732
  158.2 11.9 %copy-start.1 = (bf16[448,768]{1,0:T(8,128)(2,1)S(1)}, bf16[448,768]{1,0:T(8,128)(2,1)}, u32[]{:S(2)}) copy-start(bf16[448,768]{1,0:T(8,128)(2,1)} %weight_ref.7) | copy-start | bytes 2064388
  171.4 20.4 %all-to-all-start.9 = ((bf16[16,32,448]{2,1,0:T(8,128)(2,1)}), bf16[16,32,448]{2,1,0:T(8,128)(2,1)S(1)}, u32[]{:S(2)}, u32[]{:S(2)}) async-start(bf16[16,32,448]{2,1,0:T(8,128)(2,1)} %bitcast.12), calls=%async_computation.9 | async-start | bytes 1048576 | tf_op jit(solution)/shard_map/all_to_all | solution.py:35

commit v5 on v4

--- a/solution.py
+++ b/solution.py
@@ -41,20 +41,6 @@
 
 def other_core(block):
     return lax.ppermute(block, "c", [(0, 1), (1, 0)])
-
-
-def split3(v):
-    hi = lax.reduce_precision(v, 8, 7)
-    mid = lax.reduce_precision(v - hi, 8, 7)
-    lo = lax.reduce_precision(v - hi - mid, 8, 7)
-    return jnp.stack([hi, mid, lo], axis=-1).astype(bf16)
-
-
-def near_gather(far):
-    side = far[:, :12, 768:].astype(f32).reshape(FARS, 2, 768)
-    rows = far[:, :, :768].reshape(FARS * 16, 768)
-    extra = jnp.pad(split3(jnp.sum(side, axis=(0, 1))).T, ((0, 5), (0, 0)))
-    return spread(jnp.concatenate([rows, extra], axis=0), NEAR, NEARS)
 
 
 def token_rows(ref, first, count):
@@ -184,21 +170,27 @@
 
 
 def weights_kernel(
-    core_ref, mine_ref, others_ref, x_ref, gain_ref, rows_ref, head_ref, down_ref
+    core_ref, mine_ref, others_ref, x_ref, gain_ref, rows_ref, head_ref, down_ref, sum_ref
 ):
-    def add(ref, side, a, b):
-        part = lax.dot_general(a, b, (((0,), (0,)), ((), ())), preferred_element_type=f32)
+    def add(ref, side, part):
         ref[...] = part if side == 0 else ref[...] + part
 
+    def product(a, b):
+        return lax.dot_general(a, b, (((0,), (0,)), ((), ())), preferred_element_type=f32)
+
+    gain = gain_ref[...].reshape(1, 768)
     for side in range(2):
         got = half_rows(core_ref, side, mine_ref, others_ref, slice(0, 1024))
         tail = got[:, 896:].astype(f32)
         inv = tail[:, 64:65] + tail[:, 65:66] + tail[:, 66:67]
-        x = x_ref[2 * side : 2 * side + 2].reshape(256, 768).astype(f32)
-        normed = (x * inv * gain_ref[...].reshape(1, 768)).astype(bf16)
-        add(head_ref, side, got[:, :512], normed)
-        rows = rows_ref[2 * side : 2 * side + 2, :128].reshape(256, 768)
-        add(down_ref, side, got[:, 512:960], rows)
+        inner = tail[:, 67:68] + tail[:, 68:69] + tail[:, 69:70]
+        unit_rows = x_ref[2 * side : 2 * side + 2].reshape(256, 768).astype(f32) * inv
+        add(head_ref, side, product(got[:, :512], (unit_rows * gain).astype(bf16)))
+        rows = rows_ref[2 * side : 2 * side + 2].reshape(256, 768)
+        add(down_ref, side, product(got[:, 512:960], rows))
+        scaled = rows.astype(f32) * (1.0 / inv) + unit_rows * inner
+        add(sum_ref, side, jnp.sum(scaled * unit_rows, axis=0, keepdims=True))
+    sum_ref[...] = sum_ref[...] / gain
 
 
 def grad_kernel(
@@ -217,15 +209,8 @@
         normed_back = normed_back + got_ref[k].astype(f32)
     unit_rows = x_ref[...].astype(f32) * inv
     grad = (inv * (normed_back * gain_ref[...].reshape(1, 768) - unit_rows * inner)).astype(bf16)
-    term = thirds(jnp.sum(normed_back * unit_rows, axis=0, keepdims=True))
-    row = lax.broadcasted_iota(jnp.int32, (16, 128), 0)
-    side = jnp.zeros((16, 128), f32)
-    for k in range(12):
-        piece = term[k // 6][:, k % 6 * 128 : k % 6 * 128 + 128]
-        side = jnp.where(row == k, piece, side)
     for k in range(FARS):
-        out_ref[k, :, :768] = grad
-        out_ref[k, :, 768:] = side.astype(bf16)
+        out_ref[k] = grad
 
 
 def hidden_back_kernel(rows_ref, weight_ref, out_ref):
@@ -287,7 +272,7 @@
     got = exchange(near.reshape(FARS, 16, 768), FAR)
     sent = on_core(
         grad_kernel,
-        [((FARS, 16, 896), bf16)],
+        [((FARS, 16, 768), bf16)],
         *places,
         got,
         mine,
@@ -295,7 +280,7 @@
         stream,
         norm_gain,
     )[0]
-    gathered = near_gather(exchange(sent, FAR))
+    gathered = spread(exchange(sent, FAR).reshape(FARS * 16, 768), NEAR, NEARS)
     hidden_part = on_core(
         hidden_back_kernel,
         [((512, 448), bf16)],
@@ -306,11 +291,10 @@
     gathered, sent, x_blocks, mine, others, hidden_part = lax.optimization_barrier(
         (gathered, sent, x_blocks, mine, others, hidden_part)
     )
-    stream_grad = sent[0, :, :768]
-    gain_grad = jnp.sum(gathered[:, 128:131].astype(f32), axis=(0, 1))
-    head_grad, down_grad = on_core(
+    stream_grad = sent[0]
+    head_grad, down_grad, gain_grad = on_core(
         weights_kernel,
-        [((512, 768), f32), ((448, 768), f32)],
+        [((512, 768), f32), ((448, 768), f32), ((1, 768), f32)],
         core,
         mine,
         others,
@@ -327,7 +311,7 @@
     gate_grad = (
         hidden_back * up_float * sigmoid_gate * (1.0 + gate_float * (1.0 - sigmoid_gate))
     ).astype(bf16)
-    return (head_grad, down_grad, stream_grad, gain_grad, gate_grad, up_grad)
+    return (head_grad, down_grad, stream_grad, gain_grad[0], gate_grad, up_grad)
 
 
 def solution(mesh):

time: 193 us -> 191 us (0.990)
  blocking collectives: 160 us -> 158 us
  transfers between devices with their start and end apart: 2 -> 2, of which waited for: 2 -> 2; matrix products, arithmetic and copies ran while one was open for 1% -> 1% of each run, Pallas kernels for 1% -> 2%
where the time goes in v5:
time: 191 us
  blocking collectives  158 us (83%)
  starting transfers between devices  13.5 us (7%)
  waiting for transfers between devices  8.87 us (5%)
  Pallas kernels  6.31 us (3%)
    all_to_all x9, blocking collectives, exchange(): return lax.all_to_all(blocks, axes, 0, 0, tiled=True)  158 us
    all_to_all x1, starting transfers between devices, exchange(): return lax.all_to_all(blocks, axes, 0, 0, tiled=True)  8.57 us
    all_to_all x1, waiting for transfers between devices, exchange(): return lax.all_to_all(blocks, axes, 0, 0, tiled=True)  7.36 us
    pallas_call x7, Pallas kernels, on_core(): pl.pallas_call(kernel, out_shape=outs, in_specs=[pl.BlockSpec(memory_spac...  6.31 us
    ppermute x1, starting transfers between devices, other_core(): return lax.ppermute(block, 'c', [(0, 1), (1, 0)])  4.88 us
  transfers between devices with their start and end apart: 2, of which 2 were waited for; matrix products, arithmetic and copies ran while one was open for 1% of the time, Pallas kernels for 2%

profile of v5, /device:TPU:1, one launch (start us, length us, event | category | flops | bytes accessed | tf_op | source)
XLA Modules:
  0.0 190.6 jit_solution(1449440854479925328)
XLA Ops:
  0.7 0.8 broadcast_in_dim.39
  1.5 30.6 %all_to_all.50 = bf16[8,16,768]{2,1,0:T(8,128)(2,1)S(1)} all-to-all(bf16[8,16,768]{2,1,0:T(8,128)(2,1)S(1)} %broadcast_in_dim.39), channel_id=1, replica_groups=mesh['zf'=8,'zn'=2,'yl'=2,'yh'=2,'x'=4,'c'=2] {'zf'}, dimensions={0} | all-to-all | bytes 393216 | tf_op jit(solution)/shard_map/all_to_all | solution.py:35
  32.1 9.9 %all_to_all.51 = bf16[4,8,16,768]{3,2,1,0:T(8,128)(2,1)S(1)} all-to-all(bf16[4,8,16,768]{3,2,1,0:T(8,128)(2,1)S(1)} %broadcast_in_dim.40), channel_id=1, replica_groups=mesh['zf'=8,'zn'=2,'yl'=2,'yh'=2,'x'=4,'c'=2] {'zn','yl'}, dimensions={0} | all-to-all | bytes 1572864 | tf_op jit(solution)/shard_map/all_to_all | solution.py:35
  42.0 0.6 shard_map.127
  42.7 25.5 %all_to_all.52.got_ref = bf16[16,32,640]{2,1,0:T(8,128)(2,1)S(1)} all-to-all(bf16[16,32,640]{2,1,0:T(8,128)(2,1)S(1)} %bitcast.15), channel_id=1, replica_groups=mesh['zf'=8,'zn'=2,'yl'=2,'yh'=2,'x'=4,'c'=2] {'yh','x','c'}, dimensions={0} | all-to-all | bytes 1310720 | tf_op jit(solution)/shard_map/all_to_all | solution.py:35
  68.2 0.3 shard_map.128
  68.5 18.0 %all_to_all.53.stats_ref = f32[32,1,128]{2,1,0:T(1,128)S(1)} all-to-all(f32[32,1,128]{2,1,0:T(1,128)S(1)} %get-tuple-element.31), channel_id=1, replica_groups=mesh['zf'=8,'zn'=2,'yl'=2,'yh'=2,'x'=4,'c'=2] {'zf','zn','yl'}, dimensions={0} | all-to-all | bytes 32768 | tf_op jit(solution)/shard_map/all_to_all | solution.py:35
  86.5 0.3 shard_map.129
  86.8 12.1 %all_to_all.54.mine_ref = bf16[8,32,1024]{2,1,0:T(8,128)(2,1)S(1)} all-to-all(bf16[8,32,1024]{2,1,0:T(8,128)(2,1)S(1)} %shard_map.129), channel_id=1, replica_groups=mesh['zf'=8,'zn'=2,'yl'=2,'yh'=2,'x'=4,'c'=2] {'yh','x'}, dimensions={0} | all-to-all | bytes 1048576 | tf_op jit(solution)/shard_map/all_to_all | solution.py:35
  99.0 4.9 %collective-permute-start = (bf16[8,32,1024]{2,1,0:T(8,128)(2,1)S(1)}, bf16[8,32,1024]{2,1,0:T(8,128)(2,1)S(1)}, u32[]{:S(2)}, u32[]{:S(2)}) collective-permute-start(bf16[8,32,1024]{2,1,0:T(8,128)(2,1)S(1)} %all_to_all.54.mine_ref), channel_id=1, source_target_pairs={{0,1},{1,0},{2,3},{3,2},{4,5},{5,4},{6,7},{7,6},{8,9},{9,8},{10,11... | collective-permute-start | bytes 1572872 | tf_op jit(solution)/shard_map/ppermute | solution.py:43
  103.9 1.5 collective-permute-done.others_ref
  105.4 0.6 shard_map.130
  106.0 13.1 %all_to_all.55 = bf16[4,128,768]{2,1,0:T(8,128)(2,1)S(1)} all-to-all(bf16[4,128,768]{2,1,0:T(8,128)(2,1)S(1)} %shard_map.130), channel_id=1, replica_groups=mesh['zf'=8,'zn'=2,'yl'=2,'yh'=2,'x'=4,'c'=2] {'zn','yl'}, dimensions={0} | all-to-all | bytes 1572864 | tf_op jit(solution)/shard_map/all_to_all | solution.py:35
  119.2 18.7 %all_to_all.56.got_ref = bf16[8,16,768]{2,1,0:T(8,128)(2,1)S(1)} all-to-all(bf16[8,16,768]{2,1,0:T(8,128)(2,1)S(1)} %bitcast.16), channel_id=1, replica_groups=mesh['zf'=8,'zn'=2,'yl'=2,'yh'=2,'x'=4,'c'=2] {'zf'}, dimensions={0} | all-to-all | bytes 393216 | tf_op jit(solution)/shard_map/all_to_all | solution.py:35
  138.0 0.2 shard_map.131
  138.1 19.7 %all_to_all.57 = bf16[8,16,768]{2,1,0:T(8,128)(2,1)S(1)} all-to-all(bf16[8,16,768]{2,1,0:T(8,128)(2,1)S(1)} %shard_map.131), channel_id=1, replica_groups=mesh['zf'=8,'zn'=2,'yl'=2,'yh'=2,'x'=4,'c'=2] {'zf'}, dimensions={0} | all-to-all | bytes 393216 | tf_op jit(solution)/shard_map/all_to_all | solution.py:35
  157.9 10.5 %all_to_all.58.rows_ref = bf16[4,128,768]{2,1,0:T(8,128)(2,1)S(1)} all-to-all(bf16[4,128,768]{2,1,0:T(8,128)(2,1)S(1)} %broadcast_in_dim.42), channel_id=1, replica_groups=mesh['zf'=8,'zn'=2,'yl'=2,'yh'=2,'x'=4,'c'=2] {'zn','yl'}, dimensions={0} | all-to-all | bytes 1572864 | tf_op jit(solution)/shard_map/all_to_all | solution.py:35
  168.4 1.4 shard_map.132
  169.8 8.6 %all-to-all-start.9 = ((bf16[16,32,448]{2,1,0:T(8,128)(2,1)}), bf16[16,32,448]{2,1,0:T(8,128)(2,1)S(1)}, u32[]{:S(2)}, u32[]{:S(2)}) async-start(bf16[16,32,448]{2,1,0:T(8,128)(2,1)} %bitcast.11), calls=%async_computation.9 | async-start | bytes 1048576 | tf_op jit(solution)/shard_map/all_to_all | solution.py:35
  178.4 2.9 %shard_map.133 = (f32[512,768]{1,0:T(8,128)}, f32[448,768]{1,0:T(8,128)}, f32[1,768]{1,0:T(1,128)S(1)}) custom-call(s32[1]{0:T(128)} %bitcast.1.core_ref, bf16[8,32,1024]{2,1,0:T(8,128)(2,1)S(1)} %all_to_all.54.mine_ref, bf16[8,32,1024]{2,1,0:T(8,128)(2,1)S(1)} %collective-permute-done.others_ref, bf16[4,128,768]{2,1,0:T(8,128)(2,1)S(1)} %bitcast.14, ...), custom_call_target="tpu_custom_call" | custom-call | flops 754974720 | bytes 5576708 | tf_op jit(solution)/shard_map/pallas_call | solution.py:22
  181.3 0.6 reduce.1
  181.9 0.6 slice_bitcast_fusion
  182.5 7.4 %all-to-all-done.9 = bf16[16,32,448]{2,1,0:T(8,128)(2,1)S(1)} async-done(((bf16[16,32,448]{2,1,0:T(8,128)(2,1)}), bf16[16,32,448]{2,1,0:T(8,128)(2,1)S(1)}, u32[]{:S(2)}, u32[]{:S(2)}) %all-to-all-start.9) | async-done | bytes 458784 | tf_op jit(solution)/shard_map/all_to_all | solution.py:35
  189.9 0.7 fusion.7
  (20 shorter events, 0.4 us)
Async XLA Ops:
  0.6 41.4 %copy-start = (bf16[512,768]{1,0:T(8,128)(2,1)S(1)}, bf16[512,768]{1,0:T(8,128)(2,1)}, u32[]{:S(2)}) copy-start(bf16[512,768]{1,0:T(8,128)(2,1)} %weight_ref.6) | copy-start | bytes 2359300
  0.7 41.4 %copy-start.5 = (f32[768]{0:T(1024)S(1)}, f32[768]{0:T(1024)}, u32[]{:S(2)}) copy-start(f32[768]{0:T(1024)} %gain_ref.5) | copy-start | bytes 9220
  42.0 26.1 %copy-start.6 = (s32[32]{0:T(128)S(1)}, s32[32]{0:T(128)}, u32[]{:S(2)}) copy-start(s32[32]{0:T(128)} %targets_ref.1) | copy-start | bytes 388
  42.0 26.1 %copy-start.7 = (f32[32]{0:T(128)S(1)}, f32[32]{0:T(128)}, u32[]{:S(2)}) copy-start(f32[32]{0:T(128)} %weight_ref.5) | copy-start | bytes 388
  42.0 44.5 %copy-start.2 = (bf16[32,448]{1,0:T(8,128)(2,1)S(1)}, bf16[32,448]{1,0:T(8,128)(2,1)}, u32[]{:S(2)}) copy-start(bf16[32,448]{1,0:T(8,128)(2,1)} %gate_ref.1) | copy-start | bytes 86020
  42.0 44.5 %copy-start.3 = (bf16[32,448]{1,0:T(8,128)(2,1)S(1)}, bf16[32,448]{1,0:T(8,128)(2,1)}, u32[]{:S(2)}) copy-start(bf16[32,448]{1,0:T(8,128)(2,1)} %up_ref.1) | copy-start | bytes 86020
  99.0 6.4 %collective-permute-start = (bf16[8,32,1024]{2,1,0:T(8,128)(2,1)S(1)}, bf16[8,32,1024]{2,1,0:T(8,128)(2,1)S(1)}, u32[]{:S(2)}, u32[]{:S(2)}) collective-permute-start(bf16[8,32,1024]{2,1,0:T(8,128)(2,1)S(1)} %all_to_all.54.mine_ref), channel_id=1, source_target_pairs={{0,1},{1,0},{2,3},{3,2},{4,5},{5,4},{6,7},{7,6},{8,9},{9,8},{10,11... | collective-permute-start | bytes 1572872 | tf_op jit(solution)/shard_map/ppermute | solution.py:43
  106.0 32.0 %copy-start.4 = (bf16[16,768]{1,0:T(8,128)(2,1)S(1)}, bf16[16,768]{1,0:T(8,128)(2,1)}, u32[]{:S(2)}) copy-start(bf16[16,768]{1,0:T(8,128)(2,1)} %x_ref.1) | copy-start | bytes 73732
  138.1 30.3 %copy-start.1 = (bf16[448,768]{1,0:T(8,128)(2,1)S(1)}, bf16[448,768]{1,0:T(8,128)(2,1)}, u32[]{:S(2)}) copy-start(bf16[448,768]{1,0:T(8,128)(2,1)} %weight_ref.7) | copy-start | bytes 2064388
  169.8 20.1 %all-to-all-start.9 = ((bf16[16,32,448]{2,1,0:T(8,128)(2,1)}), bf16[16,32,448]{2,1,0:T(8,128)(2,1)S(1)}, u32[]{:S(2)}, u32[]{:S(2)}) async-start(bf16[16,32,448]{2,1,0:T(8,128)(2,1)} %bitcast.11), calls=%async_computation.9 | async-start | bytes 1048576 | tf_op jit(solution)/shard_map/all_to_all | solution.py:35

commit v6 on v5

--- a/solution.py
+++ b/solution.py
@@ -71,10 +71,14 @@
         part = lax.dot_general(
             scaled, weight_ref[...], (((1,), (1,)), ((), ())), preferred_element_type=f32
         )
-        rows = pl.ds(256 * half, 256)
-        out_ref[rows, :512] = part.astype(bf16)
+        part = part.astype(bf16)
         squares = jnp.sum(x * x, axis=1, keepdims=True)
-        out_ref[rows, 512:] = columns_of(thirds(squares), 128).astype(bf16)
+        for k in range(8):
+            to, rows = 8 * half + k, slice(32 * k, 32 * k + 32)
+            for j in range(4):
+                out_ref[to, 32 * j : 32 * j + 32, :] = part[rows, 128 * j : 128 * j + 128]
+            row = row_of(thirds(squares[rows]))
+            out_ref[to, 128:, :] = jnp.broadcast_to(row, (16, 128)).astype(bf16)
 
 
 def row_of(columns):
@@ -104,12 +108,15 @@
 ):
     at = column(targets_ref).astype(jnp.int32) - first_ref[0]
     mark = (lax.broadcasted_iota(jnp.int32, (32, 512), 1) == at).astype(f32)
-    total = jnp.zeros((32, 640), f32)
+    total = jnp.zeros((144, 128), f32)
     for k in range(16):
         total = total + got_ref[k].astype(f32)
-    squares = jnp.sum(total[:, 512:], axis=1, keepdims=True)
+    lane = lax.broadcasted_iota(jnp.int32, (32, 128), 1)
+    token = lax.broadcasted_iota(jnp.int32, (32, 128), 0)
+    held = (lax.rem(lane, 32) == token) & (lane < 96)
+    squares = jnp.sum(jnp.where(held, total[128:129], 0.0), axis=1, keepdims=True)
     inv = lax.rsqrt(squares / D + EPSILON)
-    logits = total[:, :512] * inv
+    logits = jnp.concatenate([total[32 * j : 32 * j + 32] for j in range(4)], axis=1) * inv
     top = jnp.max(logits, axis=1, keepdims=True)
     e = jnp.exp(logits - top)
     row = row_of(
@@ -213,15 +220,36 @@
         out_ref[k] = grad
 
 
-def hidden_back_kernel(rows_ref, weight_ref, out_ref):
+def hidden_back_kernel(rows_ref, weight_ref, out_ref, held, sems):
+    copies = []
     for half in range(2):
+        rows = pl.ds(256 * half, 256)
         part = lax.dot_general(
             token_rows(rows_ref, 4 * half, 4),
             weight_ref[...],
             (((1,), (1,)), ((), ())),
             preferred_element_type=f32,
         )
-        out_ref[pl.ds(256 * half, 256), :] = part.astype(bf16)
+        held[rows, :] = part.astype(bf16)
+        copies.append(pltpu.make_async_copy(held.at[rows], out_ref.at[rows], sems.at[half]))
+        copies[-1].start()
+    for copy in copies:
+        copy.wait()
+
+
+def hidden_back(rows, weight):
+    shape, whole = (512, 448), pl.BlockSpec(memory_space=pltpu.VMEM)
+    return pl.pallas_call(
+        hidden_back_kernel,
+        out_shape=jax.ShapeDtypeStruct(shape, bf16),
+        in_specs=[whole, whole],
+        out_specs=pl.BlockSpec(memory_space=pl.ANY),
+        scratch_shapes=[pltpu.VMEM(shape, bf16), pltpu.SemaphoreType.DMA((2,))],
+        compiler_params=pltpu.CompilerParams(vmem_limit_bytes=16 << 20),
+        cost_estimate=pl.CostEstimate(
+            flops=2 * 512 * 448 * 768, bytes_accessed=2 << 20, transcendentals=0
+        ),
+    )(rows, weight)
 
 
 def per_device(
@@ -237,13 +265,13 @@
     x_blocks = spread(far, NEAR, NEARS)
     part = on_core(
         logits_kernel,
-        [((512, 640), bf16)],
+        [((16, 144, 128), bf16)],
         x_blocks.reshape(NEARS, FARS * 16, 768),
         norm_gain,
         head_weight,
         flops=2 * 512 * 512 * 768,
     )[0]
-    got = exchange(part.reshape(16, 32, 640), DP)
+    got = exchange(part, DP)
     logits, scale, stats, mark = on_core(
         stats_kernel,
         [((32, 512), f32), ((32, 128), f32), ((32, 1, 128), f32), ((32, 512), f32)],
@@ -281,13 +309,7 @@
         norm_gain,
     )[0]
     gathered = spread(exchange(sent, FAR).reshape(FARS * 16, 768), NEAR, NEARS)
-    hidden_part = on_core(
-        hidden_back_kernel,
-        [((512, 448), bf16)],
-        gathered,
-        down_weight,
-        flops=2 * 512 * 448 * 768,
-    )[0]
+    hidden_part = hidden_back(gathered, down_weight)
     gathered, sent, x_blocks, mine, others, hidden_part = lax.optimization_barrier(
         (gathered, sent, x_blocks, mine, others, hidden_part)
     )
@@ -303,13 +325,13 @@
         gathered,
         flops=2 * 512 * 960 * 768,
     )
-    hidden_back = jnp.sum(exchange(hidden_part.reshape(16, 32, 448), DP).astype(f32), axis=0)
+    hidden_grad = jnp.sum(exchange(hidden_part.reshape(16, 32, 448), DP).astype(f32), axis=0)
     gate_float = gate_pre.astype(f32)
     up_float = up_pre.astype(f32)
     sigmoid_gate = jax.nn.sigmoid(gate_float)
-    up_grad = (hidden_back * gate_float * sigmoid_gate).astype(bf16)
+    up_grad = (hidden_grad * gate_float * sigmoid_gate).astype(bf16)
     gate_grad = (
-        hidden_back * up_float * sigmoid_gate * (1.0 + gate_float * (1.0 - sigmoid_gate))
+        hidden_grad * up_float * sigmoid_gate * (1.0 + gate_float * (1.0 - sigmoid_gate))
     ).astype(bf16)
     return (head_grad, down_grad, stream_grad, gain_grad[0], gate_grad, up_grad)
 

time: 191 us -> 191 us (level)
    pallas_call x7 -> x6, Pallas kernels: 6.31 us -> 4.93 us  [on_core(): pl.pallas_call(kernel, out_shape=outs, in_specs=[pl.BlockSpec(memory_spac...]
where the time goes in v6:
time: 191 us; the launch traced here: 190 us
  blocking collectives  157 us (82%)
  starting transfers between devices  13.6 us (7%)
  waiting for transfers between devices  8.87 us (5%)
  Pallas kernels  6.23 us (3%)
    all_to_all x9, blocking collectives, exchange(): return lax.all_to_all(blocks, axes, 0, 0, tiled=True)  157 us
    all_to_all x1, starting transfers between devices, exchange(): return lax.all_to_all(blocks, axes, 0, 0, tiled=True)  8.58 us
    all_to_all x1, waiting for transfers between devices, exchange(): return lax.all_to_all(blocks, axes, 0, 0, tiled=True)  7.36 us
    ppermute x1, starting transfers between devices, other_core(): return lax.ppermute(block, 'c', [(0, 1), (1, 0)])  5.06 us
    pallas_call x6, Pallas kernels, on_core(): pl.pallas_call(kernel, out_shape=outs, in_specs=[pl.BlockSpec(memory_spac...  4.93 us
  transfers between devices with their start and end apart: 2, of which 2 were waited for; matrix products, arithmetic and copies ran while one was open for 1% of the time, Pallas kernels for 2%

profile of v6, /device:TPU:1, one launch (start us, length us, event | category | flops | bytes accessed | tf_op | source)
XLA Modules:
  0.0 190.0 jit_solution(8150437045787063601)
XLA Ops:
  0.7 0.8 broadcast_in_dim.39
  1.5 30.6 %all_to_all.50 = bf16[8,16,768]{2,1,0:T(8,128)(2,1)S(1)} all-to-all(bf16[8,16,768]{2,1,0:T(8,128)(2,1)S(1)} %broadcast_in_dim.39), channel_id=1, replica_groups=mesh['zf'=8,'zn'=2,'yl'=2,'yh'=2,'x'=4,'c'=2] {'zf'}, dimensions={0} | all-to-all | bytes 393216 | tf_op jit(solution)/shard_map/all_to_all | solution.py:35
  32.1 9.9 %all_to_all.51 = bf16[4,8,16,768]{3,2,1,0:T(8,128)(2,1)S(1)} all-to-all(bf16[4,8,16,768]{3,2,1,0:T(8,128)(2,1)S(1)} %broadcast_in_dim.40), channel_id=1, replica_groups=mesh['zf'=8,'zn'=2,'yl'=2,'yh'=2,'x'=4,'c'=2] {'zn','yl'}, dimensions={0} | all-to-all | bytes 1572864 | tf_op jit(solution)/shard_map/all_to_all | solution.py:35
  42.0 0.6 shard_map.127
  42.7 25.0 %all_to_all.52.got_ref = bf16[16,144,128]{2,1,0:T(8,128)(2,1)S(1)} all-to-all(bf16[16,144,128]{2,1,0:T(8,128)(2,1)S(1)} %shard_map.127), channel_id=1, replica_groups=mesh['zf'=8,'zn'=2,'yl'=2,'yh'=2,'x'=4,'c'=2] {'yh','x','c'}, dimensions={0} | all-to-all | bytes 1179648 | tf_op jit(solution)/shard_map/all_to_all | solution.py:35
  67.7 0.3 shard_map.128
  68.0 18.0 %all_to_all.53.stats_ref = f32[32,1,128]{2,1,0:T(1,128)S(1)} all-to-all(f32[32,1,128]{2,1,0:T(1,128)S(1)} %get-tuple-element.31), channel_id=1, replica_groups=mesh['zf'=8,'zn'=2,'yl'=2,'yh'=2,'x'=4,'c'=2] {'zf','zn','yl'}, dimensions={0} | all-to-all | bytes 32768 | tf_op jit(solution)/shard_map/all_to_all | solution.py:35
  86.0 0.3 shard_map.129
  86.4 11.8 %all_to_all.54.mine_ref = bf16[8,32,1024]{2,1,0:T(8,128)(2,1)S(1)} all-to-all(bf16[8,32,1024]{2,1,0:T(8,128)(2,1)S(1)} %shard_map.129), channel_id=1, replica_groups=mesh['zf'=8,'zn'=2,'yl'=2,'yh'=2,'x'=4,'c'=2] {'yh','x'}, dimensions={0} | all-to-all | bytes 1048576 | tf_op jit(solution)/shard_map/all_to_all | solution.py:35
  98.2 5.1 %collective-permute-start = (bf16[8,32,1024]{2,1,0:T(8,128)(2,1)S(1)}, bf16[8,32,1024]{2,1,0:T(8,128)(2,1)S(1)}, u32[]{:S(2)}, u32[]{:S(2)}) collective-permute-start(bf16[8,32,1024]{2,1,0:T(8,128)(2,1)S(1)} %all_to_all.54.mine_ref), channel_id=1, source_target_pairs={{0,1},{1,0},{2,3},{3,2},{4,5},{5,4},{6,7},{7,6},{8,9},{9,8},{10,11... | collective-permute-start | bytes 1572872 | tf_op jit(solution)/shard_map/ppermute | solution.py:43
  103.3 1.5 collective-permute-done.others_ref
  104.8 0.6 shard_map.130
  105.4 13.1 %all_to_all.55 = bf16[4,128,768]{2,1,0:T(8,128)(2,1)S(1)} all-to-all(bf16[4,128,768]{2,1,0:T(8,128)(2,1)S(1)} %shard_map.130), channel_id=1, replica_groups=mesh['zf'=8,'zn'=2,'yl'=2,'yh'=2,'x'=4,'c'=2] {'zn','yl'}, dimensions={0} | all-to-all | bytes 1572864 | tf_op jit(solution)/shard_map/all_to_all | solution.py:35
  118.7 18.7 %all_to_all.56.got_ref = bf16[8,16,768]{2,1,0:T(8,128)(2,1)S(1)} all-to-all(bf16[8,16,768]{2,1,0:T(8,128)(2,1)S(1)} %bitcast.14), channel_id=1, replica_groups=mesh['zf'=8,'zn'=2,'yl'=2,'yh'=2,'x'=4,'c'=2] {'zf'}, dimensions={0} | all-to-all | bytes 393216 | tf_op jit(solution)/shard_map/all_to_all | solution.py:35
  137.4 0.2 shard_map.131
  137.5 19.7 %all_to_all.57 = bf16[8,16,768]{2,1,0:T(8,128)(2,1)S(1)} all-to-all(bf16[8,16,768]{2,1,0:T(8,128)(2,1)S(1)} %shard_map.131), channel_id=1, replica_groups=mesh['zf'=8,'zn'=2,'yl'=2,'yh'=2,'x'=4,'c'=2] {'zf'}, dimensions={0} | all-to-all | bytes 393216 | tf_op jit(solution)/shard_map/all_to_all | solution.py:35
  157.3 10.5 %all_to_all.58.rows_ref = bf16[4,128,768]{2,1,0:T(8,128)(2,1)S(1)} all-to-all(bf16[4,128,768]{2,1,0:T(8,128)(2,1)S(1)} %broadcast_in_dim.42), channel_id=1, replica_groups=mesh['zf'=8,'zn'=2,'yl'=2,'yh'=2,'x'=4,'c'=2] {'zn','yl'}, dimensions={0} | all-to-all | bytes 1572864 | tf_op jit(solution)/shard_map/all_to_all | solution.py:35
  167.8 1.3 shard_map.132
  169.1 8.6 %all-to-all-start.9 = ((bf16[16,32,448]{2,1,0:T(8,128)(2,1)}), bf16[16,32,448]{2,1,0:T(8,128)(2,1)S(1)}, u32[]{:S(2)}, u32[]{:S(2)}) async-start(bf16[16,32,448]{2,1,0:T(8,128)(2,1)} %bitcast.10), calls=%async_computation.9 | async-start | bytes 1048576 | tf_op jit(solution)/shard_map/all_to_all | solution.py:35
  177.7 2.9 %shard_map.133 = (f32[512,768]{1,0:T(8,128)}, f32[448,768]{1,0:T(8,128)}, f32[1,768]{1,0:T(1,128)S(1)}) custom-call(s32[1]{0:T(128)} %bitcast.1.core_ref, bf16[8,32,1024]{2,1,0:T(8,128)(2,1)S(1)} %all_to_all.54.mine_ref, bf16[8,32,1024]{2,1,0:T(8,128)(2,1)S(1)} %collective-permute-done.others_ref, bf16[4,128,768]{2,1,0:T(8,128)(2,1)S(1)} %bitcast.13, ...), custom_call_target="tpu_custom_call" | custom-call | flops 754974720 | bytes 5576708 | tf_op jit(solution)/shard_map/pallas_call | solution.py:22
  180.6 0.6 reduce.1
  181.3 0.6 slice_bitcast_fusion
  181.9 7.4 %all-to-all-done.9 = bf16[16,32,448]{2,1,0:T(8,128)(2,1)S(1)} async-done(((bf16[16,32,448]{2,1,0:T(8,128)(2,1)}), bf16[16,32,448]{2,1,0:T(8,128)(2,1)S(1)}, u32[]{:S(2)}, u32[]{:S(2)}) %all-to-all-start.9) | async-done | bytes 458784 | tf_op jit(solution)/shard_map/all_to_all | solution.py:35
  189.3 0.7 fusion.7
  (20 shorter events, 0.4 us)
Async XLA Ops:
  0.6 41.4 %copy-start = (bf16[512,768]{1,0:T(8,128)(2,1)S(1)}, bf16[512,768]{1,0:T(8,128)(2,1)}, u32[]{:S(2)}) copy-start(bf16[512,768]{1,0:T(8,128)(2,1)} %weight_ref.6) | copy-start | bytes 2359300
  0.7 41.4 %copy-start.5 = (f32[768]{0:T(1024)S(1)}, f32[768]{0:T(1024)}, u32[]{:S(2)}) copy-start(f32[768]{0:T(1024)} %gain_ref.5) | copy-start | bytes 9220
  42.0 25.7 %copy-start.6 = (s32[32]{0:T(128)S(1)}, s32[32]{0:T(128)}, u32[]{:S(2)}) copy-start(s32[32]{0:T(128)} %targets_ref.1) | copy-start | bytes 388
  42.0 25.7 %copy-start.7 = (f32[32]{0:T(128)S(1)}, f32[32]{0:T(128)}, u32[]{:S(2)}) copy-start(f32[32]{0:T(128)} %weight_ref.5) | copy-start | bytes 388
  42.0 44.0 %copy-start.2 = (bf16[32,448]{1,0:T(8,128)(2,1)S(1)}, bf16[32,448]{1,0:T(8,128)(2,1)}, u32[]{:S(2)}) copy-start(bf16[32,448]{1,0:T(8,128)(2,1)} %gate_ref.1) | copy-start | bytes 86020
  42.0 44.0 %copy-start.3 = (bf16[32,448]{1,0:T(8,128)(2,1)S(1)}, bf16[32,448]{1,0:T(8,128)(2,1)}, u32[]{:S(2)}) copy-start(bf16[32,448]{1,0:T(8,128)(2,1)} %up_ref.1) | copy-start | bytes 86020
  98.2 6.6 %collective-permute-start = (bf16[8,32,1024]{2,1,0:T(8,128)(2,1)S(1)}, bf16[8,32,1024]{2,1,0:T(8,128)(2,1)S(1)}, u32[]{:S(2)}, u32[]{:S(2)}) collective-permute-start(bf16[8,32,1024]{2,1,0:T(8,128)(2,1)S(1)} %all_to_all.54.mine_ref), channel_id=1, source_target_pairs={{0,1},{1,0},{2,3},{3,2},{4,5},{5,4},{6,7},{7,6},{8,9},{9,8},{10,11... | collective-permute-start | bytes 1572872 | tf_op jit(solution)/shard_map/ppermute | solution.py:43
  105.4 32.0 %copy-start.4 = (bf16[16,768]{1,0:T(8,128)(2,1)S(1)}, bf16[16,768]{1,0:T(8,128)(2,1)}, u32[]{:S(2)}) copy-start(bf16[16,768]{1,0:T(8,128)(2,1)} %x_ref.1) | copy-start | bytes 73732
  137.5 30.3 %copy-start.1 = (bf16[448,768]{1,0:T(8,128)(2,1)S(1)}, bf16[448,768]{1,0:T(8,128)(2,1)}, u32[]{:S(2)}) copy-start(bf16[448,768]{1,0:T(8,128)(2,1)} %weight_ref.7) | copy-start | bytes 2064388
  169.1 20.1 %all-to-all-start.9 = ((bf16[16,32,448]{2,1,0:T(8,128)(2,1)}), bf16[16,32,448]{2,1,0:T(8,128)(2,1)S(1)}, u32[]{:S(2)}, u32[]{:S(2)}) async-start(bf16[16,32,448]{2,1,0:T(8,128)(2,1)} %bitcast.10), calls=%async_computation.9 | async-start | bytes 1048576 | tf_op jit(solution)/shard_map/all_to_all | solution.py:35

commit v7 on v6

--- a/solution.py
+++ b/solution.py
@@ -7,10 +7,11 @@
 
 D = 12288
 EPSILON = 1e-05
-FAR, NEAR = ("zf",), ("zn", "yl")
-TENSOR = FAR + NEAR
-CHIPS = ("yh", "x")
-DP = CHIPS + ("c",)
+TENSOR = ("z3", "z2", "z1", "z0", "yl")
+DP = ("yh", "x1", "x0", "c")
+FAR, NEAR = ("z1", "z3", "z2"), ("z0", "yl")
+CHIPS = ("x0", "yh", "x1")
+DEVICES = CHIPS + ("c",)
 FARS, NEARS = 8, 4
 f32, bf16 = jnp.float32, jnp.bfloat16
 
@@ -258,7 +259,7 @@
     vocab_local = head_weight.shape[0]
     t = lax.axis_index(TENSOR)
     first = (t * vocab_local).astype(jnp.int32)[None]
-    places = [lax.axis_index(a).astype(jnp.int32)[None] for a in ("c", "zn", "zf", "yl")]
+    places = [lax.axis_index(a).astype(jnp.int32)[None] for a in ("c", "z0", FAR, "yl")]
     rows, first, places = lax.optimization_barrier((stream, first, places))
     core = places[0]
     far = spread(rows, FAR, FARS)
@@ -271,7 +272,7 @@
         head_weight,
         flops=2 * 512 * 512 * 768,
     )[0]
-    got = exchange(part, DP)
+    got = exchange(part, DEVICES)
     logits, scale, stats, mark = on_core(
         stats_kernel,
         [((32, 512), f32), ((32, 128), f32), ((32, 1, 128), f32), ((32, 512), f32)],
@@ -280,7 +281,7 @@
         targets,
         token_weight,
     )
-    stats = exchange(stats, TENSOR)
+    stats = exchange(stats, TENSOR[::-1])
     sent = on_core(
         dlogits_kernel, [((8, 32, 1024), bf16)], stats, logits, scale, mark, gate_pre, up_pre
     )[0]
@@ -325,7 +326,7 @@
         gathered,
         flops=2 * 512 * 960 * 768,
     )
-    hidden_grad = jnp.sum(exchange(hidden_part.reshape(16, 32, 448), DP).astype(f32), axis=0)
+    hidden_grad = jnp.sum(exchange(hidden_part.reshape(16, 32, 448), DEVICES).astype(f32), axis=0)
     gate_float = gate_pre.astype(f32)
     up_float = up_pre.astype(f32)
     sigmoid_gate = jax.nn.sigmoid(gate_float)
@@ -337,7 +338,7 @@
 
 
 def solution(mesh):
-    fine = Mesh(mesh.devices.reshape(8, 2, 2, 2, 4, 2), ("zf", "zn", "yl", "yh", "x", "c"))
+    fine = Mesh(mesh.devices.reshape((2,) * 9), TENSOR + DP)
     return jax.shard_map(
         per_device,
         mesh=fine,

time: 191 us -> 189 us (0.990)
  no operation moved by 1% of the time
where the time goes in v7:
time: 189 us
  blocking collectives  156 us (83%)
  starting transfers between devices  14.1 us (7%)
  waiting for transfers between devices  9.13 us (5%)
  Pallas kernels  6.22 us (3%)
    all_to_all x9, blocking collectives, exchange(): return lax.all_to_all(blocks, axes, 0, 0, tiled=True)  156 us
    all_to_all x1, starting transfers between devices, exchange(): return lax.all_to_all(blocks, axes, 0, 0, tiled=True)  8.9 us
    all_to_all x1, waiting for transfers between devices, exchange(): return lax.all_to_all(blocks, axes, 0, 0, tiled=True)  7.61 us
    ppermute x1, starting transfers between devices, other_core(): return lax.ppermute(block, 'c', [(0, 1), (1, 0)])  5.2 us
    pallas_call x6, Pallas kernels, on_core(): pl.pallas_call(kernel, out_shape=outs, in_specs=[pl.BlockSpec(memory_spac...  4.91 us
  transfers between devices with their start and end apart: 2, of which 2 were waited for; matrix products, arithmetic and copies ran while one was open for 1% of the time, Pallas kernels for 2%

profile of v7, /device:TPU:1, one launch (start us, length us, event | category | flops | bytes accessed | tf_op | source)
XLA Modules:
  0.0 188.8 jit_solution(8801060010010581042)
XLA Ops:
  0.7 0.8 broadcast_in_dim.39
  1.5 27.8 %all_to_all.50 = bf16[8,16,768]{2,1,0:T(8,128)(2,1)S(1)} all-to-all(bf16[8,16,768]{2,1,0:T(8,128)(2,1)S(1)} %broadcast_in_dim.39), channel_id=1, replica_groups=mesh['z3'=2,'z2'=2,'z1'=2,'z0'=2,'yl'=2,'yh'=2,'x1'=2,'x0'=2,'c'=2] {'z1..., dimensions={0} | all-to-all | bytes 393216 | tf_op jit(solution)/shard_map/all_to_all | solution.py:36
  29.4 11.7 %all_to_all.51 = bf16[4,8,16,768]{3,2,1,0:T(8,128)(2,1)S(1)} all-to-all(bf16[4,8,16,768]{3,2,1,0:T(8,128)(2,1)S(1)} %broadcast_in_dim.40), channel_id=1, replica_groups=mesh['z3'=2,'z2'=2,'z1'=2,'z0'=2,'yl'=2,'yh'=2,'x1'=2,'x0'=2,'c'=2] {'z0..., dimensions={0} | all-to-all | bytes 1572864 | tf_op jit(solution)/shard_map/all_to_all | solution.py:36
  41.1 0.6 shard_map.127
  41.7 25.2 %all_to_all.52.got_ref = bf16[16,144,128]{2,1,0:T(8,128)(2,1)S(1)} all-to-all(bf16[16,144,128]{2,1,0:T(8,128)(2,1)S(1)} %shard_map.127), channel_id=1, replica_groups=mesh['z3'=2,'z2'=2,'z1'=2,'z0'=2,'yl'=2,'yh'=2,'x1'=2,'x0'=2,'c'=2] {'x0..., dimensions={0} | all-to-all | bytes 1179648 | tf_op jit(solution)/shard_map/all_to_all | solution.py:36
  66.9 0.3 shard_map.128
  67.2 18.8 %all_to_all.53.stats_ref = f32[32,1,128]{2,1,0:T(1,128)S(1)} all-to-all(f32[32,1,128]{2,1,0:T(1,128)S(1)} %get-tuple-element.31), channel_id=1, replica_groups=mesh['z3'=2,'z2'=2,'z1'=2,'z0'=2,'yl'=2,'yh'=2,'x1'=2,'x0'=2,'c'=2] {'yl..., dimensions={0} | all-to-all | bytes 32768 | tf_op jit(solution)/shard_map/all_to_all | solution.py:36
  86.0 0.3 shard_map.129
  86.3 11.6 %all_to_all.54.mine_ref = bf16[8,32,1024]{2,1,0:T(8,128)(2,1)S(1)} all-to-all(bf16[8,32,1024]{2,1,0:T(8,128)(2,1)S(1)} %shard_map.129), channel_id=1, replica_groups=mesh['z3'=2,'z2'=2,'z1'=2,'z0'=2,'yl'=2,'yh'=2,'x1'=2,'x0'=2,'c'=2] {'x0..., dimensions={0} | all-to-all | bytes 1048576 | tf_op jit(solution)/shard_map/all_to_all | solution.py:36
  98.0 5.2 %collective-permute-start = (bf16[8,32,1024]{2,1,0:T(8,128)(2,1)S(1)}, bf16[8,32,1024]{2,1,0:T(8,128)(2,1)S(1)}, u32[]{:S(2)}, u32[]{:S(2)}) collective-permute-start(bf16[8,32,1024]{2,1,0:T(8,128)(2,1)S(1)} %all_to_all.54.mine_ref), channel_id=1, source_target_pairs={{0,1},{1,0},{2,3},{3,2},{4,5},{5,4},{6,7},{7,6},{8,9},{9,8},{10,11... | collective-permute-start | bytes 1572872 | tf_op jit(solution)/shard_map/ppermute | solution.py:44
  103.2 1.5 collective-permute-done.others_ref
  104.7 0.6 shard_map.130
  105.3 13.1 %all_to_all.55 = bf16[4,128,768]{2,1,0:T(8,128)(2,1)S(1)} all-to-all(bf16[4,128,768]{2,1,0:T(8,128)(2,1)S(1)} %shard_map.130), channel_id=1, replica_groups=mesh['z3'=2,'z2'=2,'z1'=2,'z0'=2,'yl'=2,'yh'=2,'x1'=2,'x0'=2,'c'=2] {'z0..., dimensions={0} | all-to-all | bytes 1572864 | tf_op jit(solution)/shard_map/all_to_all | solution.py:36
  118.6 14.9 %all_to_all.56.got_ref = bf16[8,16,768]{2,1,0:T(8,128)(2,1)S(1)} all-to-all(bf16[8,16,768]{2,1,0:T(8,128)(2,1)S(1)} %bitcast.14), channel_id=1, replica_groups=mesh['z3'=2,'z2'=2,'z1'=2,'z0'=2,'yl'=2,'yh'=2,'x1'=2,'x0'=2,'c'=2] {'z1..., dimensions={0} | all-to-all | bytes 393216 | tf_op jit(solution)/shard_map/all_to_all | solution.py:36
  133.5 0.2 shard_map.131
  133.7 20.0 %all_to_all.57 = bf16[8,16,768]{2,1,0:T(8,128)(2,1)S(1)} all-to-all(bf16[8,16,768]{2,1,0:T(8,128)(2,1)S(1)} %shard_map.131), channel_id=1, replica_groups=mesh['z3'=2,'z2'=2,'z1'=2,'z0'=2,'yl'=2,'yh'=2,'x1'=2,'x0'=2,'c'=2] {'z1..., dimensions={0} | all-to-all | bytes 393216 | tf_op jit(solution)/shard_map/all_to_all | solution.py:36
  153.7 12.4 %all_to_all.58.rows_ref = bf16[4,128,768]{2,1,0:T(8,128)(2,1)S(1)} all-to-all(bf16[4,128,768]{2,1,0:T(8,128)(2,1)S(1)} %broadcast_in_dim.42), channel_id=1, replica_groups=mesh['z3'=2,'z2'=2,'z1'=2,'z0'=2,'yl'=2,'yh'=2,'x1'=2,'x0'=2,'c'=2] {'z0..., dimensions={0} | all-to-all | bytes 1572864 | tf_op jit(solution)/shard_map/all_to_all | solution.py:36
  166.1 1.3 shard_map.132
  167.4 8.9 %all-to-all-start.9 = ((bf16[16,32,448]{2,1,0:T(8,128)(2,1)}), bf16[16,32,448]{2,1,0:T(8,128)(2,1)S(1)}, u32[]{:S(2)}, u32[]{:S(2)}) async-start(bf16[16,32,448]{2,1,0:T(8,128)(2,1)} %bitcast.10), calls=%async_computation.9 | async-start | bytes 1048576 | tf_op jit(solution)/shard_map/all_to_all | solution.py:36
  176.3 2.9 %shard_map.133 = (f32[512,768]{1,0:T(8,128)}, f32[448,768]{1,0:T(8,128)}, f32[1,768]{1,0:T(1,128)S(1)}) custom-call(s32[1]{0:T(128)} %bitcast.1.core_ref, bf16[8,32,1024]{2,1,0:T(8,128)(2,1)S(1)} %all_to_all.54.mine_ref, bf16[8,32,1024]{2,1,0:T(8,128)(2,1)S(1)} %collective-permute-done.others_ref, bf16[4,128,768]{2,1,0:T(8,128)(2,1)S(1)} %bitcast.13, ...), custom_call_target="tpu_custom_call" | custom-call | flops 754974720 | bytes 5576708 | tf_op jit(solution)/shard_map/pallas_call | solution.py:23
  179.2 0.6 reduce.1
  179.8 0.6 slice_bitcast_fusion
  180.4 7.6 %all-to-all-done.9 = bf16[16,32,448]{2,1,0:T(8,128)(2,1)S(1)} async-done(((bf16[16,32,448]{2,1,0:T(8,128)(2,1)}), bf16[16,32,448]{2,1,0:T(8,128)(2,1)S(1)}, u32[]{:S(2)}, u32[]{:S(2)}) %all-to-all-start.9) | async-done | bytes 458784 | tf_op jit(solution)/shard_map/all_to_all | solution.py:36
  188.1 0.7 fusion.7
  (20 shorter events, 0.4 us)
Async XLA Ops:
  0.7 40.4 %copy-start = (bf16[512,768]{1,0:T(8,128)(2,1)S(1)}, bf16[512,768]{1,0:T(8,128)(2,1)}, u32[]{:S(2)}) copy-start(bf16[512,768]{1,0:T(8,128)(2,1)} %weight_ref.6) | copy-start | bytes 2359300
  0.7 40.4 %copy-start.5 = (f32[768]{0:T(1024)S(1)}, f32[768]{0:T(1024)}, u32[]{:S(2)}) copy-start(f32[768]{0:T(1024)} %gain_ref.5) | copy-start | bytes 9220
  41.1 25.9 %copy-start.6 = (s32[32]{0:T(128)S(1)}, s32[32]{0:T(128)}, u32[]{:S(2)}) copy-start(s32[32]{0:T(128)} %targets_ref.1) | copy-start | bytes 388
  41.1 25.9 %copy-start.7 = (f32[32]{0:T(128)S(1)}, f32[32]{0:T(128)}, u32[]{:S(2)}) copy-start(f32[32]{0:T(128)} %weight_ref.5) | copy-start | bytes 388
  41.1 44.9 %copy-start.2 = (bf16[32,448]{1,0:T(8,128)(2,1)S(1)}, bf16[32,448]{1,0:T(8,128)(2,1)}, u32[]{:S(2)}) copy-start(bf16[32,448]{1,0:T(8,128)(2,1)} %gate_ref.1) | copy-start | bytes 86020
  41.1 44.9 %copy-start.3 = (bf16[32,448]{1,0:T(8,128)(2,1)S(1)}, bf16[32,448]{1,0:T(8,128)(2,1)}, u32[]{:S(2)}) copy-start(bf16[32,448]{1,0:T(8,128)(2,1)} %up_ref.1) | copy-start | bytes 86020
  98.0 6.7 %collective-permute-start = (bf16[8,32,1024]{2,1,0:T(8,128)(2,1)S(1)}, bf16[8,32,1024]{2,1,0:T(8,128)(2,1)S(1)}, u32[]{:S(2)}, u32[]{:S(2)}) collective-permute-start(bf16[8,32,1024]{2,1,0:T(8,128)(2,1)S(1)} %all_to_all.54.mine_ref), channel_id=1, source_target_pairs={{0,1},{1,0},{2,3},{3,2},{4,5},{5,4},{6,7},{7,6},{8,9},{9,8},{10,11... | collective-permute-start | bytes 1572872 | tf_op jit(solution)/shard_map/ppermute | solution.py:44
  105.3 28.2 %copy-start.4 = (bf16[16,768]{1,0:T(8,128)(2,1)S(1)}, bf16[16,768]{1,0:T(8,128)(2,1)}, u32[]{:S(2)}) copy-start(bf16[16,768]{1,0:T(8,128)(2,1)} %x_ref.1) | copy-start | bytes 73732
  133.7 32.4 %copy-start.1 = (bf16[448,768]{1,0:T(8,128)(2,1)S(1)}, bf16[448,768]{1,0:T(8,128)(2,1)}, u32[]{:S(2)}) copy-start(bf16[448,768]{1,0:T(8,128)(2,1)} %weight_ref.7) | copy-start | bytes 2064388
  167.4 20.6 %all-to-all-start.9 = ((bf16[16,32,448]{2,1,0:T(8,128)(2,1)}), bf16[16,32,448]{2,1,0:T(8,128)(2,1)S(1)}, u32[]{:S(2)}, u32[]{:S(2)}) async-start(bf16[16,32,448]{2,1,0:T(8,128)(2,1)} %bitcast.10), calls=%async_computation.9 | async-start | bytes 1048576 | tf_op jit(solution)/shard_map/all_to_all | solution.py:36

commit v8 on v7

--- a/solution.py
+++ b/solution.py
@@ -281,7 +281,7 @@
         targets,
         token_weight,
     )
-    stats = exchange(stats, TENSOR[::-1])
+    stats = exchange(stats, FAR + NEAR)
     sent = on_core(
         dlogits_kernel, [((8, 32, 1024), bf16)], stats, logits, scale, mark, gate_pre, up_pre
     )[0]

time: 189 us -> 189 us (level)
  no operation moved by 1% of the time
where the time goes in v8:
time: 189 us
  blocking collectives  156 us (83%)
  starting transfers between devices  14.1 us (7%)
  waiting for transfers between devices  9.13 us (5%)
  Pallas kernels  6.22 us (3%)
    all_to_all x9, blocking collectives, exchange(): return lax.all_to_all(blocks, axes, 0, 0, tiled=True)  156 us
    all_to_all x1, starting transfers between devices, exchange(): return lax.all_to_all(blocks, axes, 0, 0, tiled=True)  8.9 us
    all_to_all x1, waiting for transfers between devices, exchange(): return lax.all_to_all(blocks, axes, 0, 0, tiled=True)  7.61 us
    ppermute x1, starting transfers between devices, other_core(): return lax.ppermute(block, 'c', [(0, 1), (1, 0)])  5.2 us
    pallas_call x6, Pallas kernels, on_core(): pl.pallas_call(kernel, out_shape=outs, in_specs=[pl.BlockSpec(memory_spac...  4.91 us
  transfers between devices with their start and end apart: 2, of which 2 were waited for; matrix products, arithmetic and copies ran while one was open for 1% of the time, Pallas kernels for 2%

profile of v8, /device:TPU:1, one launch (start us, length us, event | category | flops | bytes accessed | tf_op | source)
XLA Modules:
  0.0 188.8 jit_solution(8714708289869921117)
XLA Ops:
  0.7 0.8 broadcast_in_dim.39
  1.5 27.8 %all_to_all.50 = bf16[8,16,768]{2,1,0:T(8,128)(2,1)S(1)} all-to-all(bf16[8,16,768]{2,1,0:T(8,128)(2,1)S(1)} %broadcast_in_dim.39), channel_id=1, replica_groups=mesh['z3'=2,'z2'=2,'z1'=2,'z0'=2,'yl'=2,'yh'=2,'x1'=2,'x0'=2,'c'=2] {'z1..., dimensions={0} | all-to-all | bytes 393216 | tf_op jit(solution)/shard_map/all_to_all | solution.py:36
  29.4 11.7 %all_to_all.51 = bf16[4,8,16,768]{3,2,1,0:T(8,128)(2,1)S(1)} all-to-all(bf16[4,8,16,768]{3,2,1,0:T(8,128)(2,1)S(1)} %broadcast_in_dim.40), channel_id=1, replica_groups=mesh['z3'=2,'z2'=2,'z1'=2,'z0'=2,'yl'=2,'yh'=2,'x1'=2,'x0'=2,'c'=2] {'z0..., dimensions={0} | all-to-all | bytes 1572864 | tf_op jit(solution)/shard_map/all_to_all | solution.py:36
  41.1 0.6 shard_map.127
  41.7 25.2 %all_to_all.52.got_ref = bf16[16,144,128]{2,1,0:T(8,128)(2,1)S(1)} all-to-all(bf16[16,144,128]{2,1,0:T(8,128)(2,1)S(1)} %shard_map.127), channel_id=1, replica_groups=mesh['z3'=2,'z2'=2,'z1'=2,'z0'=2,'yl'=2,'yh'=2,'x1'=2,'x0'=2,'c'=2] {'x0..., dimensions={0} | all-to-all | bytes 1179648 | tf_op jit(solution)/shard_map/all_to_all | solution.py:36
  66.9 0.3 shard_map.128
  67.2 18.8 %all_to_all.53.stats_ref = f32[32,1,128]{2,1,0:T(1,128)S(1)} all-to-all(f32[32,1,128]{2,1,0:T(1,128)S(1)} %get-tuple-element.31), channel_id=1, replica_groups=mesh['z3'=2,'z2'=2,'z1'=2,'z0'=2,'yl'=2,'yh'=2,'x1'=2,'x0'=2,'c'=2] {'z1..., dimensions={0} | all-to-all | bytes 32768 | tf_op jit(solution)/shard_map/all_to_all | solution.py:36
  86.0 0.3 shard_map.129
  86.3 11.6 %all_to_all.54.mine_ref = bf16[8,32,1024]{2,1,0:T(8,128)(2,1)S(1)} all-to-all(bf16[8,32,1024]{2,1,0:T(8,128)(2,1)S(1)} %shard_map.129), channel_id=1, replica_groups=mesh['z3'=2,'z2'=2,'z1'=2,'z0'=2,'yl'=2,'yh'=2,'x1'=2,'x0'=2,'c'=2] {'x0..., dimensions={0} | all-to-all | bytes 1048576 | tf_op jit(solution)/shard_map/all_to_all | solution.py:36
  98.0 5.2 %collective-permute-start = (bf16[8,32,1024]{2,1,0:T(8,128)(2,1)S(1)}, bf16[8,32,1024]{2,1,0:T(8,128)(2,1)S(1)}, u32[]{:S(2)}, u32[]{:S(2)}) collective-permute-start(bf16[8,32,1024]{2,1,0:T(8,128)(2,1)S(1)} %all_to_all.54.mine_ref), channel_id=1, source_target_pairs={{0,1},{1,0},{2,3},{3,2},{4,5},{5,4},{6,7},{7,6},{8,9},{9,8},{10,11... | collective-permute-start | bytes 1572872 | tf_op jit(solution)/shard_map/ppermute | solution.py:44
  103.2 1.5 collective-permute-done.others_ref
  104.7 0.6 shard_map.130
  105.3 13.1 %all_to_all.55 = bf16[4,128,768]{2,1,0:T(8,128)(2,1)S(1)} all-to-all(bf16[4,128,768]{2,1,0:T(8,128)(2,1)S(1)} %shard_map.130), channel_id=1, replica_groups=mesh['z3'=2,'z2'=2,'z1'=2,'z0'=2,'yl'=2,'yh'=2,'x1'=2,'x0'=2,'c'=2] {'z0..., dimensions={0} | all-to-all | bytes 1572864 | tf_op jit(solution)/shard_map/all_to_all | solution.py:36
  118.6 14.9 %all_to_all.56.got_ref = bf16[8,16,768]{2,1,0:T(8,128)(2,1)S(1)} all-to-all(bf16[8,16,768]{2,1,0:T(8,128)(2,1)S(1)} %bitcast.14), channel_id=1, replica_groups=mesh['z3'=2,'z2'=2,'z1'=2,'z0'=2,'yl'=2,'yh'=2,'x1'=2,'x0'=2,'c'=2] {'z1..., dimensions={0} | all-to-all | bytes 393216 | tf_op jit(solution)/shard_map/all_to_all | solution.py:36
  133.5 0.2 shard_map.131
  133.7 20.0 %all_to_all.57 = bf16[8,16,768]{2,1,0:T(8,128)(2,1)S(1)} all-to-all(bf16[8,16,768]{2,1,0:T(8,128)(2,1)S(1)} %shard_map.131), channel_id=1, replica_groups=mesh['z3'=2,'z2'=2,'z1'=2,'z0'=2,'yl'=2,'yh'=2,'x1'=2,'x0'=2,'c'=2] {'z1..., dimensions={0} | all-to-all | bytes 393216 | tf_op jit(solution)/shard_map/all_to_all | solution.py:36
  153.8 12.3 %all_to_all.58.rows_ref = bf16[4,128,768]{2,1,0:T(8,128)(2,1)S(1)} all-to-all(bf16[4,128,768]{2,1,0:T(8,128)(2,1)S(1)} %broadcast_in_dim.42), channel_id=1, replica_groups=mesh['z3'=2,'z2'=2,'z1'=2,'z0'=2,'yl'=2,'yh'=2,'x1'=2,'x0'=2,'c'=2] {'z0..., dimensions={0} | all-to-all | bytes 1572864 | tf_op jit(solution)/shard_map/all_to_all | solution.py:36
  166.1 1.3 shard_map.132
  167.4 8.9 %all-to-all-start.9 = ((bf16[16,32,448]{2,1,0:T(8,128)(2,1)}), bf16[16,32,448]{2,1,0:T(8,128)(2,1)S(1)}, u32[]{:S(2)}, u32[]{:S(2)}) async-start(bf16[16,32,448]{2,1,0:T(8,128)(2,1)} %bitcast.10), calls=%async_computation.9 | async-start | bytes 1048576 | tf_op jit(solution)/shard_map/all_to_all | solution.py:36
  176.3 2.9 %shard_map.133 = (f32[512,768]{1,0:T(8,128)}, f32[448,768]{1,0:T(8,128)}, f32[1,768]{1,0:T(1,128)S(1)}) custom-call(s32[1]{0:T(128)} %bitcast.1.core_ref, bf16[8,32,1024]{2,1,0:T(8,128)(2,1)S(1)} %all_to_all.54.mine_ref, bf16[8,32,1024]{2,1,0:T(8,128)(2,1)S(1)} %collective-permute-done.others_ref, bf16[4,128,768]{2,1,0:T(8,128)(2,1)S(1)} %bitcast.13, ...), custom_call_target="tpu_custom_call" | custom-call | flops 754974720 | bytes 5576708 | tf_op jit(solution)/shard_map/pallas_call | solution.py:23
  179.2 0.6 reduce.1
  179.8 0.6 slice_bitcast_fusion
  180.4 7.6 %all-to-all-done.9 = bf16[16,32,448]{2,1,0:T(8,128)(2,1)S(1)} async-done(((bf16[16,32,448]{2,1,0:T(8,128)(2,1)}), bf16[16,32,448]{2,1,0:T(8,128)(2,1)S(1)}, u32[]{:S(2)}, u32[]{:S(2)}) %all-to-all-start.9) | async-done | bytes 458784 | tf_op jit(solution)/shard_map/all_to_all | solution.py:36
  188.1 0.7 fusion.7
  (20 shorter events, 0.4 us)
Async XLA Ops:
  0.7 40.4 %copy-start = (bf16[512,768]{1,0:T(8,128)(2,1)S(1)}, bf16[512,768]{1,0:T(8,128)(2,1)}, u32[]{:S(2)}) copy-start(bf16[512,768]{1,0:T(8,128)(2,1)} %weight_ref.6) | copy-start | bytes 2359300
  0.7 40.4 %copy-start.5 = (f32[768]{0:T(1024)S(1)}, f32[768]{0:T(1024)}, u32[]{:S(2)}) copy-start(f32[768]{0:T(1024)} %gain_ref.5) | copy-start | bytes 9220
  41.1 25.9 %copy-start.6 = (s32[32]{0:T(128)S(1)}, s32[32]{0:T(128)}, u32[]{:S(2)}) copy-start(s32[32]{0:T(128)} %targets_ref.1) | copy-start | bytes 388
  41.1 25.9 %copy-start.7 = (f32[32]{0:T(128)S(1)}, f32[32]{0:T(128)}, u32[]{:S(2)}) copy-start(f32[32]{0:T(128)} %weight_ref.5) | copy-start | bytes 388
  41.1 44.9 %copy-start.2 = (bf16[32,448]{1,0:T(8,128)(2,1)S(1)}, bf16[32,448]{1,0:T(8,128)(2,1)}, u32[]{:S(2)}) copy-start(bf16[32,448]{1,0:T(8,128)(2,1)} %gate_ref.1) | copy-start | bytes 86020
  41.1 44.9 %copy-start.3 = (bf16[32,448]{1,0:T(8,128)(2,1)S(1)}, bf16[32,448]{1,0:T(8,128)(2,1)}, u32[]{:S(2)}) copy-start(bf16[32,448]{1,0:T(8,128)(2,1)} %up_ref.1) | copy-start | bytes 86020
  98.0 6.7 %collective-permute-start = (bf16[8,32,1024]{2,1,0:T(8,128)(2,1)S(1)}, bf16[8,32,1024]{2,1,0:T(8,128)(2,1)S(1)}, u32[]{:S(2)}, u32[]{:S(2)}) collective-permute-start(bf16[8,32,1024]{2,1,0:T(8,128)(2,1)S(1)} %all_to_all.54.mine_ref), channel_id=1, source_target_pairs={{0,1},{1,0},{2,3},{3,2},{4,5},{5,4},{6,7},{7,6},{8,9},{9,8},{10,11... | collective-permute-start | bytes 1572872 | tf_op jit(solution)/shard_map/ppermute | solution.py:44
  105.3 28.2 %copy-start.4 = (bf16[16,768]{1,0:T(8,128)(2,1)S(1)}, bf16[16,768]{1,0:T(8,128)(2,1)}, u32[]{:S(2)}) copy-start(bf16[16,768]{1,0:T(8,128)(2,1)} %x_ref.1) | copy-start | bytes 73732
  133.7 32.4 %copy-start.1 = (bf16[448,768]{1,0:T(8,128)(2,1)S(1)}, bf16[448,768]{1,0:T(8,128)(2,1)}, u32[]{:S(2)}) copy-start(bf16[448,768]{1,0:T(8,128)(2,1)} %weight_ref.7) | copy-start | bytes 2064388
  167.4 20.6 %all-to-all-start.9 = ((bf16[16,32,448]{2,1,0:T(8,128)(2,1)}), bf16[16,32,448]{2,1,0:T(8,128)(2,1)S(1)}, u32[]{:S(2)}, u32[]{:S(2)}) async-start(bf16[16,32,448]{2,1,0:T(8,128)(2,1)} %bitcast.10), calls=%async_computation.9 | async-start | bytes 1048576 | tf_op jit(solution)/shard_map/all_to_all | solution.py:36

commit v9 on v8

--- a/solution.py
+++ b/solution.py
@@ -169,12 +169,27 @@
     )
 
 
-def back_kernel(core_ref, mine_ref, others_ref, weight_ref, out_ref):
-    for side in range(2):
-        rows = half_rows(core_ref, side, mine_ref, others_ref, slice(0, 512))
-        part = jnp.dot(rows, weight_ref[...], preferred_element_type=f32)
-        out_ref[2 * side] = part[:128].astype(bf16)
-        out_ref[2 * side + 1] = part[128:].astype(bf16)
+def back_kernel(core_ref, got_ref, weight_ref, *refs):
+    out_ref = refs[-1]
+    rows = [got_ref[f, y : y + 16, :512] for y in (0, 16) for f in range(FARS)]
+    part = jnp.dot(jnp.concatenate(rows), weight_ref[...], preferred_element_type=f32)
+    out_ref[2 * core_ref[0]] = part[:128].astype(bf16)
+    out_ref[2 * core_ref[0] + 1] = part[128:].astype(bf16)
+
+
+def back_half(core, got, weight, *into):
+    whole = pl.BlockSpec(memory_space=pltpu.VMEM)
+    return pl.pallas_call(
+        back_kernel,
+        out_shape=jax.ShapeDtypeStruct((NEARS, FARS * 16, 768), bf16),
+        in_specs=[pl.BlockSpec(memory_space=pltpu.SMEM)] + [whole] * (2 + len(into)),
+        out_specs=whole,
+        input_output_aliases={3: 0} if into else {},
+        compiler_params=pltpu.CompilerParams(vmem_limit_bytes=16 << 20),
+        cost_estimate=pl.CostEstimate(
+            flops=2 * 256 * 512 * 768, bytes_accessed=2 << 20, transcendentals=0
+        ),
+    )(core, got, weight, *into)
 
 
 def weights_kernel(
@@ -260,7 +275,7 @@
     t = lax.axis_index(TENSOR)
     first = (t * vocab_local).astype(jnp.int32)[None]
     places = [lax.axis_index(a).astype(jnp.int32)[None] for a in ("c", "z0", FAR, "yl")]
-    rows, first, places = lax.optimization_barrier((stream, first, places))
+    rows, first, places, twin = lax.optimization_barrier((stream, first, places, 1 - places[0]))
     core = places[0]
     far = spread(rows, FAR, FARS)
     x_blocks = spread(far, NEAR, NEARS)
@@ -288,15 +303,8 @@
     mine = exchange(sent, CHIPS)
     others = other_core(mine)
 
-    back = on_core(
-        back_kernel,
-        [((NEARS, FARS * 16, 768), bf16)],
-        core,
-        mine,
-        others,
-        head_weight,
-        flops=2 * 512 * 512 * 768,
-    )[0]
+    back = back_half(core, mine, head_weight)
+    back = back_half(twin, others, head_weight, back)
     near = jnp.sum(exchange(back, NEAR).astype(f32), axis=0).astype(bf16)
     got = exchange(near.reshape(FARS, 16, 768), FAR)
     sent = on_core(

time: 189 us -> 189 us (level)
    pallas_call x6 -> x5, Pallas kernels: 4.91 us -> 4.32 us  [on_core(): pl.pallas_call(kernel, out_shape=outs, in_specs=[pl.BlockSpec(memory_spac...]
where the time goes in v9:
time: 189 us
  blocking collectives  156 us (83%)
  starting transfers between devices  14.1 us (7%)
  waiting for transfers between devices  8.75 us (5%)
  Pallas kernels  6.38 us (3%)
    all_to_all x9, blocking collectives, exchange(): return lax.all_to_all(blocks, axes, 0, 0, tiled=True)  156 us
    all_to_all x1, starting transfers between devices, exchange(): return lax.all_to_all(blocks, axes, 0, 0, tiled=True)  8.89 us
    all_to_all x1, waiting for transfers between devices, exchange(): return lax.all_to_all(blocks, axes, 0, 0, tiled=True)  7.61 us
    ppermute x1, starting transfers between devices, other_core(): return lax.ppermute(block, 'c', [(0, 1), (1, 0)])  5.2 us
    pallas_call x5, Pallas kernels, on_core(): pl.pallas_call(kernel, out_shape=outs, in_specs=[pl.BlockSpec(memory_spac...  4.32 us
  transfers between devices with their start and end apart: 2, of which 2 were waited for; matrix products, arithmetic and copies ran while one was open for 1% of the time, Pallas kernels for 2%

profile of v9, /device:TPU:1, one launch (start us, length us, event | category | flops | bytes accessed | tf_op | source)
XLA Modules:
  0.0 188.6 jit_solution(986262692039277579)
XLA Ops:
  0.7 0.8 broadcast_in_dim.39
  1.5 27.8 %all_to_all.50 = bf16[8,16,768]{2,1,0:T(8,128)(2,1)S(1)} all-to-all(bf16[8,16,768]{2,1,0:T(8,128)(2,1)S(1)} %broadcast_in_dim.39), channel_id=1, replica_groups=mesh['z3'=2,'z2'=2,'z1'=2,'z0'=2,'yl'=2,'yh'=2,'x1'=2,'x0'=2,'c'=2] {'z1..., dimensions={0} | all-to-all | bytes 393216 | tf_op jit(solution)/shard_map/all_to_all | solution.py:36
  29.4 11.7 %all_to_all.51 = bf16[4,8,16,768]{3,2,1,0:T(8,128)(2,1)S(1)} all-to-all(bf16[4,8,16,768]{3,2,1,0:T(8,128)(2,1)S(1)} %broadcast_in_dim.40), channel_id=1, replica_groups=mesh['z3'=2,'z2'=2,'z1'=2,'z0'=2,'yl'=2,'yh'=2,'x1'=2,'x0'=2,'c'=2] {'z0..., dimensions={0} | all-to-all | bytes 1572864 | tf_op jit(solution)/shard_map/all_to_all | solution.py:36
  41.1 0.6 shard_map.127
  41.7 25.2 %all_to_all.52.got_ref = bf16[16,144,128]{2,1,0:T(8,128)(2,1)S(1)} all-to-all(bf16[16,144,128]{2,1,0:T(8,128)(2,1)S(1)} %shard_map.127), channel_id=1, replica_groups=mesh['z3'=2,'z2'=2,'z1'=2,'z0'=2,'yl'=2,'yh'=2,'x1'=2,'x0'=2,'c'=2] {'x0..., dimensions={0} | all-to-all | bytes 1179648 | tf_op jit(solution)/shard_map/all_to_all | solution.py:36
  66.9 0.3 shard_map.128
  67.2 18.8 %all_to_all.53.stats_ref = f32[32,1,128]{2,1,0:T(1,128)S(1)} all-to-all(f32[32,1,128]{2,1,0:T(1,128)S(1)} %get-tuple-element.33), channel_id=1, replica_groups=mesh['z3'=2,'z2'=2,'z1'=2,'z0'=2,'yl'=2,'yh'=2,'x1'=2,'x0'=2,'c'=2] {'z1..., dimensions={0} | all-to-all | bytes 32768 | tf_op jit(solution)/shard_map/all_to_all | solution.py:36
  86.0 0.3 shard_map.129
  86.3 11.6 %all_to_all.54.got_ref.mine_ref = bf16[8,32,1024]{2,1,0:T(8,128)(2,1)S(1)} all-to-all(bf16[8,32,1024]{2,1,0:T(8,128)(2,1)S(1)} %shard_map.129), channel_id=1, replica_groups=mesh['z3'=2,'z2'=2,'z1'=2,'z0'=2,'yl'=2,'yh'=2,'x1'=2,'x0'=2,'c'=2] {'x0..., dimensions={0} | all-to-all | bytes 1048576 | tf_op jit(solution)/shard_map/all_to_all | solution.py:36
  98.0 5.2 %collective-permute-start = (bf16[8,32,1024]{2,1,0:T(8,128)(2,1)S(1)}, bf16[8,32,1024]{2,1,0:T(8,128)(2,1)S(1)}, u32[]{:S(2)}, u32[]{:S(2)}) collective-permute-start(bf16[8,32,1024]{2,1,0:T(8,128)(2,1)S(1)} %all_to_all.54.got_ref.mine_ref), channel_id=1, source_target_pairs={{0,1},{1,0},{2,3},{3,2},{4,5},{5,4},{6,7},{7,6},{8,9},{9,8},{10,11... | collective-permute-start | bytes 1572872 | tf_op jit(solution)/shard_map/ppermute | solution.py:44
  103.2 0.4 shard_map.130.refs_0_
  103.6 1.1 collective-permute-done.got_ref.others_ref
  104.7 0.4 shard_map.131
  105.1 13.1 %all_to_all.55 = bf16[4,128,768]{2,1,0:T(8,128)(2,1)S(1)} all-to-all(bf16[4,128,768]{2,1,0:T(8,128)(2,1)S(1)} %shard_map.131), channel_id=1, replica_groups=mesh['z3'=2,'z2'=2,'z1'=2,'z0'=2,'yl'=2,'yh'=2,'x1'=2,'x0'=2,'c'=2] {'z0..., dimensions={0} | all-to-all | bytes 1572864 | tf_op jit(solution)/shard_map/all_to_all | solution.py:36
  118.4 14.9 %all_to_all.56.got_ref = bf16[8,16,768]{2,1,0:T(8,128)(2,1)S(1)} all-to-all(bf16[8,16,768]{2,1,0:T(8,128)(2,1)S(1)} %bitcast.14), channel_id=1, replica_groups=mesh['z3'=2,'z2'=2,'z1'=2,'z0'=2,'yl'=2,'yh'=2,'x1'=2,'x0'=2,'c'=2] {'z1..., dimensions={0} | all-to-all | bytes 393216 | tf_op jit(solution)/shard_map/all_to_all | solution.py:36
  133.5 20.0 %all_to_all.57 = bf16[8,16,768]{2,1,0:T(8,128)(2,1)S(1)} all-to-all(bf16[8,16,768]{2,1,0:T(8,128)(2,1)S(1)} %shard_map.132), channel_id=1, replica_groups=mesh['z3'=2,'z2'=2,'z1'=2,'z0'=2,'yl'=2,'yh'=2,'x1'=2,'x0'=2,'c'=2] {'z1..., dimensions={0} | all-to-all | bytes 393216 | tf_op jit(solution)/shard_map/all_to_all | solution.py:36
  153.5 12.3 %all_to_all.58.rows_ref = bf16[4,128,768]{2,1,0:T(8,128)(2,1)S(1)} all-to-all(bf16[4,128,768]{2,1,0:T(8,128)(2,1)S(1)} %broadcast_in_dim.42), channel_id=1, replica_groups=mesh['z3'=2,'z2'=2,'z1'=2,'z0'=2,'yl'=2,'yh'=2,'x1'=2,'x0'=2,'c'=2] {'z0..., dimensions={0} | all-to-all | bytes 1572864 | tf_op jit(solution)/shard_map/all_to_all | solution.py:36
  165.9 1.3 shard_map.133
  167.2 8.9 %all-to-all-start.9 = ((bf16[16,32,448]{2,1,0:T(8,128)(2,1)}), bf16[16,32,448]{2,1,0:T(8,128)(2,1)S(1)}, u32[]{:S(2)}, u32[]{:S(2)}) async-start(bf16[16,32,448]{2,1,0:T(8,128)(2,1)} %bitcast.10), calls=%async_computation.9 | async-start | bytes 1048576 | tf_op jit(solution)/shard_map/all_to_all | solution.py:36
  176.1 2.9 %shard_map.134 = (f32[512,768]{1,0:T(8,128)}, f32[448,768]{1,0:T(8,128)}, f32[1,768]{1,0:T(1,128)S(1)}) custom-call(s32[1]{0:T(128)} %bitcast.1.core_ref, bf16[8,32,1024]{2,1,0:T(8,128)(2,1)S(1)} %all_to_all.54.got_ref.mine_ref, bf16[8,32,1024]{2,1,0:T(8,128)(2,1)S(1)} %collective-permute-done.got_ref.others_ref, bf16[4,128,768]{2,1,0:T(8,128)(2,1)S(1)} %bitcast.13, ...), custom_call_target="tpu_custom_call" | custom-call | flops 754974720 | bytes 5576708 | tf_op jit(solution)/shard_map/pallas_call | solution.py:23
  179.0 0.6 reduce.1
  179.6 0.6 slice_bitcast_fusion
  180.2 7.6 %all-to-all-done.9 = bf16[16,32,448]{2,1,0:T(8,128)(2,1)S(1)} async-done(((bf16[16,32,448]{2,1,0:T(8,128)(2,1)}), bf16[16,32,448]{2,1,0:T(8,128)(2,1)S(1)}, u32[]{:S(2)}, u32[]{:S(2)}) %all-to-all-start.9) | async-done | bytes 458784 | tf_op jit(solution)/shard_map/all_to_all | solution.py:36
  187.9 0.7 fusion.7
  (21 shorter events, 0.5 us)
Async XLA Ops:
  0.7 40.4 %copy-start = (bf16[512,768]{1,0:T(8,128)(2,1)S(1)}, bf16[512,768]{1,0:T(8,128)(2,1)}, u32[]{:S(2)}) copy-start(bf16[512,768]{1,0:T(8,128)(2,1)} %weight_ref.8) | copy-start | bytes 2359300
  0.7 40.4 %copy-start.5 = (f32[768]{0:T(1024)S(1)}, f32[768]{0:T(1024)}, u32[]{:S(2)}) copy-start(f32[768]{0:T(1024)} %gain_ref.5) | copy-start | bytes 9220
  41.1 25.9 %copy-start.6 = (s32[32]{0:T(128)S(1)}, s32[32]{0:T(128)}, u32[]{:S(2)}) copy-start(s32[32]{0:T(128)} %targets_ref.1) | copy-start | bytes 388
  41.1 25.9 %copy-start.7 = (f32[32]{0:T(128)S(1)}, f32[32]{0:T(128)}, u32[]{:S(2)}) copy-start(f32[32]{0:T(128)} %weight_ref.6) | copy-start | bytes 388
  41.1 44.9 %copy-start.2 = (bf16[32,448]{1,0:T(8,128)(2,1)S(1)}, bf16[32,448]{1,0:T(8,128)(2,1)}, u32[]{:S(2)}) copy-start(bf16[32,448]{1,0:T(8,128)(2,1)} %gate_ref.1) | copy-start | bytes 86020
  41.1 44.9 %copy-start.3 = (bf16[32,448]{1,0:T(8,128)(2,1)S(1)}, bf16[32,448]{1,0:T(8,128)(2,1)}, u32[]{:S(2)}) copy-start(bf16[32,448]{1,0:T(8,128)(2,1)} %up_ref.1) | copy-start | bytes 86020
  98.0 6.7 %collective-permute-start = (bf16[8,32,1024]{2,1,0:T(8,128)(2,1)S(1)}, bf16[8,32,1024]{2,1,0:T(8,128)(2,1)S(1)}, u32[]{:S(2)}, u32[]{:S(2)}) collective-permute-start(bf16[8,32,1024]{2,1,0:T(8,128)(2,1)S(1)} %all_to_all.54.got_ref.mine_ref), channel_id=1, source_target_pairs={{0,1},{1,0},{2,3},{3,2},{4,5},{5,4},{6,7},{7,6},{8,9},{9,8},{10,11... | collective-permute-start | bytes 1572872 | tf_op jit(solution)/shard_map/ppermute | solution.py:44
  105.1 28.2 %copy-start.4 = (bf16[16,768]{1,0:T(8,128)(2,1)S(1)}, bf16[16,768]{1,0:T(8,128)(2,1)}, u32[]{:S(2)}) copy-start(bf16[16,768]{1,0:T(8,128)(2,1)} %x_ref.1) | copy-start | bytes 73732
  133.5 32.4 %copy-start.1 = (bf16[448,768]{1,0:T(8,128)(2,1)S(1)}, bf16[448,768]{1,0:T(8,128)(2,1)}, u32[]{:S(2)}) copy-start(bf16[448,768]{1,0:T(8,128)(2,1)} %weight_ref.9) | copy-start | bytes 2064388
  167.2 20.6 %all-to-all-start.9 = ((bf16[16,32,448]{2,1,0:T(8,128)(2,1)}), bf16[16,32,448]{2,1,0:T(8,128)(2,1)S(1)}, u32[]{:S(2)}, u32[]{:S(2)}) async-start(bf16[16,32,448]{2,1,0:T(8,128)(2,1)} %bitcast.10), calls=%async_computation.9 | async-start | bytes 1048576 | tf_op jit(solution)/shard_map/all_to_all | solution.py:36

commit v10 on v8

--- a/solution.py
+++ b/solution.py
@@ -9,8 +9,8 @@
 EPSILON = 1e-05
 TENSOR = ("z3", "z2", "z1", "z0", "yl")
 DP = ("yh", "x1", "x0", "c")
-FAR, NEAR = ("z1", "z3", "z2"), ("z0", "yl")
-CHIPS = ("x0", "yh", "x1")
+FAR, NEAR = ("z1", "z2", "z3"), ("z0", "yl")
+CHIPS = ("x0", "x1", "yh")
 DEVICES = CHIPS + ("c",)
 FARS, NEARS = 8, 4
 f32, bf16 = jnp.float32, jnp.bfloat16

time: 189 us -> 188 us (level)
  blocking collectives: 156 us -> 154 us
where the time goes in v10:
time: 188 us; the launch traced here: 187 us
  blocking collectives  154 us (82%)
  starting transfers between devices  13.6 us (7%)
  waiting for transfers between devices  9.13 us (5%)
  Pallas kernels  6.22 us (3%)
    all_to_all x9, blocking collectives, exchange(): return lax.all_to_all(blocks, axes, 0, 0, tiled=True)  154 us
    all_to_all x1, starting transfers between devices, exchange(): return lax.all_to_all(blocks, axes, 0, 0, tiled=True)  8.24 us
    all_to_all x1, waiting for transfers between devices, exchange(): return lax.all_to_all(blocks, axes, 0, 0, tiled=True)  7.61 us
    ppermute x1, starting transfers between devices, other_core(): return lax.ppermute(block, 'c', [(0, 1), (1, 0)])  5.4 us
    pallas_call x6, Pallas kernels, on_core(): pl.pallas_call(kernel, out_shape=outs, in_specs=[pl.BlockSpec(memory_spac...  4.91 us
  transfers between devices with their start and end apart: 2, of which 2 were waited for; matrix products, arithmetic and copies ran while one was open for 1% of the time, Pallas kernels for 2%

profile of v10, /device:TPU:1, one launch (start us, length us, event | category | flops | bytes accessed | tf_op | source)
XLA Modules:
  0.0 187.3 jit_solution(5233887710897138578)
XLA Ops:
  0.7 0.8 broadcast_in_dim.39
  1.5 27.4 %all_to_all.50 = bf16[8,16,768]{2,1,0:T(8,128)(2,1)S(1)} all-to-all(bf16[8,16,768]{2,1,0:T(8,128)(2,1)S(1)} %broadcast_in_dim.39), channel_id=1, replica_groups=mesh['z3'=2,'z2'=2,'z1'=2,'z0'=2,'yl'=2,'yh'=2,'x1'=2,'x0'=2,'c'=2] {'z1..., dimensions={0} | all-to-all | bytes 393216 | tf_op jit(solution)/shard_map/all_to_all | solution.py:36
  28.9 10.8 %all_to_all.51 = bf16[4,8,16,768]{3,2,1,0:T(8,128)(2,1)S(1)} all-to-all(bf16[4,8,16,768]{3,2,1,0:T(8,128)(2,1)S(1)} %broadcast_in_dim.40), channel_id=1, replica_groups=mesh['z3'=2,'z2'=2,'z1'=2,'z0'=2,'yl'=2,'yh'=2,'x1'=2,'x0'=2,'c'=2] {'z0..., dimensions={0} | all-to-all | bytes 1572864 | tf_op jit(solution)/shard_map/all_to_all | solution.py:36
  39.8 0.6 shard_map.127
  40.4 24.4 %all_to_all.52.got_ref = bf16[16,144,128]{2,1,0:T(8,128)(2,1)S(1)} all-to-all(bf16[16,144,128]{2,1,0:T(8,128)(2,1)S(1)} %shard_map.127), channel_id=1, replica_groups=mesh['z3'=2,'z2'=2,'z1'=2,'z0'=2,'yl'=2,'yh'=2,'x1'=2,'x0'=2,'c'=2] {'x0..., dimensions={0} | all-to-all | bytes 1179648 | tf_op jit(solution)/shard_map/all_to_all | solution.py:36
  64.8 0.3 shard_map.128
  65.1 20.8 %all_to_all.53.stats_ref = f32[32,1,128]{2,1,0:T(1,128)S(1)} all-to-all(f32[32,1,128]{2,1,0:T(1,128)S(1)} %get-tuple-element.31), channel_id=1, replica_groups=mesh['z3'=2,'z2'=2,'z1'=2,'z0'=2,'yl'=2,'yh'=2,'x1'=2,'x0'=2,'c'=2] {'z1..., dimensions={0} | all-to-all | bytes 32768 | tf_op jit(solution)/shard_map/all_to_all | solution.py:36
  85.9 0.3 shard_map.129
  86.2 11.5 %all_to_all.54.mine_ref = bf16[8,32,1024]{2,1,0:T(8,128)(2,1)S(1)} all-to-all(bf16[8,32,1024]{2,1,0:T(8,128)(2,1)S(1)} %shard_map.129), channel_id=1, replica_groups=mesh['z3'=2,'z2'=2,'z1'=2,'z0'=2,'yl'=2,'yh'=2,'x1'=2,'x0'=2,'c'=2] {'x0..., dimensions={0} | all-to-all | bytes 1048576 | tf_op jit(solution)/shard_map/all_to_all | solution.py:36
  97.7 5.4 %collective-permute-start = (bf16[8,32,1024]{2,1,0:T(8,128)(2,1)S(1)}, bf16[8,32,1024]{2,1,0:T(8,128)(2,1)S(1)}, u32[]{:S(2)}, u32[]{:S(2)}) collective-permute-start(bf16[8,32,1024]{2,1,0:T(8,128)(2,1)S(1)} %all_to_all.54.mine_ref), channel_id=1, source_target_pairs={{0,1},{1,0},{2,3},{3,2},{4,5},{5,4},{6,7},{7,6},{8,9},{9,8},{10,11... | collective-permute-start | bytes 1572872 | tf_op jit(solution)/shard_map/ppermute | solution.py:44
  103.1 1.5 collective-permute-done.others_ref
  104.6 0.6 shard_map.130
  105.2 13.1 %all_to_all.55 = bf16[4,128,768]{2,1,0:T(8,128)(2,1)S(1)} all-to-all(bf16[4,128,768]{2,1,0:T(8,128)(2,1)S(1)} %shard_map.130), channel_id=1, replica_groups=mesh['z3'=2,'z2'=2,'z1'=2,'z0'=2,'yl'=2,'yh'=2,'x1'=2,'x0'=2,'c'=2] {'z0..., dimensions={0} | all-to-all | bytes 1572864 | tf_op jit(solution)/shard_map/all_to_all | solution.py:36
  118.5 14.5 %all_to_all.56.got_ref = bf16[8,16,768]{2,1,0:T(8,128)(2,1)S(1)} all-to-all(bf16[8,16,768]{2,1,0:T(8,128)(2,1)S(1)} %bitcast.14), channel_id=1, replica_groups=mesh['z3'=2,'z2'=2,'z1'=2,'z0'=2,'yl'=2,'yh'=2,'x1'=2,'x0'=2,'c'=2] {'z1..., dimensions={0} | all-to-all | bytes 393216 | tf_op jit(solution)/shard_map/all_to_all | solution.py:36
  133.0 0.2 shard_map.131
  133.2 19.2 %all_to_all.57 = bf16[8,16,768]{2,1,0:T(8,128)(2,1)S(1)} all-to-all(bf16[8,16,768]{2,1,0:T(8,128)(2,1)S(1)} %shard_map.131), channel_id=1, replica_groups=mesh['z3'=2,'z2'=2,'z1'=2,'z0'=2,'yl'=2,'yh'=2,'x1'=2,'x0'=2,'c'=2] {'z1..., dimensions={0} | all-to-all | bytes 393216 | tf_op jit(solution)/shard_map/all_to_all | solution.py:36
  152.4 12.8 %all_to_all.58.rows_ref = bf16[4,128,768]{2,1,0:T(8,128)(2,1)S(1)} all-to-all(bf16[4,128,768]{2,1,0:T(8,128)(2,1)S(1)} %broadcast_in_dim.42), channel_id=1, replica_groups=mesh['z3'=2,'z2'=2,'z1'=2,'z0'=2,'yl'=2,'yh'=2,'x1'=2,'x0'=2,'c'=2] {'z0..., dimensions={0} | all-to-all | bytes 1572864 | tf_op jit(solution)/shard_map/all_to_all | solution.py:36
  165.2 1.3 shard_map.132
  166.6 8.2 %all-to-all-start.9 = ((bf16[16,32,448]{2,1,0:T(8,128)(2,1)}), bf16[16,32,448]{2,1,0:T(8,128)(2,1)S(1)}, u32[]{:S(2)}, u32[]{:S(2)}) async-start(bf16[16,32,448]{2,1,0:T(8,128)(2,1)} %bitcast.10), calls=%async_computation.9 | async-start | bytes 1048576 | tf_op jit(solution)/shard_map/all_to_all | solution.py:36
  174.8 2.9 %shard_map.133 = (f32[512,768]{1,0:T(8,128)}, f32[448,768]{1,0:T(8,128)}, f32[1,768]{1,0:T(1,128)S(1)}) custom-call(s32[1]{0:T(128)} %bitcast.1.core_ref, bf16[8,32,1024]{2,1,0:T(8,128)(2,1)S(1)} %all_to_all.54.mine_ref, bf16[8,32,1024]{2,1,0:T(8,128)(2,1)S(1)} %collective-permute-done.others_ref, bf16[4,128,768]{2,1,0:T(8,128)(2,1)S(1)} %bitcast.13, ...), custom_call_target="tpu_custom_call" | custom-call | flops 754974720 | bytes 5576708 | tf_op jit(solution)/shard_map/pallas_call | solution.py:23
  177.7 0.6 reduce.1
  178.3 0.6 slice_bitcast_fusion
  178.9 7.6 %all-to-all-done.9 = bf16[16,32,448]{2,1,0:T(8,128)(2,1)S(1)} async-done(((bf16[16,32,448]{2,1,0:T(8,128)(2,1)}), bf16[16,32,448]{2,1,0:T(8,128)(2,1)S(1)}, u32[]{:S(2)}, u32[]{:S(2)}) %all-to-all-start.9) | async-done | bytes 458784 | tf_op jit(solution)/shard_map/all_to_all | solution.py:36
  186.6 0.7 fusion.7
  (20 shorter events, 0.4 us)
Async XLA Ops:
  0.7 39.1 %copy-start = (bf16[512,768]{1,0:T(8,128)(2,1)S(1)}, bf16[512,768]{1,0:T(8,128)(2,1)}, u32[]{:S(2)}) copy-start(bf16[512,768]{1,0:T(8,128)(2,1)} %weight_ref.6) | copy-start | bytes 2359300
  0.7 39.1 %copy-start.5 = (f32[768]{0:T(1024)S(1)}, f32[768]{0:T(1024)}, u32[]{:S(2)}) copy-start(f32[768]{0:T(1024)} %gain_ref.5) | copy-start | bytes 9220
  39.7 25.1 %copy-start.6 = (s32[32]{0:T(128)S(1)}, s32[32]{0:T(128)}, u32[]{:S(2)}) copy-start(s32[32]{0:T(128)} %targets_ref.1) | copy-start | bytes 388
  39.7 25.1 %copy-start.7 = (f32[32]{0:T(128)S(1)}, f32[32]{0:T(128)}, u32[]{:S(2)}) copy-start(f32[32]{0:T(128)} %weight_ref.5) | copy-start | bytes 388
  39.7 46.1 %copy-start.2 = (bf16[32,448]{1,0:T(8,128)(2,1)S(1)}, bf16[32,448]{1,0:T(8,128)(2,1)}, u32[]{:S(2)}) copy-start(bf16[32,448]{1,0:T(8,128)(2,1)} %gate_ref.1) | copy-start | bytes 86020
  39.7 46.1 %copy-start.3 = (bf16[32,448]{1,0:T(8,128)(2,1)S(1)}, bf16[32,448]{1,0:T(8,128)(2,1)}, u32[]{:S(2)}) copy-start(bf16[32,448]{1,0:T(8,128)(2,1)} %up_ref.1) | copy-start | bytes 86020
  97.7 6.9 %collective-permute-start = (bf16[8,32,1024]{2,1,0:T(8,128)(2,1)S(1)}, bf16[8,32,1024]{2,1,0:T(8,128)(2,1)S(1)}, u32[]{:S(2)}, u32[]{:S(2)}) collective-permute-start(bf16[8,32,1024]{2,1,0:T(8,128)(2,1)S(1)} %all_to_all.54.mine_ref), channel_id=1, source_target_pairs={{0,1},{1,0},{2,3},{3,2},{4,5},{5,4},{6,7},{7,6},{8,9},{9,8},{10,11... | collective-permute-start | bytes 1572872 | tf_op jit(solution)/shard_map/ppermute | solution.py:44
  105.2 27.8 %copy-start.4 = (bf16[16,768]{1,0:T(8,128)(2,1)S(1)}, bf16[16,768]{1,0:T(8,128)(2,1)}, u32[]{:S(2)}) copy-start(bf16[16,768]{1,0:T(8,128)(2,1)} %x_ref.1) | copy-start | bytes 73732
  133.2 32.1 %copy-start.1 = (bf16[448,768]{1,0:T(8,128)(2,1)S(1)}, bf16[448,768]{1,0:T(8,128)(2,1)}, u32[]{:S(2)}) copy-start(bf16[448,768]{1,0:T(8,128)(2,1)} %weight_ref.7) | copy-start | bytes 2064388
  166.6 20.0 %all-to-all-start.9 = ((bf16[16,32,448]{2,1,0:T(8,128)(2,1)}), bf16[16,32,448]{2,1,0:T(8,128)(2,1)S(1)}, u32[]{:S(2)}, u32[]{:S(2)}) async-start(bf16[16,32,448]{2,1,0:T(8,128)(2,1)} %bitcast.10), calls=%async_computation.9 | async-start | bytes 1048576 | tf_op jit(solution)/shard_map/all_to_all | solution.py:36
